TPU v7x, 32 devices: a whole 2x2x4 slice. The times are simulated.
32 devices in a mesh: group: 2 (over y), blk: 4 (over z), dp: 4 (over x, core).
Axes of the slice: x: 2, y: 2, z: 4, core: 2. Of those that a mesh axis runs over, the one named last changes fastest.
Arguments:
- activations: bfloat16 [1024, 4096], P(('group', 'dp'), 'blk'), parts along dimension 0, may hold values from -6 to 6
- output_grad: bfloat16 [1024, 4096], P(('group', 'dp'), 'blk'), parts along dimension 0, may hold values from -6 to 6
- gate_weight: bfloat16 [16, 128, 128, 128], P('dp', 'blk'), may hold values from -0.125 to 0.125
- up_weight: bfloat16 [16, 128, 128, 128], P('dp', 'blk'), may hold values from -0.125 to 0.125
- down_weight: bfloat16 [16, 128, 128, 128], P('dp', 'blk'), may hold values from -0.125 to 0.125
- gate_rows: int32 [112, 16], replicated, may hold values from 0 to 31, as said below
- up_rows: int32 [112, 16], replicated, may hold values from 0 to 31, as said below
- down_columns: int32 [112, 16], replicated, may hold values from 0 to 31, as said below
- owner_map: int32 [112], replicated, may hold values from 0 to 3, as said below
Outputs:
- input_grad: bfloat16 [1024, 4096], P(('group', 'dp'), 'blk'), parts along dimension 0
- gate_grad: bfloat16 [16, 256, 128, 128], P('dp', ('group', 'blk')), parts along dimension 1
- up_grad: bfloat16 [16, 256, 128, 128], P('dp', ('group', 'blk')), parts along dimension 1
- down_grad: bfloat16 [16, 256, 128, 128], P('dp', ('group', 'blk')), parts along dimension 1
There are 2 independent parts, one for each index of `group`. A program takes and returns all parts, laid end to end along the dimension named above; an argument that names none is the same for every part. Nothing has to cross between parts.
Inputs may be any that keep to these rules, and one draw needn't show every extreme that they name: `owner_map`: each index of blk owns between 24 and 32 hidden blocks, and some index owns exactly 32. `gate_rows`: each row holds 16 distinct row blocks. `up_rows`: each row holds 16 distinct row blocks. `down_columns`: each row holds 16 distinct output blocks.
All inputs are finite; a program needn't handle non-finite values.
Results may differ from a plain program's by a relative error of at most 0.0058.
Values may be sent and summed in bfloat16 or wider, within the bound.
A program may use at most 320 MiB of HBM per device.

v0:
```python
import jax
import jax.numpy as jnp
from jax import lax
from jax.sharding import PartitionSpec as P


def weight_term(selected, deltas, pattern, pieces):
    partial_term = jnp.einsum(pattern, selected, deltas, preferred_element_type=jnp.float32).astype(
        jnp.bfloat16
    )
    return partial_term.reshape((pieces, partial_term.shape[0] // pieces) + partial_term.shape[1:])


def reduce_pieces(received):
    return jnp.sum(received.astype(jnp.float32), axis=0).astype(jnp.bfloat16)


def body(
    activations,
    output_grad,
    gate_weight,
    up_weight,
    down_weight,
    gate_rows,
    up_rows,
    down_columns,
    owner_map,
):
    tokens_here = activations.shape[0]
    slot_count = gate_weight.shape[1]
    block_size = gate_weight.shape[2]
    data_count = lax.axis_size("dp")
    full_inputs, full_grads = (
        lax.all_gather(activations, "blk", axis=1, tiled=True),
        lax.all_gather(output_grad, "blk", axis=1, tiled=True),
    )
    row_blocks = full_inputs.shape[1] // block_size
    input_blocks = full_inputs.reshape(tokens_here, row_blocks, block_size)
    grad_blocks = full_grads.reshape(tokens_here, row_blocks, block_size)
    own_index = lax.axis_index("blk")
    owned = (owner_map == own_index).astype(jnp.int32)
    position = jnp.cumsum(owned) - 1
    slot_ids = jnp.arange(slot_count, dtype=jnp.int32)
    chosen = owned[None, :] * (position[None, :] == slot_ids[:, None]).astype(jnp.int32)
    live_mask = jnp.sum(chosen, axis=1).astype(jnp.bfloat16)[None, :, None, None]

    def lookup(listing):
        return jnp.sum(chosen[:, :, None] * listing[None, :, :], axis=1)

    gate_lists = lookup(gate_rows)
    up_lists = lookup(up_rows)
    down_lists = lookup(down_columns)
    gate_inputs = input_blocks[:, gate_lists]
    up_inputs = input_blocks[:, up_lists]
    down_inputs = grad_blocks[:, down_lists]
    gate_full, up_full, down_full = (
        lax.all_gather(gate_weight, "dp", axis=0, tiled=True),
        lax.all_gather(up_weight, "dp", axis=0, tiled=True),
        lax.all_gather(down_weight, "dp", axis=0, tiled=True),
    )
    backward = jnp.einsum(
        "thme,mhce->thc", down_inputs, down_full * live_mask, preferred_element_type=jnp.float32
    )
    gate_full = gate_full * live_mask
    up_full = up_full * live_mask
    gate_value = jnp.einsum(
        "thmc,mhcd->thd", gate_inputs, gate_full, preferred_element_type=jnp.float32
    )
    up_value = jnp.einsum("thmc,mhcd->thd", up_inputs, up_full, preferred_element_type=jnp.float32)
    sigmoid_gate = jax.nn.sigmoid(gate_value)
    activated = gate_value * sigmoid_gate
    hidden = (activated * up_value).astype(jnp.bfloat16)
    up_delta = (backward * activated).astype(jnp.bfloat16)
    gate_delta = (
        backward * up_value * sigmoid_gate * (1.0 + gate_value * (1.0 - sigmoid_gate))
    ).astype(jnp.bfloat16)

    def add_block(block_index, running):
        gate_slice = lax.dynamic_index_in_dim(gate_full, block_index, 0, keepdims=False)
        up_slice = lax.dynamic_index_in_dim(up_full, block_index, 0, keepdims=False)
        gate_part = jnp.einsum(
            "thd,hcd->thc", gate_delta, gate_slice, preferred_element_type=jnp.float32
        )
        up_part = jnp.einsum("thd,hcd->thc", up_delta, up_slice, preferred_element_type=jnp.float32)
        gate_targets = lax.dynamic_index_in_dim(gate_lists, block_index, 1, keepdims=False)
        up_targets = lax.dynamic_index_in_dim(up_lists, block_index, 1, keepdims=False)
        running = running.at[:, gate_targets].add(gate_part)
        return running.at[:, up_targets].add(up_part)

    empty_input = jnp.zeros((tokens_here, row_blocks, block_size), jnp.float32)
    input_term = lax.fori_loop(0, gate_full.shape[0], add_block, empty_input)
    input_grad = lax.psum_scatter(
        input_term.reshape(tokens_here, row_blocks * block_size),
        "blk",
        scatter_dimension=1,
        tiled=True,
    ).astype(jnp.bfloat16)
    gate_term = weight_term(gate_inputs, gate_delta, "thmc,thd->mhcd", data_count)
    up_term = weight_term(up_inputs, up_delta, "thmc,thd->mhcd", data_count)
    gate_moved = lax.all_to_all(gate_term, "dp", split_axis=0, concat_axis=0, tiled=True)
    up_moved = lax.all_to_all(up_term, "dp", split_axis=0, concat_axis=0, tiled=True)
    down_term = weight_term(down_inputs, hidden, "thme,thc->mhce", data_count)
    down_moved = lax.all_to_all(down_term, "dp", split_axis=0, concat_axis=0, tiled=True)
    return (
        input_grad,
        reduce_pieces(gate_moved),
        reduce_pieces(up_moved),
        reduce_pieces(down_moved),
    )


def solution(mesh):
    in_specs = (
        P(("group", "dp"), "blk"),
        P(("group", "dp"), "blk"),
        P("dp", "blk", None, None),
        P("dp", "blk", None, None),
        P("dp", "blk", None, None),
        P(),
        P(),
        P(),
        P(),
    )
    out_specs = (
        P(("group", "dp"), "blk"),
        P("dp", ("group", "blk"), None, None),
        P("dp", ("group", "blk"), None, None),
        P("dp", ("group", "blk"), None, None),
    )
    return jax.shard_map(body, mesh=mesh, in_specs=in_specs, out_specs=out_specs, check_vma=False)
```

profile of v0, /device:TPU:0, one launch (start us, length us, event | category | flops | bytes accessed | tf_op | source)
XLA Modules:
  0.0 1284.1 jit_solution(9627945221501354605)
XLA Ops:
  18.0 22.8 %all-gather.14.cloned.1.call-done = bf16[128,4096]{0,1:T(8,128)(2,1)} async-done(((bf16[128,1024]{0,1:T(8,128)(2,1)}), bf16[128,4096]{0,1:T(8,128)(2,1)}) %all-gather.14.cloned.1.call-update) | async-done | bytes 1048592 | tf_op jit(solution)/shard_map/all_gather | solution.py:34
  42.4 13.8 %gather_fusion.1 = bf16[512,128,128]{2,1,0:T(8,128)(2,1)} fusion(bf16[128,32,128]{2,0,1:T(8,128)(2,1)S(1)} %copy.103, s32[1024]{0:T(1024)S(1)} %pad_clamp_fusion.1), kind=kCustom, calls=%fused_computation.1 | custom fusion | bytes 33556480 | tf_op jit(solution)/shard_map/gather | solution.py:54
  56.3 13.9 %gather_fusion.2 = bf16[512,128,128]{2,1,0:T(8,128)(2,1)} fusion(bf16[128,32,128]{2,0,1:T(8,128)(2,1)S(1)} %copy.103, s32[1024]{0:T(1024)S(1)} %pad_clamp_fusion), kind=kCustom, calls=%fused_computation.2 | custom fusion | bytes 33556480 | tf_op jit(solution)/shard_map/gather | solution.py:53
  72.0 15.2 %gather_fusion = bf16[512,128,128]{2,1,0:T(8,128)(2,1)} fusion(bf16[128,32,128]{2,0,1:T(8,128)(2,1)S(1)} %copy.100, s32[1024]{0:T(1024)S(1)} %pad_clamp_fusion.2), kind=kCustom, calls=%fused_computation | custom fusion | bytes 33556480 | tf_op jit(solution)/shard_map/gather | solution.py:55
  87.2 90.2 %all-gather.12.cloned.1.call-done = bf16[16,32,128,128]{3,2,1,0:T(8,128)(2,1)} async-done(((bf16[4,32,128,128]{3,2,1,0:T(8,128)(2,1)}), bf16[16,32,128,128]{3,2,1,0:T(8,128)(2,1)}) %all-gather.12.cloned.1.call-update) | async-done | bytes 16777232 | tf_op jit(solution)/shard_map/all_gather | solution.py:58
  177.4 107.4 %all-gather.6.cloned.1.call-done = bf16[16,32,128,128]{3,2,1,0:T(8,128)(2,1)} async-done(((bf16[4,32,128,128]{3,2,1,0:T(8,128)(2,1)}), bf16[16,32,128,128]{3,2,1,0:T(8,128)(2,1)}) %all-gather.6.cloned.1.call-update) | async-done | bytes 16777232 | tf_op jit(solution)/shard_map/all_gather | solution.py:57
  284.8 24.2 %broadcast_multiply_fusion = (bf16[16,32,128,128]{3,2,1,0:T(8,128)(2,1)}, bf16[16,32,128,128]{3,2,1,0:T(8,128)(2,1)}) fusion(bf16[16,32,128,128]{3,2,1,0:T(8,128)(2,1)} %all-gather.12.cloned.1.call-done, bf16[32]{0:T(256)(128)(2,1)S(1)} %convert_element_type.48, bf16[16,32,128,128]{3,2,1,0:T(8,128)(2,1)} %all-gather.6.cloned.1.call-done), kind=kLoop, calls=%fused_computation.29 | loop fusion | flops 16777216 | bytes 67108928 | tf_op jit(solution)/shard_map/mul | solution.py:65
  309.0 14.2 %fusion.10 = f32[32,128,128,1]{2,1,0,3:T(8,128)} fusion(bf16[16,32,128,128]{3,2,1,0:T(8,128)(2,1)} %get-tuple-element.280, bf16[128,32,16,128]{3,0,2,1:T(8,128)(2,1)} %bitcast.144), kind=kOutput, calls=%fused_computation.21 | convolution fusion | flops 2147483648 | bytes 35651584 | tf_op jit(solution)/shard_map/thmc,mhcd->thd/dot_general | solution.py:69
  323.2 14.2 %fusion.8 = f32[32,128,128,1]{2,1,0,3:T(8,128)} fusion(bf16[16,32,128,128]{3,2,1,0:T(8,128)(2,1)} %get-tuple-element.277, bf16[128,32,16,128]{3,0,2,1:T(8,128)(2,1)} %bitcast.142), kind=kOutput, calls=%fused_computation.19 | convolution fusion | flops 2147483648 | bytes 35651584 | tf_op jit(solution)/shard_map/thmc,mhcd->thd/dot_general | solution.py:66
  337.3 54.8 %all-gather.8.cloned.1.call-done = bf16[16,32,128,128]{3,2,1,0:T(8,128)(2,1)} async-done(((bf16[4,32,128,128]{3,2,1,0:T(8,128)(2,1)}), bf16[16,32,128,128]{3,2,1,0:T(8,128)(2,1)}) %all-gather.8.cloned.1.call-update) | async-done | bytes 16777232 | tf_op jit(solution)/shard_map/all_gather | solution.py:59
  392.2 13.7 %fusion.20 = (bf16[128,32,128]{0,2,1:T(8,128)(2,1)S(1)}, bf16[128,32,128]{0,2,1:T(8,128)(2,1)S(1)}) fusion(f32[32,128,128,1]{2,1,0,3:T(8,128)} %fusion.8, f32[32,128,128,1]{2,1,0,3:T(8,128)} %fusion.10, bf16[128,32,16,128]{3,0,2,1:T(8,128)(2,1)} %bitcast.140, bf16[16,32,128,128]{3,2,1,0:T(8,128)(2,1)} %all-gather.8.cloned.1.call-done, ...), kind=kOutput, calls=%fused_computation.40 | convolution fusion | flops 2162688000 | bytes 39845952 | tf_op jit(solution)/shard_map/thme,mhce->thc/dot_general | solution.py:61
  405.9 11.4 convolution_convert_fusion.1
  417.3 14.1 %copy.116 = bf16[4,4,32,128,128]{3,4,1,2,0:T(8,128)(2,1)} copy(bf16[4,4,32,128,128]{3,4,1,0,2:T(8,128)(2,1)} %bitcast.138) | data formatting | bytes 33554432 | tf_op jit(solution)/shard_map/reshape | solution.py:11
  431.4 7.1 all-to-all-start.1
  438.4 11.4 convolution_convert_fusion.2
  449.9 14.1 %copy.114 = bf16[4,4,32,128,128]{3,4,1,2,0:T(8,128)(2,1)} copy(bf16[4,4,32,128,128]{3,4,1,0,2:T(8,128)(2,1)} %bitcast.139) | data formatting | bytes 33554432 | tf_op jit(solution)/shard_map/reshape | solution.py:11
  464.0 157.5 %all-to-all-done.1 = bf16[4,4,32,128,128]{3,4,1,2,0:T(8,128)(2,1)} async-done(((bf16[4,4,32,128,128]{3,4,1,2,0:T(8,128)(2,1)}), bf16[4,4,32,128,128]{3,4,1,2,0:T(8,128)(2,1)}, u32[]{:S(2)}, u32[]{:S(2)}) %all-to-all-start.1) | async-done | bytes 16777248 | tf_op jit(solution)/shard_map/all_to_all | solution.py:101
  621.5 7.3 all-to-all-start
  630.9 12.7 convolution_convert_fusion
  643.6 14.1 %copy.118 = bf16[4,4,32,128,128]{4,3,1,2,0:T(8,128)(2,1)} copy(bf16[4,4,32,128,128]{4,3,1,0,2:T(8,128)(2,1)} %bitcast.137) | data formatting | bytes 33554432 | tf_op jit(solution)/shard_map/reshape | solution.py:11
  657.8 153.9 %all-to-all-done = bf16[4,4,32,128,128]{3,4,1,2,0:T(8,128)(2,1)} async-done(((bf16[4,4,32,128,128]{3,4,1,2,0:T(8,128)(2,1)}), bf16[4,4,32,128,128]{3,4,1,2,0:T(8,128)(2,1)}, u32[]{:S(2)}, u32[]{:S(2)}) %all-to-all-start) | async-done | bytes 16777248 | tf_op jit(solution)/shard_map/all_to_all | solution.py:100
  811.6 7.0 all-to-all-start.2
  818.9 355.9 %while.13 = (s32[]{:T(128)}, f32[128,32,128]{2,0,1:T(8,128)S(1)}, s32[32,16]{0,1:T(8,128)S(1)}, bf16[16,32,128,128]{3,2,1,0:T(8,128)(2,1)}, bf16[128,32,128]{2,0...) while((s32[]{:T(128)}, f32[128,32,128]{2,0,1:T(8,128)S(1)}, ...), condition=%wide.region_8.9_spmd, body=%wide.region_5.8_spmd.sunk | while | flops 269484224 | bytes 29362016 | solution.py:91
  825.2 4.7 scatter_fusion
  836.5 4.7 scatter_fusion.1
  847.5 4.7 scatter_fusion
  858.8 4.7 scatter_fusion.1
  881.0 4.7 scatter_fusion.1
  892.0 4.7 scatter_fusion
  903.2 4.7 scatter_fusion.1
  914.2 4.7 scatter_fusion
  925.5 4.7 scatter_fusion.1
  947.7 4.7 scatter_fusion.1
  958.7 4.7 scatter_fusion
  981.0 4.7 scatter_fusion
  1003.2 4.7 scatter_fusion
  1014.5 4.7 scatter_fusion.1
  1036.7 4.7 scatter_fusion.1
  1047.7 4.7 scatter_fusion
  1103.5 4.7 scatter_fusion.1
  1148.0 4.7 scatter_fusion.1
  1176.4 45.3 %reduce-scatter.2.cloned.1.call-done = f32[128,1024]{1,0:T(8,128)} async-done(((f32[128,4096]{1,0:T(8,128)}), f32[128,1024]{1,0:T(8,128)}) %reduce-scatter.2.cloned.1.call-update) | async-done | bytes 524304 | tf_op jit(solution)/shard_map/reduce_scatter | solution.py:92
  1223.5 12.1 reduce_sum.86
  1235.6 6.3 copy.121
  1242.0 12.1 reduce_sum.85
  1254.1 6.3 copy.120
  1260.5 12.0 reduce_sum.87
  1272.5 4.8 copy.122
  (143 shorter events, 291.1 us)
Async XLA Ops:
  7.2 33.6 %all-gather.14.cloned.1.call-start = ((), (), s32[]{:S(2)}) async-start(), calls=%async_computation.8 | async-start | bytes 1310720 | tf_op jit(solution)/shard_map/all_gather | solution.py:34
  9.0 61.4 %all-gather.10.cloned.1.call-start = ((), (), s32[]{:S(2)}) async-start(), calls=%async_computation.6 | async-start | bytes 1310720 | tf_op jit(solution)/shard_map/all_gather | solution.py:35
  10.9 166.5 %all-gather.12.cloned.1.call-start = ((), (), s32[]{:S(2)}) async-start(), calls=%async_computation.7 | async-start | bytes 20971520 | tf_op jit(solution)/shard_map/all_gather | solution.py:58
  11.6 273.2 %all-gather.6.cloned.1.call-start = ((), (), s32[]{:S(2)}) async-start(), calls=%async_computation.4 | async-start | bytes 20971520 | tf_op jit(solution)/shard_map/all_gather | solution.py:57
  12.2 379.9 %all-gather.8.cloned.1.call-start = ((), (), s32[]{:S(2)}) async-start(), calls=%async_computation.5 | async-start | bytes 20971520 | tf_op jit(solution)/shard_map/all_gather | solution.py:59
  17.0 0.6 copy-start
  17.1 0.6 copy-start.2
  431.4 190.1 %all-to-all-start.1 = ((bf16[4,4,32,128,128]{3,4,1,2,0:T(8,128)(2,1)}), bf16[4,4,32,128,128]{3,4,1,2,0:T(8,128)(2,1)}, u32[]{:S(2)}, u32[]{:S(2)}) async-start(bf16[4,4,32,128,128]{3,4,1,2,0:T(8,128)(2,1)} %copy.116), calls=%async_computation.2 | async-start | bytes 33554432 | tf_op jit(solution)/shard_map/all_to_all | solution.py:101
  464.0 164.8 %copy-start.3 = (s32[32,16]{1,0:T(8,128)S(1)}, s32[32,16]{1,0:T(8,128)}, u32[]{:S(2)}) copy-start(s32[32,16]{1,0:T(8,128)} %copy-done.2) | copy-start | bytes 6148
  464.0 164.9 %copy-start.1 = (s32[32,16]{1,0:T(8,128)S(1)}, s32[32,16]{1,0:T(8,128)}, u32[]{:S(2)}) copy-start(s32[32,16]{1,0:T(8,128)} %copy-done) | copy-start | bytes 6148
  621.5 190.1 %all-to-all-start = ((bf16[4,4,32,128,128]{3,4,1,2,0:T(8,128)(2,1)}), bf16[4,4,32,128,128]{3,4,1,2,0:T(8,128)(2,1)}, u32[]{:S(2)}, u32[]{:S(2)}) async-start(bf16[4,4,32,128,128]{3,4,1,2,0:T(8,128)(2,1)} %copy.114), calls=%async_computation.1 | async-start | bytes 33554432 | tf_op jit(solution)/shard_map/all_to_all | solution.py:100
  811.6 448.8 %all-to-all-start.2 = ((bf16[4,4,32,128,128]{4,3,1,2,0:T(8,128)(2,1)}), bf16[4,4,32,128,128]{4,3,1,2,0:T(8,128)(2,1)}, u32[]{:S(2)}, u32[]{:S(2)}) async-start(bf16[4,4,32,128,128]{4,3,1,2,0:T(8,128)(2,1)} %copy.118), calls=%async_computation.3 | async-start | bytes 33554432 | tf_op jit(solution)/shard_map/all_to_all | solution.py:103
  818.6 403.1 %reduce-scatter.2.cloned.1.call-start = ((), (), s32[]{:S(2)}) async-start(), calls=%async_computation.9 | async-start | bytes 2621440 | tf_op jit(solution)/shard_map/reduce_scatter | solution.py:92
Sparse Core Ops, SparseCore 0:
  10.1 30.6 all-gather.13
  42.9 27.4 all-gather.9
  72.0 105.3 all-gather.11
  178.8 105.9 all-gather.5
  286.2 105.9 all-gather.7
  1176.5 45.1 reduce-scatter.1
where the time goes:
time: 1290 us; the launch traced here: 1280 us
  waiting for transfers between devices  634 us (49%)
  other arithmetic  216 us (17%)
  local copies, waits for them, and re-layouts  207 us (16%)
  matrix products  191 us (15%)
  starting transfers between devices  21.6 us (2%)
  between operations  14.3 us (1%)
    all_to_all x1, waiting for transfers between devices, body(): lax.all_to_all(up_term, 'dp', split_axis=0, concat_axis=0, tiled=True)  157 us
    all_to_all x1, waiting for transfers between devices, body(): lax.all_to_all(gate_term, 'dp', split_axis=0, concat_axis=0, tiled=True)  154 us
    all_gather x1, waiting for transfers between devices, body(): lax.all_gather(gate_weight, 'dp', axis=0, tiled=True)  107 us
    all_gather x1, waiting for transfers between devices, body(): lax.all_gather(up_weight, 'dp', axis=0, tiled=True)  90.2 us
    scatter-add x16, other arithmetic, add_block(): return running.at[:, up_targets].add(up_part)  74.7 us
    scatter-add x16, other arithmetic, add_block(): running = running.at[:, gate_targets].add(gate_part)  74.7 us
    dot_general x16, matrix products, add_block(): jnp.einsum('thd,hcd->thc', up_delta, up_slice, preferred_element_type=jnp...  59.3 us
    all_gather x1, waiting for transfers between devices, body(): lax.all_gather(down_weight, 'dp', axis=0, tiled=True)  54.8 us
  transfers between devices with their start and end apart: 9, of which 8 were waited for; matrix products, arithmetic and copies ran while one was open for 43% of the time, Pallas kernels for 0%

commit v1 on v0

v1 whole, which is shorter than its diff:
```python
import functools

import jax
import jax.numpy as jnp
from jax import lax
from jax.experimental import pallas as pl
from jax.experimental.pallas import tpu as pltpu
from jax.sharding import PartitionSpec as P

BF16 = jnp.bfloat16
F32 = jnp.float32
CHUNKS = 4
VMEM_LIMIT = 60 * 1024 * 1024


def dot(a, b, dims):
    return lax.dot_general(a, b, (dims, ((), ())), preferred_element_type=F32)


def forward_kernel(n_dp, keep, per, offset, rows_ref, live_ref, *refs):
    token_refs = refs[:n_dp]
    gate_ref, up_ref, down_ref, out_ref = refs[n_dp:]
    slot = offset + pl.program_id(0)
    tokens = token_refs[0].shape[2]
    size = gate_ref.shape[-1]
    live = live_ref[slot]

    def picked(which, array):
        parts = []
        for m in range(keep):
            r = rows_ref[which, slot, m]
            column = pl.multiple_of(lax.rem(r, per) * size, size)
            parts.append(
                jnp.concatenate(
                    [ref[lax.div(r, per), array, :, pl.ds(column, size)] for ref in token_refs], axis=0
                )
            )
        return jnp.concatenate(parts, axis=1)

    def store(which, value):
        for i in range(n_dp):
            out_ref[i, which, 0] = value[i * tokens : (i + 1) * tokens].astype(BF16)

    @pl.when(live == 0)
    def _():
        out_ref[...] = jnp.zeros_like(out_ref)

    @pl.when(live != 0)
    def _():
        store(0, dot(picked(0, 0), gate_ref[:, 0].reshape(keep * size, size), ((1,), (0,))))
        store(1, dot(picked(1, 0), up_ref[:, 0].reshape(keep * size, size), ((1,), (0,))))
        down = jnp.concatenate([down_ref[m, 0] for m in range(keep)], axis=1)
        store(2, dot(picked(2, 1), down, ((1,), (1,))))


def backward_kernel(n_dp, keep, per, offset, first, rows_ref, *refs):
    count = 2 * n_dp + 3 + (0 if first else 4)
    inputs, (gg_ref, ug_ref, dg_ref, total_ref) = refs[:count], refs[count:]
    token_refs, delta_refs = inputs[:n_dp], inputs[n_dp : 2 * n_dp]
    turned_ref, gate_ref, up_ref = inputs[2 * n_dp : 2 * n_dp + 3]
    slot = offset + pl.program_id(0)
    tokens = token_refs[0].shape[2]
    size = gate_ref.shape[-1]

    @pl.when(pl.program_id(0) == 0)
    def _():
        if first:
            total_ref[...] = jnp.zeros_like(total_ref)
        else:
            total_ref[...] = inputs[-1][...]

    def whole(which):
        return jnp.concatenate([ref[which, 0] for ref in delta_refs], axis=0)

    for which, weight_ref, grad_ref in ((0, gate_ref, gg_ref), (1, up_ref, ug_ref)):
        delta = whole(which)
        left = jnp.concatenate([turned_ref[rows_ref[which, slot, m]] for m in range(keep)], axis=0)
        grad = dot(left, delta, ((1,), (0,))).astype(BF16)
        for m in range(keep):
            grad_ref[m, 0] = grad[m * size : (m + 1) * size]
        back = dot(delta, weight_ref[:, 0].reshape(keep * size, size), ((1,), (1,)))
        for m in range(keep):
            r = rows_ref[which, slot, m]
            column = pl.multiple_of(lax.rem(r, per) * size, size)
            for i in range(n_dp):
                at = (i, lax.div(r, per), slice(None), pl.ds(column, size))
                total_ref[at] = total_ref[at] + back[i * tokens : (i + 1) * tokens, m * size : (m + 1) * size]

    hidden = whole(2).T
    parts = []
    for m in range(keep):
        q = rows_ref[2, slot, m]
        column = pl.multiple_of(lax.rem(q, per) * size, size)
        parts.append(
            jnp.concatenate([ref[lax.div(q, per), 1, :, pl.ds(column, size)] for ref in token_refs], axis=0)
        )
    grad = dot(hidden, jnp.concatenate(parts, axis=1), ((1,), (0,))).astype(BF16)
    for m in range(keep):
        dg_ref[m, 0] = grad[:, m * size : (m + 1) * size]


def constant(shape):
    return pl.BlockSpec(shape, lambda s, *_: (0,) * len(shape), pipeline_mode=pl.Buffered(1))


def body(
    activations,
    output_grad,
    gate_weight,
    up_weight,
    down_weight,
    gate_rows,
    up_rows,
    down_columns,
    owner_map,
):
    tokens, features = activations.shape
    keep, slots, size, _ = gate_weight.shape
    n_dp, n_blk = lax.axis_size("dp"), lax.axis_size("blk")
    n_x = n_dp // 2
    per = features // size
    row_blocks = per * n_blk
    chunks = CHUNKS if slots % CHUNKS == 0 else 1
    part = slots // chunks

    def other_core(value):
        return lax.ppermute(value, "dp", [(i, i ^ 1) for i in range(n_dp)])

    def from_x(value, step):
        return lax.ppermute(value, "dp", [((i + 2 * step) % n_dp, i) for i in range(n_dp)])

    def gather_dp(value):
        column = [value] + [from_x(value, k) for k in range(1, n_x)]
        return column + [other_core(v) for v in column]

    def scatter_dp(mine, theirs):
        got = other_core(theirs)
        total = mine.astype(F32) + got.astype(F32)
        result = total[0]
        for k in range(1, n_x):
            result = result + from_x(total[k].astype(BF16), n_x - k).astype(F32)
        return result

    own = lax.axis_index("blk")
    owned = (owner_map == own).astype(jnp.int32)
    position = jnp.cumsum(owned) - 1
    slot_ids = jnp.arange(slots, dtype=jnp.int32)
    chosen = owned[None, :] * (position[None, :] == slot_ids[:, None]).astype(jnp.int32)
    live = jnp.sum(chosen, axis=1)
    listing = jnp.stack([gate_rows, up_rows, down_columns])
    listing = lax.dynamic_slice_in_dim(listing, lax.axis_index("dp") * keep, keep, axis=2)
    rows = jnp.sum(chosen[None, :, :, None] * listing[:, None, :, :], axis=2)

    both = lax.all_gather(jnp.stack([activations, output_grad]), "blk", axis=0)
    gathered = gather_dp(both)
    token_shape = (n_blk, 2, tokens, features)
    params = pltpu.CompilerParams(vmem_limit_bytes=VMEM_LIMIT)

    def weight_spec(offset):
        return pl.BlockSpec((keep, 1, size, size), lambda s, *_: (0, offset + s, 0, 0))

    flops = 6 * n_dp * tokens * part * keep * size * size
    moved = 3 * keep * part * size * size * 2 + 3 * n_dp * tokens * part * size * 2 + 8 * n_dp * tokens * row_blocks * size
    deltas = []
    for c in range(chunks):
        terms = pl.pallas_call(
            functools.partial(forward_kernel, n_dp, keep, per, c * part),
            grid_spec=pltpu.PrefetchScalarGridSpec(
                num_scalar_prefetch=2,
                grid=(part,),
                in_specs=[constant(token_shape)] * n_dp + [weight_spec(c * part)] * 3,
                out_specs=[
                    pl.BlockSpec((n_dp, 3, 1, tokens, size), lambda s, *_: (0, 0, s, 0, 0)),
                ],
            ),
            out_shape=[jax.ShapeDtypeStruct((n_dp, 3, part, tokens, size), BF16)],
            compiler_params=params,
            cost_estimate=pl.CostEstimate(flops=2 * flops, bytes_accessed=moved, transcendentals=0),
            name="forward",
        )(rows, live, *gathered, gate_weight, up_weight, down_weight)[0]
        value = scatter_dp(terms[:n_x], terms[n_x:])
        gate, up, back = value[0], value[1], value[2]
        sig = jax.nn.sigmoid(gate)
        act = gate * sig
        delta = jnp.stack(
            [
                (back * up * sig * (1.0 + gate * (1.0 - sig))).astype(BF16),
                (back * act).astype(BF16),
                (act * up).astype(BF16),
            ]
        )
        deltas.append(gather_dp(delta))

    turned = jnp.stack([g[:, 0] for g in gathered])
    turned = turned.reshape(n_dp, n_blk, tokens, per, size).transpose(1, 3, 4, 0, 2)
    turned = turned.reshape(row_blocks, size, n_dp * tokens)

    grad_shape = jax.ShapeDtypeStruct(gate_weight.shape, BF16)
    total_shape = (n_dp, n_blk, tokens, features)
    state = ()
    for c in range(chunks):
        first = c == 0
        base = 1 + 2 * n_dp + 3
        held = [] if first else [pl.BlockSpec(memory_space=pl.ANY)] * 3 + [constant(total_shape)]
        state = pl.pallas_call(
            functools.partial(backward_kernel, n_dp, keep, per, c * part, first),
            grid_spec=pltpu.PrefetchScalarGridSpec(
                num_scalar_prefetch=1,
                grid=(part,),
                in_specs=[constant(token_shape)] * n_dp
                + [pl.BlockSpec((3, 1, tokens, size), lambda s, *_: (0, s, 0, 0))] * n_dp
                + [constant((row_blocks, size, n_dp * tokens))]
                + [weight_spec(c * part)] * 2
                + held,
                out_specs=[weight_spec(c * part)] * 3 + [constant(total_shape)],
            ),
            out_shape=[grad_shape] * 3 + [jax.ShapeDtypeStruct(total_shape, F32)],
            input_output_aliases={} if first else {base + i: i for i in range(4)},
            compiler_params=params,
            cost_estimate=pl.CostEstimate(flops=3 * flops, bytes_accessed=2 * moved, transcendentals=0),
            name="backward",
        )(rows, *gathered, *deltas[c], turned, gate_weight, up_weight, *state)
    gate_grad, up_grad, down_grad, total = state

    summed = scatter_dp(total[:n_x], total[n_x:].astype(BF16))
    input_grad = lax.psum_scatter(summed, "blk", scatter_dimension=0, tiled=True)
    return input_grad.reshape(tokens, features).astype(BF16), gate_grad, up_grad, down_grad


def solution(mesh):
    in_specs = (
        P(("group", "dp"), "blk"),
        P(("group", "dp"), "blk"),
        P("dp", "blk", None, None),
        P("dp", "blk", None, None),
        P("dp", "blk", None, None),
        P(),
        P(),
        P(),
        P(),
    )
    out_specs = (
        P(("group", "dp"), "blk"),
        P("dp", ("group", "blk"), None, None),
        P("dp", ("group", "blk"), None, None),
        P("dp", ("group", "blk"), None, None),
    )
    return jax.shard_map(body, mesh=mesh, in_specs=in_specs, out_specs=out_specs, check_vma=False)
```

time: 1290 us -> 492 us (0.38)
  waiting for transfers between devices: 634 us -> 249 us
  matrix products: 191 us -> 0 us
  other arithmetic: 216 us -> 34.5 us
  local copies, waits for them, and re-layouts: 207 us -> 38.3 us
  Pallas kernels: 0 us -> 137 us
    all_to_all x3 -> x0, waiting for transfers between devices: 311 us -> none  [the longest x1 157 us: body(): lax.all_to_all(up_term, 'dp', split_axis=0, concat_axis=0, tiled=True)]
    all_gather x5 -> x1, waiting for transfers between devices: 275 us -> 49.7 us  [body(): both = lax.all_gather(jnp.stack([activations, output_grad]), 'blk', axis=0)]
    dot_general x38 -> x0, matrix products: 191 us -> none  [the longest x16 59.3 us: add_block(): jnp.einsum('thd,hcd->thc', up_delta, up_slice, preferred_element_type=jnp...]
    ppermute x0 -> x25, waiting for transfers between devices: none -> 157 us  [the longest x10 153 us: from_x(): lax.ppermute(value, 'dp', [((i + 2 * step) % n_dp, i) for i in range(n_dp)])]
    scatter-add x32 -> x0, other arithmetic: 149 us -> none  [the longest x16 74.7 us: add_block(): return running.at[:, up_targets].add(up_part)]
    pallas_call x0 -> x8, Pallas kernels: none -> 137 us  [the longest x4 86.2 us: body(): pl.pallas_call(functools.partial(backward_kernel, n_dp, keep, per, c * pa...]
    transpose x32 -> x0, local copies, waits for them, and re-layouts: 92.1 us -> none  [the longest x16 46.1 us: add_block(): jnp.einsum('thd,hcd->thc', gate_delta, gate_slice, preferred_element_type...]
    gather x3 -> x0, local copies, waits for them, and re-layouts: 42.9 us -> none  [the longest x1 15.2 us: body(): down_inputs = grad_blocks[:, down_lists]]
  transfers between devices with their start and end apart: 9 -> 27, of which waited for: 8 -> 12; matrix products, arithmetic and copies ran while one was open for 43% -> 11% of each run, Pallas kernels for 0% -> 21%
where the time goes in v1:
time: 492 us; the launch traced here: 489 us
  waiting for transfers between devices  249 us (51%)
  Pallas kernels  137 us (28%)
  local copies, waits for them, and re-layouts  38.3 us (8%)
  other arithmetic  34.5 us (7%)
  starting transfers between devices  16.2 us (3%)
  between operations  14.4 us (3%)
    ppermute x10, waiting for transfers between devices, from_x(): lax.ppermute(value, 'dp', [((i + 2 * step) % n_dp, i) for i in range(n_dp)])  153 us
    pallas_call x4, Pallas kernels, body(): pl.pallas_call(functools.partial(backward_kernel, n_dp, keep, per, c * pa...  86.2 us
    pallas_call x4, Pallas kernels, body(): pl.pallas_call(functools.partial(forward_kernel, n_dp, keep, per, c * par...  50.4 us
    all_gather x1, waiting for transfers between devices, body(): both = lax.all_gather(jnp.stack([activations, output_grad]), 'blk', axis=0)  49.7 us
    reduce_scatter x1, waiting for transfers between devices, body(): lax.psum_scatter(summed, 'blk', scatter_dimension=0, tiled=True)  42.2 us
    ppermute x10, starting transfers between devices, from_x(): lax.ppermute(value, 'dp', [((i + 2 * step) % n_dp, i) for i in range(n_dp)])  13.7 us
    transpose x1, other arithmetic, body(): turned.reshape(n_dp, n_blk, tokens, per, size).transpose(1, 3, 4, 0, 2)  11 us
    slice x4, local copies, waits for them, and re-layouts, body(): value = scatter_dp(terms[:n_x], terms[n_x:])  10.1 us
  transfers between devices with their start and end apart: 27, of which 12 were waited for; matrix products, arithmetic and copies ran while one was open for 11% of the time, Pallas kernels for 21%

profile of v1, /device:TPU:0, one launch (start us, length us, event | category | flops | bytes accessed | tf_op | source)
XLA Modules:
  0.0 488.8 jit_solution(10816957758302689742)
XLA Ops:
  7.2 1.9 pad_maximum_fusion.4
  9.2 49.7 %all-gather.3.cloned.1.call-done = bf16[8,128,1024]{2,1,0:T(8,128)(2,1)} async-done(((bf16[2,128,1024]{2,1,0:T(8,128)(2,1)}), bf16[8,128,1024]{2,1,0:T(8,128)(2,1)}) %all-gather.3.cloned.1.call-update) | async-done | bytes 2097168 | tf_op jit(solution)/shard_map/all_gather | solution.py:154
  58.8 1.5 collective-permute-start
  60.3 46.1 %collective-permute-done.refs_1_ = bf16[4,2,128,1024]{3,2,1,0:T(8,128)(2,1)S(1)} collective-permute-done((bf16[4,2,128,1024]{3,2,1,0:T(8,128)(2,1)}, bf16[4,2,128,1024]{3,2,1,0:T(8,128)(2,1)S(1)}, u32[]{:S(2)}, u32[]{:S(2)}) %collective-permute-start) | collective-permute-done | bytes 2097184 | tf_op jit(solution)/shard_map/ppermute | solution.py:130
  110.7 12.6 %forward.7 = bf16[4,3,8,128,128]{4,3,2,1,0:T(8,128)(2,1)} custom-call(s32[3,32,4]{2,1,0:T(8,128)} %copy.55.rows_ref, s32[32]{0:T(128)} %get-tuple-element.48.live_ref, bf16[4,2,128,1024]{3,2,1,0:T(8,128)(2,1)} %bitcast.64, bf16[4,2,128,1024]{3,2,1,0:T(8,128)(2,1)} %copy-done.1, bf16[4,2,128,1024]{3,2,1,0:T(8,128)(2,1)} %collective-permute-done.1.refs_2_, ...), custom_call_target="tpu_custom_call" | custom-call | flops 3221225472 | bytes 23068672 | tf_op jit(solution)/shard_map/forward/pallas_call | solution.py:166
  123.3 2.7 slice.176
  126.3 12.6 %forward.6 = bf16[4,3,8,128,128]{4,3,2,1,0:T(8,128)(2,1)} custom-call(s32[3,32,4]{2,1,0:T(8,128)} %copy.55.rows_ref, s32[32]{0:T(128)} %get-tuple-element.48.live_ref, bf16[4,2,128,1024]{3,2,1,0:T(8,128)(2,1)} %bitcast.65, bf16[4,2,128,1024]{3,2,1,0:T(8,128)(2,1)} %copy-done.1, bf16[4,2,128,1024]{3,2,1,0:T(8,128)(2,1)} %collective-permute-done.1.refs_2_, ...), custom_call_target="tpu_custom_call" | custom-call | flops 3221225472 | bytes 23068672 | tf_op jit(solution)/shard_map/forward/pallas_call | solution.py:166
  138.9 2.9 slice.169
  142.4 2.6 copy.45
  145.3 1.2 copy.46
  146.6 1.3 slice.159
  148.1 2.5 copy.47
  150.7 1.3 slice.160
  152.3 2.6 copy.48
  154.8 12.6 %forward.5 = bf16[4,3,8,128,128]{4,3,2,1,0:T(8,128)(2,1)} custom-call(s32[3,32,4]{2,1,0:T(8,128)} %copy.55.rows_ref, s32[32]{0:T(128)} %get-tuple-element.48.live_ref, bf16[4,2,128,1024]{3,2,1,0:T(8,128)(2,1)} %bitcast.66, bf16[4,2,128,1024]{3,2,1,0:T(8,128)(2,1)} %copy-done.1, bf16[4,2,128,1024]{3,2,1,0:T(8,128)(2,1)} %collective-permute-done.1.refs_2_, ...), custom_call_target="tpu_custom_call" | custom-call | flops 3221225472 | bytes 23068672 | tf_op jit(solution)/shard_map/forward/pallas_call | solution.py:166
  167.4 2.8 slice.162
  170.5 12.6 %forward.4 = bf16[4,3,8,128,128]{4,3,2,1,0:T(8,128)(2,1)} custom-call(s32[3,32,4]{2,1,0:T(8,128)} %copy.55.rows_ref, s32[32]{0:T(128)} %get-tuple-element.48.live_ref, bf16[4,2,128,1024]{3,2,1,0:T(8,128)(2,1)} %bitcast.67, bf16[4,2,128,1024]{3,2,1,0:T(8,128)(2,1)} %copy-done.1, bf16[4,2,128,1024]{3,2,1,0:T(8,128)(2,1)} %collective-permute-done.1.refs_2_, ...), custom_call_target="tpu_custom_call" | custom-call | flops 3221225472 | bytes 23068672 | tf_op jit(solution)/shard_map/forward/pallas_call | solution.py:166
  183.1 1.7 slice.151
  185.5 2.2 convert_add_fusion.1
  187.8 1.6 collective-permute-start.19
  189.4 2.0 convert_add_fusion.2
  192.4 2.0 convert_add_fusion.3
  194.6 1.2 collective-permute-start.9
  197.5 10.8 %collective-permute-done.19 = bf16[3,8,128,128]{3,2,1,0:T(8,128)(2,1)S(1)} collective-permute-done((bf16[3,8,128,128]{3,2,1,0:T(8,128)(2,1)S(1)}, bf16[3,8,128,128]{3,2,1,0:T(8,128)(2,1)S(1)}, u32[]{:S(2)}, u32[]{:S(2)}) %collective-permute-start.19) | collective-permute-done | bytes 786464 | tf_op jit(solution)/shard_map/ppermute | solution.py:130
  208.9 1.6 collective-permute-start.20
  210.4 14.7 %collective-permute-done.14 = bf16[3,8,128,128]{3,2,1,0:T(8,128)(2,1)S(1)} collective-permute-done((bf16[3,8,128,128]{3,2,1,0:T(8,128)(2,1)S(1)}, bf16[3,8,128,128]{3,2,1,0:T(8,128)(2,1)S(1)}, u32[]{:S(2)}, u32[]{:S(2)}) %collective-permute-start.14) | collective-permute-done | bytes 786464 | tf_op jit(solution)/shard_map/ppermute | solution.py:130
  225.6 1.1 pad_maximum_fusion.2.refs_4_
  226.7 1.5 collective-permute-start.15
  228.2 13.8 %collective-permute-done.9 = bf16[3,8,128,128]{3,2,1,0:T(8,128)(2,1)S(1)} collective-permute-done((bf16[3,8,128,128]{3,2,1,0:T(8,128)(2,1)S(1)}, bf16[3,8,128,128]{3,2,1,0:T(8,128)(2,1)S(1)}, u32[]{:S(2)}, u32[]{:S(2)}) %collective-permute-start.9) | collective-permute-done | bytes 786464 | tf_op jit(solution)/shard_map/ppermute | solution.py:130
  243.5 15.3 %collective-permute-done.4 = bf16[3,8,128,128]{3,2,1,0:T(8,128)(2,1)S(1)} collective-permute-done((bf16[3,8,128,128]{3,2,1,0:T(8,128)(2,1)S(1)}, bf16[3,8,128,128]{3,2,1,0:T(8,128)(2,1)S(1)}, u32[]{:S(2)}, u32[]{:S(2)}) %collective-permute-start.4) | collective-permute-done | bytes 786464 | tf_op jit(solution)/shard_map/ppermute | solution.py:130
  258.8 1.5 collective-permute-start.10
  261.8 13.9 %collective-permute-done.20.refs_5_ = bf16[3,8,128,128]{3,2,1,0:T(8,128)(2,1)} collective-permute-done((bf16[3,8,128,128]{3,2,1,0:T(8,128)(2,1)S(1)}, bf16[3,8,128,128]{3,2,1,0:T(8,128)(2,1)}, u32[]{:S(2)}, u32[]{:S(2)}) %collective-permute-start.20) | collective-permute-done | bytes 786464 | tf_op jit(solution)/shard_map/ppermute | solution.py:130
  275.8 1.5 collective-permute-start.5
  278.1 14.5 %collective-permute-done.15.refs_5_ = bf16[3,8,128,128]{3,2,1,0:T(8,128)(2,1)} collective-permute-done((bf16[3,8,128,128]{3,2,1,0:T(8,128)(2,1)}, bf16[3,8,128,128]{3,2,1,0:T(8,128)(2,1)}, u32[]{:S(2)}, u32[]{:S(2)}) %collective-permute-start.15) | collective-permute-done | bytes 786464 | tf_op jit(solution)/shard_map/ppermute | solution.py:130
  292.6 11.0 %maximum_bitcast_fusion = bf16[4,8,128,4,128]{4,3,2,1,0:T(4,128)(2,1)} fusion(bf16[1,4,128,8,128]{2,0,4,3,1:T(2,128)(2,1)S(1)} %copy-done.9, bf16[1,4,128,8,128]{2,0,4,3,1:T(2,128)(2,1)S(1)} %copy-done.8, bf16[1,4,128,8,128]{2,0,4,3,1:T(2,128)(2,1)S(1)} %copy.46, bf16[1,4,128,8,128]{2,0,4,3,1:T(2,128)(2,1)S(1)} %copy-done.7), kind=kLoop, calls=%fused_computation.1 | loop fusion | flops 16777216 | bytes 8388608 | tf_op jit(solution)/shard_map/transpose | solution.py:195
  303.6 7.2 %reshape.93.refs_8_ = bf16[32,128,512]{2,1,0:T(8,128)(2,1)} reshape(bf16[4,8,128,4,128]{4,3,2,1,0:T(4,128)(2,1)} %maximum_bitcast_fusion) | data formatting | bytes 8388608 | tf_op jit(solution)/shard_map/reshape | solution.py:196
  312.2 19.7 %backward.4 = (bf16[4,32,128,128]{3,2,1,0:T(8,128)(2,1)}, bf16[4,32,128,128]{3,2,1,0:T(8,128)(2,1)}, bf16[4,32,128,128]{3,2,1,0:T(8,128)(2,1)}, f32[4,4,128,1024]{3,2,1,0:T(8,128)}) custom-call(s32[3,32,4]{2,1,0:T(8,128)} %copy.55.rows_ref, bf16[4,2,128,1024]{3,2,1,0:T(8,128)(2,1)} %bitcast.68, bf16[4,2,128,1024]{3,2,1,0:T(8,128)(2,1)} %copy-done.1, ...), custom_call_target="tpu_custom_call" | custom-call | flops 4831838208 | bytes 46137344 | tf_op jit(solution)/shard_map/backward/pallas_call | solution.py:205
  332.5 22.2 %backward.5 = (bf16[4,32,128,128]{3,2,1,0:T(8,128)(2,1)}, bf16[4,32,128,128]{3,2,1,0:T(8,128)(2,1)}, bf16[4,32,128,128]{3,2,1,0:T(8,128)(2,1)}, f32[4,4,128,1024]{3,2,1,0:T(8,128)}) custom-call(s32[3,32,4]{2,1,0:T(8,128)} %copy.55.rows_ref, ...), custom_call_target="tpu_custom_call", output_to_operand_aliasing={{0}: (12, {}), {1}: (13, {}), {2}: (14, {}), {3}: (15, {})} | custom-call | flops 4831838208 | bytes 46137344 | tf_op jit(solution)/shard_map/backward/pallas_call | solution.py:205
  355.7 22.2 %backward.6 = (bf16[4,32,128,128]{3,2,1,0:T(8,128)(2,1)}, bf16[4,32,128,128]{3,2,1,0:T(8,128)(2,1)}, bf16[4,32,128,128]{3,2,1,0:T(8,128)(2,1)}, f32[4,4,128,1024]{3,2,1,0:T(8,128)}) custom-call(s32[3,32,4]{2,1,0:T(8,128)} %copy.55.rows_ref, ...), custom_call_target="tpu_custom_call", output_to_operand_aliasing={{0}: (12, {}), {1}: (13, {}), {2}: (14, {}), {3}: (15, {})} | custom-call | flops 4831838208 | bytes 46137344 | tf_op jit(solution)/shard_map/backward/pallas_call | solution.py:205
  379.0 22.2 %backward.7 = (bf16[4,32,128,128]{3,2,1,0:T(8,128)(2,1)}, bf16[4,32,128,128]{3,2,1,0:T(8,128)(2,1)}, bf16[4,32,128,128]{3,2,1,0:T(8,128)(2,1)}, f32[4,4,128,1024]{3,2,1,0:T(8,128)}) custom-call(s32[3,32,4]{2,1,0:T(8,128)} %copy.55.rows_ref, ...), custom_call_target="tpu_custom_call", output_to_operand_aliasing={{0}: (12, {}), {1}: (13, {}), {2}: (14, {}), {3}: (15, {})} | custom-call | flops 4831838208 | bytes 46137344 | tf_op jit(solution)/shard_map/backward/pallas_call | solution.py:205
  401.2 2.5 slice.261
  403.9 4.0 collective-permute-done.23
  407.9 2.9 convert_add_fusion
  411.0 1.6 collective-permute-start.24
  412.6 23.7 %collective-permute-done.24 = bf16[4,128,1024]{2,1,0:T(8,128)(2,1)S(1)} collective-permute-done((bf16[4,128,1024]{2,1,0:T(8,128)(2,1)S(1)}, bf16[4,128,1024]{2,1,0:T(8,128)(2,1)S(1)}, u32[]{:S(2)}, u32[]{:S(2)}) %collective-permute-start.24) | collective-permute-done | bytes 1048608 | tf_op jit(solution)/shard_map/ppermute | solution.py:130
  436.3 1.7 fusion
  438.0 42.2 %reduce-scatter.2.cloned.1.call-done = f32[1,128,1024]{2,1,0:T(8,128)} async-done(((f32[4,128,1024]{2,1,0:T(8,128)}), f32[1,128,1024]{2,1,0:T(8,128)}) %reduce-scatter.2.cloned.1.call-update) | async-done | bytes 524304 | tf_op jit(solution)/shard_map/reduce_scatter | solution.py:226
  480.2 1.8 convert_bitcast_fusion
  (101 shorter events, 19.6 us)
Async XLA Ops:
  7.2 51.6 %all-gather.3.cloned.1.call-start = ((), (), s32[]{:S(2)}) async-start(), calls=%async_computation.2 | async-start | bytes 2621440 | tf_op jit(solution)/shard_map/all_gather | solution.py:154
  9.1 471.1 %reduce-scatter.2.cloned.1.call-start = ((), (), s32[]{:S(2)}) async-start(), calls=%async_computation.1 | async-start | bytes 2621440 | tf_op jit(solution)/shard_map/reduce_scatter | solution.py:226
  58.8 47.6 %collective-permute-start = (bf16[4,2,128,1024]{3,2,1,0:T(8,128)(2,1)}, bf16[4,2,128,1024]{3,2,1,0:T(8,128)(2,1)S(1)}, u32[]{:S(2)}, u32[]{:S(2)}) collective-permute-start(bf16[4,2,128,1024]{3,2,1,0:T(8,128)(2,1)} %bitcast.62), channel_id=1, source_target_pairs={{2,0},{3,1},{0,2},{1,3},{6,4},{7,5},{4,6},{5,7},{10,8},{11,9},{8,1... | collective-permute-start | bytes 6291464 | tf_op jit(solution)/shard_map/ppermute | solution.py:130
  60.3 50.2 %collective-permute-start.1 = (bf16[4,2,128,1024]{3,2,1,0:T(8,128)(2,1)}, bf16[4,2,128,1024]{3,2,1,0:T(8,128)(2,1)}, u32[]{:S(2)}, u32[]{:S(2)}) collective-permute-start(bf16[4,2,128,1024]{3,2,1,0:T(8,128)(2,1)} %bitcast.63), channel_id=1, source_target_pairs={{0,1},{1,0},{2,3},{3,2},{4,5},{5,4},{6,7},{7,6},{8,9},{9,8},{10,11... | collective-permute-start | bytes 6291464 | tf_op jit(solution)/shard_map/ppermute | solution.py:127
  106.4 4.3 copy-start.1
  106.4 4.3 collective-permute-start.2
  126.0 59.0 %collective-permute-start.18 = (bf16[2,3,8,128,128]{4,3,2,1,0:T(8,128)(2,1)}, bf16[2,3,8,128,128]{4,3,2,1,0:T(8,128)(2,1)}, u32[]{:S(2)}, u32[]{:S(2)}) collective-permute-start(bf16[2,3,8,128,128]{4,3,2,1,0:T(8,128)(2,1)} %slice.176), channel_id=1, source_target_pairs={{0,1},{1,0},{2,3},{3,2},{4,5},{5,4},{6,7},{7,6},{8,9},{9,8},{10,11... | collective-permute-start | bytes 4718600 | tf_op jit(solution)/shard_map/ppermute | solution.py:127
  138.9 3.1 copy-start
  141.8 47.6 %collective-permute-start.13 = (bf16[2,3,8,128,128]{4,3,2,1,0:T(8,128)(2,1)}, bf16[2,3,8,128,128]{4,3,2,1,0:T(8,128)(2,1)}, u32[]{:S(2)}, u32[]{:S(2)}) collective-permute-start(bf16[2,3,8,128,128]{4,3,2,1,0:T(8,128)(2,1)} %slice.169), channel_id=1, source_target_pairs={{0,1},{1,0},{2,3},{3,2},{4,5},{5,4},{6,7},{7,6},{8,9},{9,8},{10,11... | collective-permute-start | bytes 4718600 | tf_op jit(solution)/shard_map/ppermute | solution.py:127
  142.1 2.9 copy-start.2
  170.2 22.2 %collective-permute-start.8 = (bf16[2,3,8,128,128]{4,3,2,1,0:T(8,128)(2,1)}, bf16[2,3,8,128,128]{4,3,2,1,0:T(8,128)(2,1)}, u32[]{:S(2)}, u32[]{:S(2)}) collective-permute-start(bf16[2,3,8,128,128]{4,3,2,1,0:T(8,128)(2,1)} %slice.162), channel_id=1, source_target_pairs={{0,1},{1,0},{2,3},{3,2},{4,5},{5,4},{6,7},{7,6},{8,9},{9,8},{10,11... | collective-permute-start | bytes 4718600 | tf_op jit(solution)/shard_map/ppermute | solution.py:127
  183.1 2.4 copy-start.4
  184.8 4.6 copy-start.3
  184.8 11.0 %collective-permute-start.3 = (bf16[2,3,8,128,128]{4,3,2,1,0:T(8,128)(2,1)S(1)}, bf16[2,3,8,128,128]{4,3,2,1,0:T(8,128)(2,1)S(1)}, u32[]{:S(2)}, u32[]{:S(2)}) collective-permute-start(bf16[2,3,8,128,128]{4,3,2,1,0:T(8,128)(2,1)S(1)} %slice.151), channel_id=1, source_target_pairs={{0,1},{1,0},{2,3},{3,2},{4,5},{5,4},{6,7},{7,6},{8,9},{9,8},{10,11... | collective-permute-start | bytes 4718600 | tf_op jit(solution)/shard_map/ppermute | solution.py:127
  187.8 4.6 copy-start.6
  187.8 20.4 %collective-permute-start.19 = (bf16[3,8,128,128]{3,2,1,0:T(8,128)(2,1)S(1)}, bf16[3,8,128,128]{3,2,1,0:T(8,128)(2,1)S(1)}, u32[]{:S(2)}, u32[]{:S(2)}) collective-permute-start(bf16[3,8,128,128]{3,2,1,0:T(8,128)(2,1)S(1)} %fusion.9), channel_id=1, source_target_pairs={{2,0},{3,1},{0,2},{1,3},{6,4},{7,5},{4,6},{5,7},{10,8},{11,9},{8,1... | collective-permute-start | bytes 2359304 | tf_op jit(solution)/shard_map/ppermute | solution.py:130
  191.5 4.3 copy-start.5
  191.5 33.6 %collective-permute-start.14 = (bf16[3,8,128,128]{3,2,1,0:T(8,128)(2,1)S(1)}, bf16[3,8,128,128]{3,2,1,0:T(8,128)(2,1)S(1)}, u32[]{:S(2)}, u32[]{:S(2)}) collective-permute-start(bf16[3,8,128,128]{3,2,1,0:T(8,128)(2,1)S(1)} %fusion.8), channel_id=1, source_target_pairs={{2,0},{3,1},{0,2},{1,3},{6,4},{7,5},{4,6},{5,7},{10,8},{11,9},{8,1... | collective-permute-start | bytes 2359304 | tf_op jit(solution)/shard_map/ppermute | solution.py:130
  194.6 47.4 %collective-permute-start.9 = (bf16[3,8,128,128]{3,2,1,0:T(8,128)(2,1)S(1)}, bf16[3,8,128,128]{3,2,1,0:T(8,128)(2,1)S(1)}, u32[]{:S(2)}, u32[]{:S(2)}) collective-permute-start(bf16[3,8,128,128]{3,2,1,0:T(8,128)(2,1)S(1)} %fusion.7), channel_id=1, source_target_pairs={{2,0},{3,1},{0,2},{1,3},{6,4},{7,5},{4,6},{5,7},{10,8},{11,9},{8,1... | collective-permute-start | bytes 2359304 | tf_op jit(solution)/shard_map/ppermute | solution.py:130
  196.5 62.3 %collective-permute-start.4 = (bf16[3,8,128,128]{3,2,1,0:T(8,128)(2,1)S(1)}, bf16[3,8,128,128]{3,2,1,0:T(8,128)(2,1)S(1)}, u32[]{:S(2)}, u32[]{:S(2)}) collective-permute-start(bf16[3,8,128,128]{3,2,1,0:T(8,128)(2,1)S(1)} %fusion.6), channel_id=1, source_target_pairs={{2,0},{3,1},{0,2},{1,3},{6,4},{7,5},{4,6},{5,7},{10,8},{11,9},{8,1... | collective-permute-start | bytes 2359304 | tf_op jit(solution)/shard_map/ppermute | solution.py:130
  208.9 16.8 %copy-start.10 = (bf16[3,8,128,128]{3,2,1,0:T(8,128)(2,1)}, bf16[3,8,128,128]{3,2,1,0:T(8,128)(2,1)S(1)}, u32[]{:S(2)}) copy-start(bf16[3,8,128,128]{3,2,1,0:T(8,128)(2,1)S(1)} %pad_maximum_fusion.3.refs_4_) | copy-start | bytes 2359300
  208.9 66.9 %collective-permute-start.20 = (bf16[3,8,128,128]{3,2,1,0:T(8,128)(2,1)S(1)}, bf16[3,8,128,128]{3,2,1,0:T(8,128)(2,1)}, u32[]{:S(2)}, u32[]{:S(2)}) collective-permute-start(bf16[3,8,128,128]{3,2,1,0:T(8,128)(2,1)S(1)} %pad_maximum_fusion.3.refs_4_), channel_id=1, source_target_pairs={{2,0},{3,1},{0,2},{1,3},{6,4},{7,5},{4,6},{5,7},{10,8},{11,9},{8,1... | collective-permute-start | bytes 2359304 | tf_op jit(solution)/shard_map/ppermute | solution.py:130
  210.4 66.8 %collective-permute-start.21 = (bf16[3,8,128,128]{3,2,1,0:T(8,128)(2,1)S(1)}, bf16[3,8,128,128]{3,2,1,0:T(8,128)(2,1)S(1)}, u32[]{:S(2)}, u32[]{:S(2)}) collective-permute-start(bf16[3,8,128,128]{3,2,1,0:T(8,128)(2,1)S(1)} %pad_maximum_fusion.3.refs_4_), channel_id=1, source_target_pairs={{0,1},{1,0},{2,3},{3,2},{4,5},{5,4},{6,7},{7,6},{8,9},{9,8},{10,11... | collective-permute-start | bytes 2359304 | tf_op jit(solution)/shard_map/ppermute | solution.py:127
  226.7 65.9 %collective-permute-start.15 = (bf16[3,8,128,128]{3,2,1,0:T(8,128)(2,1)}, bf16[3,8,128,128]{3,2,1,0:T(8,128)(2,1)}, u32[]{:S(2)}, u32[]{:S(2)}) collective-permute-start(bf16[3,8,128,128]{3,2,1,0:T(8,128)(2,1)} %pad_maximum_fusion.2.refs_4_), channel_id=1, source_target_pairs={{2,0},{3,1},{0,2},{1,3},{6,4},{7,5},{4,6},{5,7},{10,8},{11,9},{8,1... | collective-permute-start | bytes 2359304 | tf_op jit(solution)/shard_map/ppermute | solution.py:130
  241.9 90.0 %collective-permute-start.16 = (bf16[3,8,128,128]{3,2,1,0:T(8,128)(2,1)}, bf16[3,8,128,128]{3,2,1,0:T(8,128)(2,1)}, u32[]{:S(2)}, u32[]{:S(2)}) collective-permute-start(bf16[3,8,128,128]{3,2,1,0:T(8,128)(2,1)} %pad_maximum_fusion.2.refs_4_), channel_id=1, source_target_pairs={{0,1},{1,0},{2,3},{3,2},{4,5},{5,4},{6,7},{7,6},{8,9},{9,8},{10,11... | collective-permute-start | bytes 2359304 | tf_op jit(solution)/shard_map/ppermute | solution.py:127
  243.5 49.2 %copy-start.7 = (bf16[1,4,128,8,128]{2,0,4,3,1:T(2,128)(2,1)S(1)}, bf16[1,4,128,8,128]{2,0,4,3,1:T(2,128)(2,1)}, u32[]{:S(2)}) copy-start(bf16[1,4,128,8,128]{2,0,4,3,1:T(2,128)(2,1)} %copy.45) | copy-start | bytes 3145732
  243.5 49.2 %copy-start.8 = (bf16[1,4,128,8,128]{2,0,4,3,1:T(2,128)(2,1)S(1)}, bf16[1,4,128,8,128]{2,0,4,3,1:T(2,128)(2,1)}, u32[]{:S(2)}) copy-start(bf16[1,4,128,8,128]{2,0,4,3,1:T(2,128)(2,1)} %copy.47) | copy-start | bytes 3145732
  243.5 49.2 %copy-start.9 = (bf16[1,4,128,8,128]{2,0,4,3,1:T(2,128)(2,1)S(1)}, bf16[1,4,128,8,128]{2,0,4,3,1:T(2,128)(2,1)}, u32[]{:S(2)}) copy-start(bf16[1,4,128,8,128]{2,0,4,3,1:T(2,128)(2,1)} %copy.48) | copy-start | bytes 3145732
  258.8 52.0 %collective-permute-start.10 = (bf16[3,8,128,128]{3,2,1,0:T(8,128)(2,1)}, bf16[3,8,128,128]{3,2,1,0:T(8,128)(2,1)}, u32[]{:S(2)}, u32[]{:S(2)}) collective-permute-start(bf16[3,8,128,128]{3,2,1,0:T(8,128)(2,1)} %pad_maximum_fusion.1.refs_4_), channel_id=1, source_target_pairs={{2,0},{3,1},{0,2},{1,3},{6,4},{7,5},{4,6},{5,7},{10,8},{11,9},{8,1... | collective-permute-start | bytes 2359304 | tf_op jit(solution)/shard_map/ppermute | solution.py:130
  275.8 56.3 %collective-permute-start.5 = (bf16[3,8,128,128]{3,2,1,0:T(8,128)(2,1)}, bf16[3,8,128,128]{3,2,1,0:T(8,128)(2,1)}, u32[]{:S(2)}, u32[]{:S(2)}) collective-permute-start(bf16[3,8,128,128]{3,2,1,0:T(8,128)(2,1)} %pad_maximum_fusion.refs_4_), channel_id=1, source_target_pairs={{2,0},{3,1},{0,2},{1,3},{6,4},{7,5},{4,6},{5,7},{10,8},{11,9},{8,1... | collective-permute-start | bytes 2359304 | tf_op jit(solution)/shard_map/ppermute | solution.py:130
  277.3 0.9 copy-start.11
  278.1 33.2 %collective-permute-start.22 = (bf16[3,8,128,128]{3,2,1,0:T(8,128)(2,1)}, bf16[3,8,128,128]{3,2,1,0:T(8,128)(2,1)S(1)}, u32[]{:S(2)}, u32[]{:S(2)}) collective-permute-start(bf16[3,8,128,128]{3,2,1,0:T(8,128)(2,1)} %collective-permute-done.20.refs_5_), channel_id=1, source_target_pairs={{0,1},{1,0},{2,3},{3,2},{4,5},{5,4},{6,7},{7,6},{8,9},{9,8},{10,11... | collective-permute-start | bytes 2359304 | tf_op jit(solution)/shard_map/ppermute | solution.py:127
  292.6 39.9 %collective-permute-start.17 = (bf16[3,8,128,128]{3,2,1,0:T(8,128)(2,1)}, bf16[3,8,128,128]{3,2,1,0:T(8,128)(2,1)}, u32[]{:S(2)}, u32[]{:S(2)}) collective-permute-start(bf16[3,8,128,128]{3,2,1,0:T(8,128)(2,1)} %collective-permute-done.15.refs_5_), channel_id=1, source_target_pairs={{0,1},{1,0},{2,3},{3,2},{4,5},{5,4},{6,7},{7,6},{8,9},{9,8},{10,11... | collective-permute-start | bytes 2359304 | tf_op jit(solution)/shard_map/ppermute | solution.py:127
  310.8 43.9 %collective-permute-start.11 = (bf16[3,8,128,128]{3,2,1,0:T(8,128)(2,1)}, bf16[3,8,128,128]{3,2,1,0:T(8,128)(2,1)S(1)}, u32[]{:S(2)}, u32[]{:S(2)}) collective-permute-start(bf16[3,8,128,128]{3,2,1,0:T(8,128)(2,1)} %pad_maximum_fusion.1.refs_4_), channel_id=1, source_target_pairs={{0,1},{1,0},{2,3},{3,2},{4,5},{5,4},{6,7},{7,6},{8,9},{9,8},{10,11... | collective-permute-start | bytes 2359304 | tf_op jit(solution)/shard_map/ppermute | solution.py:127
  311.3 0.9 copy-start.12
  311.3 43.4 %collective-permute-start.12 = (bf16[3,8,128,128]{3,2,1,0:T(8,128)(2,1)}, bf16[3,8,128,128]{3,2,1,0:T(8,128)(2,1)}, u32[]{:S(2)}, u32[]{:S(2)}) collective-permute-start(bf16[3,8,128,128]{3,2,1,0:T(8,128)(2,1)} %collective-permute-done.10.refs_5_), channel_id=1, source_target_pairs={{0,1},{1,0},{2,3},{3,2},{4,5},{5,4},{6,7},{7,6},{8,9},{9,8},{10,11... | collective-permute-start | bytes 2359304 | tf_op jit(solution)/shard_map/ppermute | solution.py:127
  332.0 45.9 %collective-permute-start.6 = (bf16[3,8,128,128]{3,2,1,0:T(8,128)(2,1)}, bf16[3,8,128,128]{3,2,1,0:T(8,128)(2,1)S(1)}, u32[]{:S(2)}, u32[]{:S(2)}) collective-permute-start(bf16[3,8,128,128]{3,2,1,0:T(8,128)(2,1)} %pad_maximum_fusion.refs_4_), channel_id=1, source_target_pairs={{0,1},{1,0},{2,3},{3,2},{4,5},{5,4},{6,7},{7,6},{8,9},{9,8},{10,11... | collective-permute-start | bytes 2359304 | tf_op jit(solution)/shard_map/ppermute | solution.py:127
  332.1 45.8 %collective-permute-start.7 = (bf16[3,8,128,128]{3,2,1,0:T(8,128)(2,1)}, bf16[3,8,128,128]{3,2,1,0:T(8,128)(2,1)S(1)}, u32[]{:S(2)}, u32[]{:S(2)}) collective-permute-start(bf16[3,8,128,128]{3,2,1,0:T(8,128)(2,1)} %collective-permute-done.5.refs_5_), channel_id=1, source_target_pairs={{0,1},{1,0},{2,3},{3,2},{4,5},{5,4},{6,7},{7,6},{8,9},{9,8},{10,11... | collective-permute-start | bytes 2359304 | tf_op jit(solution)/shard_map/ppermute | solution.py:127
  354.7 1.0 copy-start.14
  377.9 0.9 copy-start.13
  377.9 1.1 copy-start.15
  403.7 4.2 collective-permute-start.23
  411.0 25.3 %collective-permute-start.24 = (bf16[4,128,1024]{2,1,0:T(8,128)(2,1)S(1)}, bf16[4,128,1024]{2,1,0:T(8,128)(2,1)S(1)}, u32[]{:S(2)}, u32[]{:S(2)}) collective-permute-start(bf16[4,128,1024]{2,1,0:T(8,128)(2,1)S(1)} %fusion.5), channel_id=1, source_target_pairs={{2,0},{3,1},{0,2},{1,3},{6,4},{7,5},{4,6},{5,7},{10,8},{11,9},{8,1... | collective-permute-start | bytes 3145736 | tf_op jit(solution)/shard_map/ppermute | solution.py:130
Sparse Core Ops, SparseCore 0:
  10.1 48.6 all-gather.2
  438.2 41.9 reduce-scatter.1

commit v2 on v1

v2 whole, which is shorter than its diff:
```python
import functools

import jax
import jax.numpy as jnp
from jax import lax
from jax.experimental import pallas as pl
from jax.experimental.pallas import tpu as pltpu
from jax.sharding import PartitionSpec as P

BF16 = jnp.bfloat16
F32 = jnp.float32
CHUNKS = 4
VMEM_LIMIT = 60 * 1024 * 1024


def dot(a, b, dims):
    return lax.dot_general(a, b, (dims, ((), ())), preferred_element_type=F32)


def picked(refs, rows_ref, which, slot, m, per, size):
    r = rows_ref[which, slot, m]
    column = pl.multiple_of(lax.rem(r, per) * size, size)
    return jnp.concatenate([ref[lax.div(r, per), :, pl.ds(column, size)] for ref in refs], axis=0)


def forward_kernel(n_dp, keep, per, offset, rows_ref, live_ref, *refs):
    token_refs, cotangent_refs = refs[:n_dp], refs[n_dp : 2 * n_dp]
    gate_ref, up_ref, down_ref, mine_ref, theirs_ref = refs[2 * n_dp :]
    slot = offset + pl.program_id(0)
    tokens = token_refs[0].shape[1]
    size = gate_ref.shape[-1]
    live = live_ref[slot]

    def side(refs, which):
        parts = [picked(refs, rows_ref, which, slot, m, per, size) for m in range(keep)]
        return jnp.concatenate(parts, axis=1)

    def store(which, value):
        for i in range(n_dp // 2):
            mine_ref[i, which, 0] = value[i * tokens : (i + 1) * tokens]
            j = n_dp // 2 + i
            theirs_ref[i, which, 0] = value[j * tokens : (j + 1) * tokens].astype(BF16)

    @pl.when(live == 0)
    def _():
        mine_ref[...] = jnp.zeros_like(mine_ref)
        theirs_ref[...] = jnp.zeros_like(theirs_ref)

    @pl.when(live != 0)
    def _():
        store(0, dot(side(token_refs, 0), gate_ref[:, 0].reshape(keep * size, size), ((1,), (0,))))
        store(1, dot(side(token_refs, 1), up_ref[:, 0].reshape(keep * size, size), ((1,), (0,))))
        down = jnp.concatenate([down_ref[m, 0] for m in range(keep)], axis=1)
        store(2, dot(side(cotangent_refs, 2), down, ((1,), (1,))))


def delta_kernel(mine_ref, got_ref, *refs):
    from_refs, out_ref = refs[:-1], refs[-1]

    def total(which):
        value = mine_ref[0, which, 0] + got_ref[0, which, 0].astype(F32)
        for ref in from_refs:
            value = value + ref[which, 0].astype(F32)
        return value

    gate, up, back = total(0), total(1), total(2)
    sig = 1.0 / (1.0 + jnp.exp(-gate))
    act = gate * sig
    out_ref[0, 0] = (back * up * sig * (1.0 + gate * (1.0 - sig))).astype(BF16)
    out_ref[1, 0] = (back * act).astype(BF16)
    out_ref[2, 0] = (act * up).astype(BF16)


def turn_kernel(*refs):
    refs, out_ref = refs[:-1], refs[-1]
    out_ref[0] = jnp.concatenate([ref[0].T for ref in refs], axis=1)


def input_kernel(n_dp, keep, per, offset, first, rows_ref, *refs):
    count = n_dp + 2 + (0 if first else 2)
    inputs, totals = refs[:count], refs[count:]
    delta_refs, (gate_ref, up_ref) = inputs[:n_dp], inputs[n_dp : n_dp + 2]
    slot = offset + pl.program_id(0)
    tokens, size = delta_refs[0].shape[2], gate_ref.shape[-1]
    n_x = n_dp // 2

    @pl.when(pl.program_id(0) == 0)
    def _():
        for i, ref in enumerate(totals):
            ref[...] = jnp.zeros_like(ref) if first else inputs[n_dp + 2 + i][...]

    for which, weight_ref in ((0, gate_ref), (1, up_ref)):
        delta = jnp.concatenate([ref[which, 0] for ref in delta_refs], axis=0)
        back = dot(delta, weight_ref[:, 0].reshape(keep * size, size), ((1,), (1,)))
        for m in range(keep):
            r = rows_ref[which, slot, m]
            column = pl.multiple_of(lax.rem(r, per) * size, size)
            for i in range(n_dp):
                ref = totals[i // n_x]
                at = (i % n_x, lax.div(r, per), slice(None), pl.ds(column, size))
                ref[at] = ref[at] + back[i * tokens : (i + 1) * tokens, m * size : (m + 1) * size]


def weight_kernel(n_dp, keep, per, offset, rows_ref, *refs):
    cotangent_refs, delta_refs = refs[:n_dp], refs[n_dp : 2 * n_dp]
    turned_ref, grads = refs[2 * n_dp], refs[-3:]
    slot = offset + pl.program_id(0)
    size = delta_refs[0].shape[-1]

    def whole(which):
        return jnp.concatenate([ref[which, 0] for ref in delta_refs], axis=0)

    for which in range(2):
        left = jnp.concatenate([turned_ref[rows_ref[which, slot, m]] for m in range(keep)], axis=0)
        grad = dot(left, whole(which), ((1,), (0,))).astype(BF16)
        for m in range(keep):
            grads[which][m, 0] = grad[m * size : (m + 1) * size]

    hidden = whole(2).T
    parts = [picked(cotangent_refs, rows_ref, 2, slot, m, per, size) for m in range(keep)]
    grad = dot(hidden, jnp.concatenate(parts, axis=1), ((1,), (0,))).astype(BF16)
    for m in range(keep):
        grads[2][m, 0] = grad[:, m * size : (m + 1) * size]


def after(rows, value):
    return rows + (value[(0,) * value.ndim] * 0).astype(jnp.int32)


def constant(shape):
    return pl.BlockSpec(shape, lambda s, *_: (0,) * len(shape), pipeline_mode=pl.Buffered(1))


def body(
    activations,
    output_grad,
    gate_weight,
    up_weight,
    down_weight,
    gate_rows,
    up_rows,
    down_columns,
    owner_map,
):
    tokens, features = activations.shape
    keep, slots, size, _ = gate_weight.shape
    n_dp, n_blk = lax.axis_size("dp"), lax.axis_size("blk")
    n_x = n_dp // 2
    per = features // size
    row_blocks = per * n_blk
    chunks = CHUNKS if slots % CHUNKS == 0 else 1
    part = slots // chunks

    def other_core(value):
        return lax.ppermute(value, "dp", [(i, i ^ 1) for i in range(n_dp)])

    def from_x(value, step):
        return lax.ppermute(value, "dp", [((i + 2 * step) % n_dp, i) for i in range(n_dp)])

    def gather_dp(value):
        column = [value] + [from_x(value, k) for k in range(1, n_x)]
        return column + [other_core(v) for v in column]

    own = lax.axis_index("blk")
    owned = (owner_map == own).astype(jnp.int32)
    position = jnp.cumsum(owned) - 1
    slot_ids = jnp.arange(slots, dtype=jnp.int32)
    chosen = owned[None, :] * (position[None, :] == slot_ids[:, None]).astype(jnp.int32)
    live = jnp.sum(chosen, axis=1)
    listing = jnp.stack([gate_rows, up_rows, down_columns])
    listing = lax.dynamic_slice_in_dim(listing, lax.axis_index("dp") * keep, keep, axis=2)
    rows = jnp.sum(chosen[None, :, :, None] * listing[:, None, :, :], axis=2)

    inputs = gather_dp(lax.all_gather(activations, "blk", axis=0))
    cotangents = gather_dp(lax.all_gather(output_grad, "blk", axis=0))
    token_shape = (n_blk, tokens, features)
    params = pltpu.CompilerParams(vmem_limit_bytes=VMEM_LIMIT)

    def weight_spec(offset):
        return pl.BlockSpec((keep, 1, size, size), lambda s, *_: (0, offset + s, 0, 0))

    per_slot = pl.BlockSpec((3, 1, tokens, size), lambda s, *_: (0, s, 0, 0))
    per_column = pl.BlockSpec((n_x, 3, 1, tokens, size), lambda s, *_: (0, 0, s, 0, 0))
    column_shape = (n_x, 3, part, tokens, size)
    delta_shape = jax.ShapeDtypeStruct((3, part, tokens, size), BF16)

    halves, sends = [], []
    for c in range(chunks):
        order = after(rows, sends[c - 2]) if c >= 2 else rows
        mine, theirs = pl.pallas_call(
            functools.partial(forward_kernel, n_dp, keep, per, c * part),
            grid_spec=pltpu.PrefetchScalarGridSpec(
                num_scalar_prefetch=2,
                grid=(part,),
                in_specs=[constant(token_shape)] * (2 * n_dp) + [weight_spec(c * part)] * 3,
                out_specs=[per_column] * 2,
            ),
            out_shape=[jax.ShapeDtypeStruct(column_shape, F32), jax.ShapeDtypeStruct(column_shape, BF16)],
            compiler_params=params,
            name="forward",
        )(order, live, *inputs, *cotangents, gate_weight, up_weight, down_weight)
        got = other_core(theirs)
        send = (mine[1:] + got[1:].astype(F32)).astype(BF16)
        sends.append(send)
        halves.append((mine, got, [from_x(send[k - 1], n_x - k) for k in range(1, n_x)]))

    turned = pl.pallas_call(
        turn_kernel,
        grid=(row_blocks,),
        in_specs=[pl.BlockSpec((1, tokens, size), lambda r: (r // per, 0, r % per))] * n_dp,
        out_specs=pl.BlockSpec((1, size, n_dp * tokens), lambda r: (r, 0, 0)),
        out_shape=jax.ShapeDtypeStruct((row_blocks, size, n_dp * tokens), BF16),
        name="turn",
    )(*inputs)

    deltas = []
    for mine, got, arrived in halves:
        delta = pl.pallas_call(
            delta_kernel,
            grid=(part,),
            in_specs=[pl.BlockSpec((1, 3, 1, tokens, size), lambda s: (0, 0, s, 0, 0))] * 2 + [per_slot] * (n_x - 1),
            out_specs=per_slot,
            out_shape=delta_shape,
            name="delta",
        )(mine, got, *arrived)
        deltas.append(gather_dp(delta))

    total_shape = (n_x, n_blk, tokens, features)
    totals = ()
    for c in range(chunks):
        first = c == 0
        held = [constant(total_shape)] * len(totals)
        totals = pl.pallas_call(
            functools.partial(input_kernel, n_dp, keep, per, c * part, first),
            grid_spec=pltpu.PrefetchScalarGridSpec(
                num_scalar_prefetch=1,
                grid=(part,),
                in_specs=[per_slot] * n_dp + [weight_spec(c * part)] * 2 + held,
                out_specs=[constant(total_shape)] * 2,
            ),
            out_shape=[jax.ShapeDtypeStruct(total_shape, F32)] * 2,
            input_output_aliases={} if first else {n_dp + 3 + i: i for i in range(2)},
            compiler_params=params,
            name="input",
        )(rows, *deltas[c], gate_weight, up_weight, *totals)

    mine, theirs = totals[0], totals[1].astype(BF16)
    got = other_core(theirs)
    send = (mine[1:] + got[1:].astype(F32)).astype(BF16)
    summed = mine[0] + got[0].astype(F32)
    for k in range(1, n_x):
        summed = summed + from_x(send[k - 1], n_x - k).astype(F32)
    rounded = summed.astype(BF16)

    def for_blk(array, step):
        return lax.dynamic_index_in_dim(array, lax.rem(own + step, n_blk), 0, keepdims=False)

    pieces = [
        lax.ppermute(for_blk(rounded, k), "blk", [(i, (i + k) % n_blk) for i in range(n_blk)])
        for k in range(1, n_blk)
    ]
    input_grad = for_blk(summed, 0)
    for piece in pieces:
        input_grad = input_grad + piece.astype(F32)

    grads = ()
    grad_shape = jax.ShapeDtypeStruct(gate_weight.shape, BF16)
    for c in range(chunks):
        order = rows
        if c == chunks - 1:
            order = after(rows, rounded)
        elif c > 0:
            order = after(rows, send if c >= 2 else theirs)
        held = [pl.BlockSpec(memory_space=pl.ANY)] * len(grads)
        grads = pl.pallas_call(
            functools.partial(weight_kernel, n_dp, keep, per, c * part),
            grid_spec=pltpu.PrefetchScalarGridSpec(
                num_scalar_prefetch=1,
                grid=(part,),
                in_specs=[constant(token_shape)] * n_dp
                + [per_slot] * n_dp
                + [constant((row_blocks, size, n_dp * tokens))]
                + held,
                out_specs=[weight_spec(c * part)] * 3,
            ),
            out_shape=[grad_shape] * 3,
            input_output_aliases={2 * n_dp + 2 + i: i for i in range(len(grads))},
            compiler_params=params,
            name="weight",
        )(order, *cotangents, *deltas[c], turned, *grads)
    return input_grad.astype(BF16), *grads


def solution(mesh):
    in_specs = (
        P(("group", "dp"), "blk"),
        P(("group", "dp"), "blk"),
        P("dp", "blk", None, None),
        P("dp", "blk", None, None),
        P("dp", "blk", None, None),
        P(),
        P(),
        P(),
        P(),
    )
    out_specs = (
        P(("group", "dp"), "blk"),
        P("dp", ("group", "blk"), None, None),
        P("dp", ("group", "blk"), None, None),
        P("dp", ("group", "blk"), None, None),
    )
    return jax.shard_map(body, mesh=mesh, in_specs=in_specs, out_specs=out_specs, check_vma=False)
```

time: 492 us -> 490 us (level)
  Pallas kernels: 137 us -> 202 us
  waiting for transfers between devices: 249 us -> 210 us
  local copies, waits for them, and re-layouts: 38.3 us -> 10.4 us
  other arithmetic: 34.5 us -> 21.2 us
  starting transfers between devices: 16.2 us -> 22.4 us
    pallas_call x4 -> x13, Pallas kernels: 86.2 us -> 153 us  [the longest x4 62.6 us: body(): pl.pallas_call(functools.partial(input_kernel, n_dp, keep, per, c * part,...]
    reduce_scatter x1 -> x0, waiting for transfers between devices: 42.2 us -> none  [body(): lax.psum_scatter(summed, 'blk', scatter_dimension=0, tiled=True)]
    transpose x1 -> x0, other arithmetic: 11 us -> none  [body(): turned.reshape(n_dp, n_blk, tokens, per, size).transpose(1, 3, 4, 0, 2)]
    add x10 -> x2, other arithmetic: 12 us -> 1.32 us  [after(): return rows + (value[(0,) * value.ndim] * 0).astype(jnp.int32)]
    slice x9 -> x5, local copies, waits for them, and re-layouts: 15.3 us -> 4.69 us  [after(): return rows + (value[(0,) * value.ndim] * 0).astype(jnp.int32)]
    all_gather x1 -> x2, waiting for transfers between devices: 49.7 us -> 59.1 us  [the longest x1 31.6 us: body(): cotangents = gather_dp(lax.all_gather(output_grad, 'blk', axis=0))]
    convert_element_type x5 -> x6, other arithmetic: 3.15 us -> 12.1 us  [the longest x3 4.61 us: body(): send = (mine[1:] + got[1:].astype(F32)).astype(BF16)]
    another operation x5 -> x1, local copies, waits for them, and re-layouts: 9.02 us -> 0.11 us  [the longest x4 8.91 us: body(): turned = jnp.stack([g[:, 0] for g in gathered])]
  transfers between devices with their start and end apart: 27 -> 33, of which waited for: 12 -> 12; matrix products, arithmetic and copies ran while one was open for 11% -> 3% of each run, Pallas kernels for 21% -> 33%
where the time goes in v2:
time: 490 us; the launch traced here: 483 us
  waiting for transfers between devices  210 us (43%)
  Pallas kernels  202 us (41%)
  starting transfers between devices  22.4 us (5%)
  other arithmetic  21.2 us (4%)
  between operations  17.6 us (4%)
  local copies, waits for them, and re-layouts  10.4 us (2%)
    ppermute x11, waiting for transfers between devices, from_x(): lax.ppermute(value, 'dp', [((i + 2 * step) % n_dp, i) for i in range(n_dp)])  145 us
    pallas_call x4, Pallas kernels, body(): pl.pallas_call(functools.partial(input_kernel, n_dp, keep, per, c * part,...  62.6 us
    pallas_call x4, Pallas kernels, body(): pl.pallas_call(functools.partial(weight_kernel, n_dp, keep, per, c * part...  49.5 us
    pallas_call x4, Pallas kernels, body(): pl.pallas_call(functools.partial(forward_kernel, n_dp, keep, per, c * par...  49.2 us
    all_gather x1, waiting for transfers between devices, body(): cotangents = gather_dp(lax.all_gather(output_grad, 'blk', axis=0))  31.6 us
    all_gather x1, waiting for transfers between devices, body(): inputs = gather_dp(lax.all_gather(activations, 'blk', axis=0))  27.6 us
    pallas_call x4, Pallas kernels, body(): pl.pallas_call(delta_kernel, grid=(part,), in_specs=[pl.BlockSpec((1, 3,...  23.5 us
    pallas_call x1, Pallas kernels, body(): pl.pallas_call(turn_kernel, grid=(row_blocks,), in_specs=[pl.BlockSpec((1...  17.5 us
  transfers between devices with their start and end apart: 33, of which 12 were waited for; matrix products, arithmetic and copies ran while one was open for 3% of the time, Pallas kernels for 33%

profile of v2, /device:TPU:0, one launch (start us, length us, event | category | flops | bytes accessed | tf_op | source)
XLA Modules:
  0.0 483.4 jit_solution(7768749697671790505)
XLA Ops:
  8.6 31.6 %all-gather.7.cloned.1.call-done = bf16[512,1024]{1,0:T(8,128)(2,1)} async-done(((bf16[128,1024]{1,0:T(8,128)(2,1)}), bf16[512,1024]{1,0:T(8,128)(2,1)}) %all-gather.7.cloned.1.call-update) | async-done | bytes 1048592 | tf_op jit(solution)/shard_map/all_gather | solution.py:175
  40.2 1.5 collective-permute-start.3
  41.7 27.6 %all-gather.5.cloned.1.call-done = bf16[512,1024]{1,0:T(8,128)(2,1)} async-done(((bf16[128,1024]{1,0:T(8,128)(2,1)}), bf16[512,1024]{1,0:T(8,128)(2,1)}) %all-gather.5.cloned.1.call-update) | async-done | bytes 1048592 | tf_op jit(solution)/shard_map/all_gather | solution.py:174
  69.3 1.5 collective-permute-start
  71.3 23.0 %collective-permute-done.refs_1_ = bf16[4,128,1024]{2,1,0:T(8,128)(2,1)} collective-permute-done((bf16[4,128,1024]{2,1,0:T(8,128)(2,1)}, bf16[4,128,1024]{2,1,0:T(8,128)(2,1)}, u32[]{:S(2)}, u32[]{:S(2)}) %collective-permute-start) | collective-permute-done | bytes 1048608 | tf_op jit(solution)/shard_map/ppermute | solution.py:158
  99.7 12.8 %forward.6 = (f32[2,3,8,128,128]{4,3,2,1,0:T(8,128)}, bf16[2,3,8,128,128]{4,3,2,1,0:T(8,128)(2,1)}) custom-call(s32[3,32,4]{2,1,0:T(8,128)} %copy.55.rows_ref, s32[32]{0:T(128)} %get-tuple-element.70.live_ref, bf16[4,128,1024]{2,1,0:T(8,128)(2,1)} %bitcast.53, bf16[4,128,1024]{2,1,0:T(8,128)(2,1)} %collective-permute-done.refs_1_, ...), custom_call_target="tpu_custom_call" | custom-call | tf_op jit(solution)/shard_map/forward/pallas_call | solution.py:190
  113.1 12.8 %forward.4 = (f32[2,3,8,128,128]{4,3,2,1,0:T(8,128)}, bf16[2,3,8,128,128]{4,3,2,1,0:T(8,128)(2,1)}) custom-call(s32[3,32,4]{2,1,0:T(8,128)} %copy.55.rows_ref, s32[32]{0:T(128)} %get-tuple-element.70.live_ref, bf16[4,128,1024]{2,1,0:T(8,128)(2,1)} %bitcast.54, bf16[4,128,1024]{2,1,0:T(8,128)(2,1)} %collective-permute-done.refs_1_, ...), custom_call_target="tpu_custom_call" | custom-call | tf_op jit(solution)/shard_map/forward/pallas_call | solution.py:190
  126.0 2.9 add_convert_fusion.2
  130.7 1.3 add_convert_fusion.4
  134.8 12.8 %forward.7 = (f32[2,3,8,128,128]{4,3,2,1,0:T(8,128)}, bf16[2,3,8,128,128]{4,3,2,1,0:T(8,128)(2,1)}) custom-call(s32[3,32,4]{2,1,0:T(8,128)} %get-tuple-element.68.rows_ref, s32[32]{0:T(128)} %get-tuple-element.70.live_ref, bf16[4,128,1024]{2,1,0:T(8,128)(2,1)} %bitcast.55, bf16[4,128,1024]{2,1,0:T(8,128)(2,1)} %collective-permute-done.refs_1_, ...), custom_call_target="tpu_custom_call" | custom-call | tf_op jit(solution)/shard_map/forward/pallas_call | solution.py:190
  148.2 10.8 %forward.5 = (f32[2,3,8,128,128]{4,3,2,1,0:T(8,128)}, bf16[2,3,8,128,128]{4,3,2,1,0:T(8,128)(2,1)}) custom-call(s32[3,32,4]{2,1,0:T(8,128)} %get-tuple-element.69.rows_ref, s32[32]{0:T(128)} %get-tuple-element.70.live_ref, bf16[4,128,1024]{2,1,0:T(8,128)(2,1)} %bitcast.56, bf16[4,128,1024]{2,1,0:T(8,128)(2,1)} %collective-permute-done.refs_1_, ...), custom_call_target="tpu_custom_call" | custom-call | tf_op jit(solution)/shard_map/forward/pallas_call | solution.py:190
  159.0 1.5 collective-permute-start.22
  161.1 18.6 %collective-permute-done.22.refs_0_ = bf16[3,8,128,128]{3,2,1,0:T(8,128)(2,1)} collective-permute-done((bf16[3,8,128,128]{3,2,1,0:T(8,128)(2,1)}, bf16[3,8,128,128]{3,2,1,0:T(8,128)(2,1)}, u32[]{:S(2)}, u32[]{:S(2)}) %collective-permute-start.22) | collective-permute-done | bytes 786464 | tf_op jit(solution)/shard_map/ppermute | solution.py:158
  179.7 5.9 %delta.7.refs_0_.refs_4_ = bf16[3,8,128,128]{3,2,1,0:T(8,128)(2,1)} custom-call(f32[2,3,8,128,128]{4,3,2,1,0:T(8,128)} %get-tuple-element.36.mine_ref, bf16[2,3,8,128,128]{4,3,2,1,0:T(8,128)(2,1)} %collective-permute-done.12.got_ref, bf16[3,8,128,128]{3,2,1,0:T(8,128)(2,1)} %collective-permute-done.22.refs_0_), custom_call_target="tpu_custom_call" | custom-call | tf_op jit(solution)/shard_map/delta/pallas_call | solution.py:218
  185.6 1.5 collective-permute-start.23
  187.1 2.3 fusion.1
  190.3 2.3 fusion
  192.5 1.2 collective-permute-start.8
  193.7 2.9 collective-permute-done.18.refs_0_
  196.6 5.9 %delta.6.refs_0_.refs_4_ = bf16[3,8,128,128]{3,2,1,0:T(8,128)(2,1)} custom-call(f32[2,3,8,128,128]{4,3,2,1,0:T(8,128)} %get-tuple-element.32.mine_ref, bf16[2,3,8,128,128]{4,3,2,1,0:T(8,128)(2,1)} %collective-permute-done.6.got_ref, bf16[3,8,128,128]{3,2,1,0:T(8,128)(2,1)} %collective-permute-done.18.refs_0_), custom_call_target="tpu_custom_call" | custom-call | tf_op jit(solution)/shard_map/delta/pallas_call | solution.py:218
  202.5 1.5 collective-permute-start.19
  203.9 26.3 %collective-permute-done.14.refs_0_ = bf16[3,8,128,128]{3,2,1,0:T(8,128)(2,1)S(1)} collective-permute-done((bf16[3,8,128,128]{3,2,1,0:T(8,128)(2,1)}, bf16[3,8,128,128]{3,2,1,0:T(8,128)(2,1)S(1)}, u32[]{:S(2)}, u32[]{:S(2)}) %collective-permute-start.14) | collective-permute-done | bytes 786464 | tf_op jit(solution)/shard_map/ppermute | solution.py:158
  231.1 5.9 %delta.5.refs_0_.refs_4_ = bf16[3,8,128,128]{3,2,1,0:T(8,128)(2,1)} custom-call(f32[2,3,8,128,128]{4,3,2,1,0:T(8,128)} %get-tuple-element.38.mine_ref, bf16[2,3,8,128,128]{4,3,2,1,0:T(8,128)(2,1)} %collective-permute-done.13.got_ref, bf16[3,8,128,128]{3,2,1,0:T(8,128)(2,1)} %copy-done.17), custom_call_target="tpu_custom_call" | custom-call | tf_op jit(solution)/shard_map/delta/pallas_call | solution.py:218
  236.9 1.5 collective-permute-start.15
  238.5 8.7 %collective-permute-done.8.refs_0_ = bf16[3,8,128,128]{3,2,1,0:T(8,128)(2,1)} collective-permute-done((bf16[3,8,128,128]{3,2,1,0:T(8,128)(2,1)}, bf16[3,8,128,128]{3,2,1,0:T(8,128)(2,1)}, u32[]{:S(2)}, u32[]{:S(2)}) %collective-permute-start.8) | collective-permute-done | bytes 786464 | tf_op jit(solution)/shard_map/ppermute | solution.py:158
  247.1 5.9 %delta.4.refs_0_.refs_4_ = bf16[3,8,128,128]{3,2,1,0:T(8,128)(2,1)} custom-call(f32[2,3,8,128,128]{4,3,2,1,0:T(8,128)} %get-tuple-element.34.mine_ref, bf16[2,3,8,128,128]{4,3,2,1,0:T(8,128)(2,1)} %collective-permute-done.7.got_ref, bf16[3,8,128,128]{3,2,1,0:T(8,128)(2,1)} %collective-permute-done.8.refs_0_), custom_call_target="tpu_custom_call" | custom-call | tf_op jit(solution)/shard_map/delta/pallas_call | solution.py:218
  253.0 1.5 collective-permute-start.9
  254.5 9.4 %collective-permute-done.19.refs_1_.refs_5_ = bf16[3,8,128,128]{3,2,1,0:T(8,128)(2,1)S(1)} collective-permute-done((bf16[3,8,128,128]{3,2,1,0:T(8,128)(2,1)}, bf16[3,8,128,128]{3,2,1,0:T(8,128)(2,1)S(1)}, u32[]{:S(2)}, u32[]{:S(2)}) %collective-permute-start.19) | collective-permute-done | bytes 786464 | tf_op jit(solution)/shard_map/ppermute | solution.py:158
  264.4 16.3 %collective-permute-done.15.refs_1_.refs_5_ = bf16[3,8,128,128]{3,2,1,0:T(8,128)(2,1)S(1)} collective-permute-done((bf16[3,8,128,128]{3,2,1,0:T(8,128)(2,1)}, bf16[3,8,128,128]{3,2,1,0:T(8,128)(2,1)S(1)}, u32[]{:S(2)}, u32[]{:S(2)}) %collective-permute-start.15) | collective-permute-done | bytes 786464 | tf_op jit(solution)/shard_map/ppermute | solution.py:158
  281.3 15.9 %collective-permute-done.9.refs_1_.refs_5_ = bf16[3,8,128,128]{3,2,1,0:T(8,128)(2,1)S(1)} collective-permute-done((bf16[3,8,128,128]{3,2,1,0:T(8,128)(2,1)}, bf16[3,8,128,128]{3,2,1,0:T(8,128)(2,1)S(1)}, u32[]{:S(2)}, u32[]{:S(2)}) %collective-permute-start.9) | collective-permute-done | bytes 786464 | tf_op jit(solution)/shard_map/ppermute | solution.py:158
  297.1 13.6 %input.4 = (f32[2,4,128,1024]{3,2,1,0:T(8,128)}, f32[2,4,128,1024]{3,2,1,0:T(8,128)}) custom-call(s32[3,32,4]{2,1,0:T(8,128)} %copy.55.rows_ref, bf16[3,8,128,128]{3,2,1,0:T(8,128)(2,1)} %delta.7.refs_0_.refs_4_, bf16[3,8,128,128]{3,2,1,0:T(8,128)(2,1)} %collective-permute-done.23.refs_1_.refs_5_, ...), custom_call_target="tpu_custom_call" | custom-call | tf_op jit(solution)/shard_map/input/pallas_call | solution.py:233
  310.7 16.2 %input.5 = (f32[2,4,128,1024]{3,2,1,0:T(8,128)}, f32[2,4,128,1024]{3,2,1,0:T(8,128)}) custom-call(s32[3,32,4]{2,1,0:T(8,128)} %copy.55.rows_ref, bf16[3,8,128,128]{3,2,1,0:T(8,128)(2,1)} %delta.6.refs_0_.refs_4_, bf16[3,8,128,128]{3,2,1,0:T(8,128)(2,1)} %copy-done.11, ...), custom_call_target="tpu_custom_call", output_to_operand_aliasing={{0}: (7, {}), {1}: (8, {})} | custom-call | tf_op jit(solution)/shard_map/input/pallas_call | solution.py:233
  327.0 16.2 %input.6 = (f32[2,4,128,1024]{3,2,1,0:T(8,128)}, f32[2,4,128,1024]{3,2,1,0:T(8,128)}) custom-call(s32[3,32,4]{2,1,0:T(8,128)} %copy.55.rows_ref, bf16[3,8,128,128]{3,2,1,0:T(8,128)(2,1)} %delta.5.refs_0_.refs_4_, bf16[3,8,128,128]{3,2,1,0:T(8,128)(2,1)} %copy-done.12, ...), custom_call_target="tpu_custom_call", output_to_operand_aliasing={{0}: (7, {}), {1}: (8, {})} | custom-call | tf_op jit(solution)/shard_map/input/pallas_call | solution.py:233
  343.2 16.6 %input.7 = (f32[2,4,128,1024]{3,2,1,0:T(8,128)}, f32[2,4,128,1024]{3,2,1,0:T(8,128)}) custom-call(s32[3,32,4]{2,1,0:T(8,128)} %copy.55.rows_ref, bf16[3,8,128,128]{3,2,1,0:T(8,128)(2,1)} %delta.4.refs_0_.refs_4_, bf16[3,8,128,128]{3,2,1,0:T(8,128)(2,1)} %copy-done.13, ...), custom_call_target="tpu_custom_call", output_to_operand_aliasing={{0}: (7, {}), {1}: (8, {})} | custom-call | tf_op jit(solution)/shard_map/input/pallas_call | solution.py:233
  359.8 2.7 convert_element_type.102
  363.0 3.8 collective-permute-done.26
  368.2 1.5 collective-permute-start.27
  369.6 24.1 %collective-permute-done.27 = bf16[4,128,1024]{2,1,0:T(8,128)(2,1)} collective-permute-done((bf16[4,128,1024]{2,1,0:T(8,128)(2,1)S(1)}, bf16[4,128,1024]{2,1,0:T(8,128)(2,1)}, u32[]{:S(2)}, u32[]{:S(2)}) %collective-permute-start.27) | collective-permute-done | bytes 1048608 | tf_op jit(solution)/shard_map/ppermute | solution.py:158
  393.7 2.9 fusion.9
  397.4 3.1 collective-permute-start.28
  401.9 17.5 %turn.1.refs_8_ = bf16[32,128,512]{2,1,0:T(8,128)(2,1)} custom-call(bf16[4,128,1024]{2,1,0:T(8,128)(2,1)} %bitcast.57, bf16[4,128,1024]{2,1,0:T(8,128)(2,1)} %collective-permute-done.refs_1_, bf16[4,128,1024]{2,1,0:T(8,128)(2,1)} %collective-permute-done.1.refs_2_, bf16[4,128,1024]{2,1,0:T(8,128)(2,1)} %collective-permute-done.2.refs_3_), custom_call_target="tpu_custom_call" | custom-call | tf_op jit(solution)/shard_map/turn/pallas_call | solution.py:207
  419.5 12.5 %weight.4 = (bf16[4,32,128,128]{3,2,1,0:T(8,128)(2,1)}, bf16[4,32,128,128]{3,2,1,0:T(8,128)(2,1)}, bf16[4,32,128,128]{3,2,1,0:T(8,128)(2,1)}) custom-call(s32[3,32,4]{2,1,0:T(8,128)} %copy.55.rows_ref, bf16[4,128,1024]{2,1,0:T(8,128)(2,1)} %bitcast.47, bf16[4,128,1024]{2,1,0:T(8,128)(2,1)} %copy-done.1, bf16[4,128,1024]{2,1,0:T(8,128)(2,1)} %copy-done.2, ...), custom_call_target="tpu_custom_call" | custom-call | tf_op jit(solution)/shard_map/weight/pallas_call | solution.py:275
  431.9 1.2 slice.78
  433.8 1.2 slice.77
  437.6 12.4 %weight.5 = (bf16[4,32,128,128]{3,2,1,0:T(8,128)(2,1)}, bf16[4,32,128,128]{3,2,1,0:T(8,128)(2,1)}, bf16[4,32,128,128]{3,2,1,0:T(8,128)(2,1)}) custom-call(s32[3,32,4]{2,1,0:T(8,128)} %get-tuple-element.65.rows_ref, bf16[4,128,1024]{2,1,0:T(8,128)(2,1)} %bitcast.48, ...), custom_call_target="tpu_custom_call", output_to_operand_aliasing={{0}: (10, {}), {1}: (11, {}), {2}: (12, {})} | custom-call | tf_op jit(solution)/shard_map/weight/pallas_call | solution.py:275
  449.9 12.4 %weight.6 = (bf16[4,32,128,128]{3,2,1,0:T(8,128)(2,1)}, bf16[4,32,128,128]{3,2,1,0:T(8,128)(2,1)}, bf16[4,32,128,128]{3,2,1,0:T(8,128)(2,1)}) custom-call(s32[3,32,4]{2,1,0:T(8,128)} %get-tuple-element.66.rows_ref, bf16[4,128,1024]{2,1,0:T(8,128)(2,1)} %bitcast.49, ...), custom_call_target="tpu_custom_call", output_to_operand_aliasing={{0}: (10, {}), {1}: (11, {}), {2}: (12, {})} | custom-call | tf_op jit(solution)/shard_map/weight/pallas_call | solution.py:275
  462.3 12.3 %weight.7 = (bf16[4,32,128,128]{3,2,1,0:T(8,128)(2,1)}, bf16[4,32,128,128]{3,2,1,0:T(8,128)(2,1)}, bf16[4,32,128,128]{3,2,1,0:T(8,128)(2,1)}) custom-call(s32[3,32,4]{2,1,0:T(8,128)} %get-tuple-element.67.rows_ref, bf16[4,128,1024]{2,1,0:T(8,128)(2,1)} %bitcast.50, ...), custom_call_target="tpu_custom_call", output_to_operand_aliasing={{0}: (10, {}), {1}: (11, {}), {2}: (12, {})} | custom-call | tf_op jit(solution)/shard_map/weight/pallas_call | solution.py:275
  474.6 2.0 fusion.4
  (100 shorter events, 20.7 us)
Async XLA Ops:
  7.2 33.1 %all-gather.7.cloned.1.call-start = ((), (), s32[]{:S(2)}) async-start(), calls=%async_computation.1 | async-start | bytes 1310720 | tf_op jit(solution)/shard_map/all_gather | solution.py:175
  7.9 61.4 %all-gather.5.cloned.1.call-start = ((), (), s32[]{:S(2)}) async-start(), calls=%async_computation | async-start | bytes 1310720 | tf_op jit(solution)/shard_map/all_gather | solution.py:174
  40.2 31.0 %collective-permute-start.3 = (bf16[4,128,1024]{2,1,0:T(8,128)(2,1)}, bf16[4,128,1024]{2,1,0:T(8,128)(2,1)S(1)}, u32[]{:S(2)}, u32[]{:S(2)}) collective-permute-start(bf16[4,128,1024]{2,1,0:T(8,128)(2,1)} %bitcast.41), channel_id=1, source_target_pairs={{2,0},{3,1},{0,2},{1,3},{6,4},{7,5},{4,6},{5,7},{10,8},{11,9},{8,1... | collective-permute-start | bytes 3145736 | tf_op jit(solution)/shard_map/ppermute | solution.py:158
  69.3 25.1 %collective-permute-start = (bf16[4,128,1024]{2,1,0:T(8,128)(2,1)}, bf16[4,128,1024]{2,1,0:T(8,128)(2,1)}, u32[]{:S(2)}, u32[]{:S(2)}) collective-permute-start(bf16[4,128,1024]{2,1,0:T(8,128)(2,1)} %bitcast.51), channel_id=1, source_target_pairs={{2,0},{3,1},{0,2},{1,3},{6,4},{7,5},{4,6},{5,7},{10,8},{11,9},{8,1... | collective-permute-start | bytes 3145736 | tf_op jit(solution)/shard_map/ppermute | solution.py:158
  70.7 27.7 %collective-permute-start.4 = (bf16[4,128,1024]{2,1,0:T(8,128)(2,1)}, bf16[4,128,1024]{2,1,0:T(8,128)(2,1)S(1)}, u32[]{:S(2)}, u32[]{:S(2)}) collective-permute-start(bf16[4,128,1024]{2,1,0:T(8,128)(2,1)} %bitcast.42), channel_id=1, source_target_pairs={{0,1},{1,0},{2,3},{3,2},{4,5},{5,4},{6,7},{7,6},{8,9},{9,8},{10,11... | collective-permute-start | bytes 3145736 | tf_op jit(solution)/shard_map/ppermute | solution.py:155
  70.7 27.7 %collective-permute-start.1 = (bf16[4,128,1024]{2,1,0:T(8,128)(2,1)}, bf16[4,128,1024]{2,1,0:T(8,128)(2,1)}, u32[]{:S(2)}, u32[]{:S(2)}) collective-permute-start(bf16[4,128,1024]{2,1,0:T(8,128)(2,1)} %bitcast.52), channel_id=1, source_target_pairs={{0,1},{1,0},{2,3},{3,2},{4,5},{5,4},{6,7},{7,6},{8,9},{9,8},{10,11... | collective-permute-start | bytes 3145736 | tf_op jit(solution)/shard_map/ppermute | solution.py:155
  71.2 27.2 %copy-start.1 = (bf16[4,128,1024]{2,1,0:T(8,128)(2,1)}, bf16[4,128,1024]{2,1,0:T(8,128)(2,1)S(1)}, u32[]{:S(2)}) copy-start(bf16[4,128,1024]{2,1,0:T(8,128)(2,1)S(1)} %collective-permute-done.3.refs_5_.refs_1_) | copy-start | bytes 3145732
  71.2 27.2 %collective-permute-start.5 = (bf16[4,128,1024]{2,1,0:T(8,128)(2,1)S(1)}, bf16[4,128,1024]{2,1,0:T(8,128)(2,1)S(1)}, u32[]{:S(2)}, u32[]{:S(2)}) collective-permute-start(bf16[4,128,1024]{2,1,0:T(8,128)(2,1)S(1)} %collective-permute-done.3.refs_5_.refs_1_), channel_id=1, source_target_pairs={{0,1},{1,0},{2,3},{3,2},{4,5},{5,4},{6,7},{7,6},{8,9},{9,8},{10,11... | collective-permute-start | bytes 3145736 | tf_op jit(solution)/shard_map/ppermute | solution.py:155
  94.3 4.1 collective-permute-start.2
  112.5 13.5 %collective-permute-start.12 = (bf16[2,3,8,128,128]{4,3,2,1,0:T(8,128)(2,1)}, bf16[2,3,8,128,128]{4,3,2,1,0:T(8,128)(2,1)}, u32[]{:S(2)}, u32[]{:S(2)}) collective-permute-start(bf16[2,3,8,128,128]{4,3,2,1,0:T(8,128)(2,1)} %get-tuple-element.37), channel_id=1, source_target_pairs={{0,1},{1,0},{2,3},{3,2},{4,5},{5,4},{6,7},{7,6},{8,9},{9,8},{10,11... | collective-permute-start | bytes 4718600 | tf_op jit(solution)/shard_map/ppermute | solution.py:155
  125.9 4.8 %copy-start.6 = (f32[2,3,8,128,128]{4,3,2,1,0:T(8,128)S(1)}, f32[2,3,8,128,128]{4,3,2,1,0:T(8,128)}, u32[]{:S(2)}) copy-start(f32[2,3,8,128,128]{4,3,2,1,0:T(8,128)} %get-tuple-element.32.mine_ref) | copy-start | bytes 9437188
  125.9 4.8 collective-permute-start.6
  128.9 5.3 %copy-start.9 = (s32[3,32,4]{2,1,0:T(8,128)S(1)}, s32[3,32,4]{2,1,0:T(8,128)}, u32[]{:S(2)}) copy-start(s32[3,32,4]{2,1,0:T(8,128)} %copy.55.rows_ref) | copy-start | bytes 4612
  147.7 39.4 %collective-permute-start.13 = (bf16[2,3,8,128,128]{4,3,2,1,0:T(8,128)(2,1)}, bf16[2,3,8,128,128]{4,3,2,1,0:T(8,128)(2,1)}, u32[]{:S(2)}, u32[]{:S(2)}) collective-permute-start(bf16[2,3,8,128,128]{4,3,2,1,0:T(8,128)(2,1)} %get-tuple-element.39), channel_id=1, source_target_pairs={{0,1},{1,0},{2,3},{3,2},{4,5},{5,4},{6,7},{7,6},{8,9},{9,8},{10,11... | collective-permute-start | bytes 4718600 | tf_op jit(solution)/shard_map/ppermute | solution.py:155
  159.0 31.3 %collective-permute-start.7 = (bf16[2,3,8,128,128]{4,3,2,1,0:T(8,128)(2,1)}, bf16[2,3,8,128,128]{4,3,2,1,0:T(8,128)(2,1)}, u32[]{:S(2)}, u32[]{:S(2)}) collective-permute-start(bf16[2,3,8,128,128]{4,3,2,1,0:T(8,128)(2,1)} %get-tuple-element.35), channel_id=1, source_target_pairs={{0,1},{1,0},{2,3},{3,2},{4,5},{5,4},{6,7},{7,6},{8,9},{9,8},{10,11... | collective-permute-start | bytes 4718600 | tf_op jit(solution)/shard_map/ppermute | solution.py:155
  159.0 20.7 %collective-permute-start.22 = (bf16[3,8,128,128]{3,2,1,0:T(8,128)(2,1)}, bf16[3,8,128,128]{3,2,1,0:T(8,128)(2,1)}, u32[]{:S(2)}, u32[]{:S(2)}) collective-permute-start(bf16[3,8,128,128]{3,2,1,0:T(8,128)(2,1)} %bitcast.11), channel_id=1, source_target_pairs={{2,0},{3,1},{0,2},{1,3},{6,4},{7,5},{4,6},{5,7},{10,8},{11,9},{8,1... | collective-permute-start | bytes 2359304 | tf_op jit(solution)/shard_map/ppermute | solution.py:158
  160.5 26.5 %copy-start.8 = (f32[2,3,8,128,128]{4,3,2,1,0:T(8,128)S(1)}, f32[2,3,8,128,128]{4,3,2,1,0:T(8,128)}, u32[]{:S(2)}) copy-start(f32[2,3,8,128,128]{4,3,2,1,0:T(8,128)} %get-tuple-element.38.mine_ref) | copy-start | bytes 9437188
  160.5 36.1 %collective-permute-start.18 = (bf16[3,8,128,128]{3,2,1,0:T(8,128)(2,1)}, bf16[3,8,128,128]{3,2,1,0:T(8,128)(2,1)}, u32[]{:S(2)}, u32[]{:S(2)}) collective-permute-start(bf16[3,8,128,128]{3,2,1,0:T(8,128)(2,1)} %bitcast.59), channel_id=1, source_target_pairs={{2,0},{3,1},{0,2},{1,3},{6,4},{7,5},{4,6},{5,7},{10,8},{11,9},{8,1... | collective-permute-start | bytes 2359304 | tf_op jit(solution)/shard_map/ppermute | solution.py:158
  185.6 4.7 copy-start.7
  185.6 51.3 %collective-permute-start.23 = (bf16[3,8,128,128]{3,2,1,0:T(8,128)(2,1)}, bf16[3,8,128,128]{3,2,1,0:T(8,128)(2,1)}, u32[]{:S(2)}, u32[]{:S(2)}) collective-permute-start(bf16[3,8,128,128]{3,2,1,0:T(8,128)(2,1)} %delta.7.refs_0_.refs_4_), channel_id=1, source_target_pairs={{2,0},{3,1},{0,2},{1,3},{6,4},{7,5},{4,6},{5,7},{10,8},{11,9},{8,1... | collective-permute-start | bytes 2359304 | tf_op jit(solution)/shard_map/ppermute | solution.py:158
  189.4 4.3 copy-start.5
  189.4 40.8 %collective-permute-start.14 = (bf16[3,8,128,128]{3,2,1,0:T(8,128)(2,1)}, bf16[3,8,128,128]{3,2,1,0:T(8,128)(2,1)S(1)}, u32[]{:S(2)}, u32[]{:S(2)}) collective-permute-start(bf16[3,8,128,128]{3,2,1,0:T(8,128)(2,1)} %fusion.1), channel_id=1, source_target_pairs={{2,0},{3,1},{0,2},{1,3},{6,4},{7,5},{4,6},{5,7},{10,8},{11,9},{8,1... | collective-permute-start | bytes 2359304 | tf_op jit(solution)/shard_map/ppermute | solution.py:158
  192.5 54.6 %collective-permute-start.8 = (bf16[3,8,128,128]{3,2,1,0:T(8,128)(2,1)}, bf16[3,8,128,128]{3,2,1,0:T(8,128)(2,1)}, u32[]{:S(2)}, u32[]{:S(2)}) collective-permute-start(bf16[3,8,128,128]{3,2,1,0:T(8,128)(2,1)} %fusion), channel_id=1, source_target_pairs={{2,0},{3,1},{0,2},{1,3},{6,4},{7,5},{4,6},{5,7},{10,8},{11,9},{8,1... | collective-permute-start | bytes 2359304 | tf_op jit(solution)/shard_map/ppermute | solution.py:158
  193.7 59.3 %collective-permute-start.24 = (bf16[3,8,128,128]{3,2,1,0:T(8,128)(2,1)S(1)}, bf16[3,8,128,128]{3,2,1,0:T(8,128)(2,1)}, u32[]{:S(2)}, u32[]{:S(2)}) collective-permute-start(bf16[3,8,128,128]{3,2,1,0:T(8,128)(2,1)S(1)} %copy-done.5), channel_id=1, source_target_pairs={{0,1},{1,0},{2,3},{3,2},{4,5},{5,4},{6,7},{7,6},{8,9},{9,8},{10,11... | collective-permute-start | bytes 2359304 | tf_op jit(solution)/shard_map/ppermute | solution.py:155
  202.5 61.4 %collective-permute-start.19 = (bf16[3,8,128,128]{3,2,1,0:T(8,128)(2,1)}, bf16[3,8,128,128]{3,2,1,0:T(8,128)(2,1)S(1)}, u32[]{:S(2)}, u32[]{:S(2)}) collective-permute-start(bf16[3,8,128,128]{3,2,1,0:T(8,128)(2,1)} %delta.6.refs_0_.refs_4_), channel_id=1, source_target_pairs={{2,0},{3,1},{0,2},{1,3},{6,4},{7,5},{4,6},{5,7},{10,8},{11,9},{8,1... | collective-permute-start | bytes 2359304 | tf_op jit(solution)/shard_map/ppermute | solution.py:158
  230.2 33.7 %collective-permute-start.20 = (bf16[3,8,128,128]{3,2,1,0:T(8,128)(2,1)}, bf16[3,8,128,128]{3,2,1,0:T(8,128)(2,1)}, u32[]{:S(2)}, u32[]{:S(2)}) collective-permute-start(bf16[3,8,128,128]{3,2,1,0:T(8,128)(2,1)} %delta.6.refs_0_.refs_4_), channel_id=1, source_target_pairs={{0,1},{1,0},{2,3},{3,2},{4,5},{5,4},{6,7},{7,6},{8,9},{9,8},{10,11... | collective-permute-start | bytes 2359304 | tf_op jit(solution)/shard_map/ppermute | solution.py:155
  236.9 27.0 %copy-start.4 = (bf16[3,8,128,128]{3,2,1,0:T(8,128)(2,1)S(1)}, bf16[3,8,128,128]{3,2,1,0:T(8,128)(2,1)}, u32[]{:S(2)}) copy-start(bf16[3,8,128,128]{3,2,1,0:T(8,128)(2,1)} %delta.5.refs_0_.refs_4_) | copy-start | bytes 2359300
  236.9 43.8 %collective-permute-start.15 = (bf16[3,8,128,128]{3,2,1,0:T(8,128)(2,1)}, bf16[3,8,128,128]{3,2,1,0:T(8,128)(2,1)S(1)}, u32[]{:S(2)}, u32[]{:S(2)}) collective-permute-start(bf16[3,8,128,128]{3,2,1,0:T(8,128)(2,1)} %delta.5.refs_0_.refs_4_), channel_id=1, source_target_pairs={{2,0},{3,1},{0,2},{1,3},{6,4},{7,5},{4,6},{5,7},{10,8},{11,9},{8,1... | collective-permute-start | bytes 2359304 | tf_op jit(solution)/shard_map/ppermute | solution.py:158
  247.1 33.6 %collective-permute-start.25 = (bf16[3,8,128,128]{3,2,1,0:T(8,128)(2,1)}, bf16[3,8,128,128]{3,2,1,0:T(8,128)(2,1)}, u32[]{:S(2)}, u32[]{:S(2)}) collective-permute-start(bf16[3,8,128,128]{3,2,1,0:T(8,128)(2,1)} %collective-permute-done.23.refs_1_.refs_5_), channel_id=1, source_target_pairs={{0,1},{1,0},{2,3},{3,2},{4,5},{5,4},{6,7},{7,6},{8,9},{9,8},{10,11... | collective-permute-start | bytes 2359304 | tf_op jit(solution)/shard_map/ppermute | solution.py:155
  253.0 44.1 %collective-permute-start.9 = (bf16[3,8,128,128]{3,2,1,0:T(8,128)(2,1)}, bf16[3,8,128,128]{3,2,1,0:T(8,128)(2,1)S(1)}, u32[]{:S(2)}, u32[]{:S(2)}) collective-permute-start(bf16[3,8,128,128]{3,2,1,0:T(8,128)(2,1)} %delta.4.refs_0_.refs_4_), channel_id=1, source_target_pairs={{2,0},{3,1},{0,2},{1,3},{6,4},{7,5},{4,6},{5,7},{10,8},{11,9},{8,1... | collective-permute-start | bytes 2359304 | tf_op jit(solution)/shard_map/ppermute | solution.py:158
  263.9 46.8 %copy-start.11 = (bf16[3,8,128,128]{3,2,1,0:T(8,128)(2,1)}, bf16[3,8,128,128]{3,2,1,0:T(8,128)(2,1)S(1)}, u32[]{:S(2)}) copy-start(bf16[3,8,128,128]{3,2,1,0:T(8,128)(2,1)S(1)} %collective-permute-done.19.refs_1_.refs_5_) | copy-start | bytes 2359300
  263.9 46.8 %collective-permute-start.21 = (bf16[3,8,128,128]{3,2,1,0:T(8,128)(2,1)S(1)}, bf16[3,8,128,128]{3,2,1,0:T(8,128)(2,1)}, u32[]{:S(2)}, u32[]{:S(2)}) collective-permute-start(bf16[3,8,128,128]{3,2,1,0:T(8,128)(2,1)S(1)} %collective-permute-done.19.refs_1_.refs_5_), channel_id=1, source_target_pairs={{0,1},{1,0},{2,3},{3,2},{4,5},{5,4},{6,7},{7,6},{8,9},{9,8},{10,11... | collective-permute-start | bytes 2359304 | tf_op jit(solution)/shard_map/ppermute | solution.py:155
  263.9 63.0 %collective-permute-start.16 = (bf16[3,8,128,128]{3,2,1,0:T(8,128)(2,1)S(1)}, bf16[3,8,128,128]{3,2,1,0:T(8,128)(2,1)}, u32[]{:S(2)}, u32[]{:S(2)}) collective-permute-start(bf16[3,8,128,128]{3,2,1,0:T(8,128)(2,1)S(1)} %copy-done.4), channel_id=1, source_target_pairs={{0,1},{1,0},{2,3},{3,2},{4,5},{5,4},{6,7},{7,6},{8,9},{9,8},{10,11... | collective-permute-start | bytes 2359304 | tf_op jit(solution)/shard_map/ppermute | solution.py:155
  280.7 30.0 %copy-start.12 = (bf16[3,8,128,128]{3,2,1,0:T(8,128)(2,1)}, bf16[3,8,128,128]{3,2,1,0:T(8,128)(2,1)S(1)}, u32[]{:S(2)}) copy-start(bf16[3,8,128,128]{3,2,1,0:T(8,128)(2,1)S(1)} %collective-permute-done.15.refs_1_.refs_5_) | copy-start | bytes 2359300
  280.7 46.2 %collective-permute-start.17 = (bf16[3,8,128,128]{3,2,1,0:T(8,128)(2,1)S(1)}, bf16[3,8,128,128]{3,2,1,0:T(8,128)(2,1)}, u32[]{:S(2)}, u32[]{:S(2)}) collective-permute-start(bf16[3,8,128,128]{3,2,1,0:T(8,128)(2,1)S(1)} %collective-permute-done.15.refs_1_.refs_5_), channel_id=1, source_target_pairs={{0,1},{1,0},{2,3},{3,2},{4,5},{5,4},{6,7},{7,6},{8,9},{9,8},{10,11... | collective-permute-start | bytes 2359304 | tf_op jit(solution)/shard_map/ppermute | solution.py:155
  280.8 62.4 %collective-permute-start.10 = (bf16[3,8,128,128]{3,2,1,0:T(8,128)(2,1)}, bf16[3,8,128,128]{3,2,1,0:T(8,128)(2,1)}, u32[]{:S(2)}, u32[]{:S(2)}) collective-permute-start(bf16[3,8,128,128]{3,2,1,0:T(8,128)(2,1)} %delta.4.refs_0_.refs_4_), channel_id=1, source_target_pairs={{0,1},{1,0},{2,3},{3,2},{4,5},{5,4},{6,7},{7,6},{8,9},{9,8},{10,11... | collective-permute-start | bytes 2359304 | tf_op jit(solution)/shard_map/ppermute | solution.py:155
  297.1 13.6 %copy-start.13 = (bf16[3,8,128,128]{3,2,1,0:T(8,128)(2,1)}, bf16[3,8,128,128]{3,2,1,0:T(8,128)(2,1)S(1)}, u32[]{:S(2)}) copy-start(bf16[3,8,128,128]{3,2,1,0:T(8,128)(2,1)S(1)} %collective-permute-done.9.refs_1_.refs_5_) | copy-start | bytes 2359300
  297.1 46.1 %collective-permute-start.11 = (bf16[3,8,128,128]{3,2,1,0:T(8,128)(2,1)S(1)}, bf16[3,8,128,128]{3,2,1,0:T(8,128)(2,1)}, u32[]{:S(2)}, u32[]{:S(2)}) collective-permute-start(bf16[3,8,128,128]{3,2,1,0:T(8,128)(2,1)S(1)} %collective-permute-done.9.refs_1_.refs_5_), channel_id=1, source_target_pairs={{0,1},{1,0},{2,3},{3,2},{4,5},{5,4},{6,7},{7,6},{8,9},{9,8},{10,11... | collective-permute-start | bytes 2359304 | tf_op jit(solution)/shard_map/ppermute | solution.py:155
  359.8 7.0 %copy-start = (f32[2,4,128,1024]{3,2,1,0:T(8,128)S(1)}, f32[2,4,128,1024]{3,2,1,0:T(8,128)}, u32[]{:S(2)}) copy-start(f32[2,4,128,1024]{3,2,1,0:T(8,128)} %get-tuple-element.46) | copy-start | bytes 12582916
  362.5 4.8 copy-start.14
  362.5 4.4 collective-permute-start.26
  366.8 1.3 copy-start.15
  368.2 1.5 copy-start.16
  368.2 25.5 %collective-permute-start.27 = (bf16[4,128,1024]{2,1,0:T(8,128)(2,1)S(1)}, bf16[4,128,1024]{2,1,0:T(8,128)(2,1)}, u32[]{:S(2)}, u32[]{:S(2)}) collective-permute-start(bf16[4,128,1024]{2,1,0:T(8,128)(2,1)S(1)} %bitcast.58), channel_id=1, source_target_pairs={{2,0},{3,1},{0,2},{1,3},{6,4},{7,5},{4,6},{5,7},{10,8},{11,9},{8,1... | collective-permute-start | bytes 3145736 | tf_op jit(solution)/shard_map/ppermute | solution.py:158
  397.4 77.2 %collective-permute-start.28 = (bf16[128,1024]{1,0:T(8,128)(2,1)}, bf16[128,1024]{1,0:T(8,128)(2,1)}, u32[]{:S(2)}, u32[]{:S(2)}) collective-permute-start(bf16[128,1024]{1,0:T(8,128)(2,1)} %get-tuple-element.62), channel_id=1, source_target_pairs={{0,4},{4,8},{8,12},{12,0},{1,5},{5,9},{9,13},{13,1},{2,6},{6,10},{... | collective-permute-start | bytes 786440 | tf_op jit(solution)/shard_map/ppermute | solution.py:259
  400.5 74.1 %collective-permute-start.30 = (bf16[128,1024]{1,0:T(8,128)(2,1)}, bf16[128,1024]{1,0:T(8,128)(2,1)}, u32[]{:S(2)}, u32[]{:S(2)}) collective-permute-start(bf16[128,1024]{1,0:T(8,128)(2,1)} %get-tuple-element.63), channel_id=1, source_target_pairs={{0,12},{4,0},{8,4},{12,8},{1,13},{5,1},{9,5},{13,9},{2,14},{6,2},{... | collective-permute-start | bytes 786440 | tf_op jit(solution)/shard_map/ppermute | solution.py:259
  401.3 73.4 %collective-permute-start.29 = (bf16[128,1024]{1,0:T(8,128)(2,1)S(1)}, bf16[128,1024]{1,0:T(8,128)(2,1)}, u32[]{:S(2)}, u32[]{:S(2)}) collective-permute-start(bf16[128,1024]{1,0:T(8,128)(2,1)S(1)} %get-tuple-element.64), channel_id=1, source_target_pairs={{0,8},{4,12},{8,0},{12,4},{1,9},{5,13},{9,1},{13,5},{2,10},{6,14},... | collective-permute-start | bytes 786440 | tf_op jit(solution)/shard_map/ppermute | solution.py:259
  419.5 17.4 %copy-start.10 = (s32[3,32,4]{2,1,0:T(8,128)S(1)}, s32[3,32,4]{2,1,0:T(8,128)}, u32[]{:S(2)}) copy-start(s32[3,32,4]{2,1,0:T(8,128)} %copy.55.rows_ref) | copy-start | bytes 4612
  (4 other events, 4.1 us)
Sparse Core Ops, SparseCore 0:
  9.6 30.6 all-gather.6
  41.8 27.4 all-gather.4

commit v3 on v2

--- a/solution.py
+++ b/solution.py
@@ -11,6 +11,7 @@
 F32 = jnp.float32
 CHUNKS = 4
 VMEM_LIMIT = 60 * 1024 * 1024
+LITTLE = pl.CostEstimate(flops=1, bytes_accessed=1, transcendentals=0)
 
 
 def dot(a, b, dims):
@@ -123,8 +124,10 @@
         grads[2][m, 0] = grad[:, m * size : (m + 1) * size]
 
 
-def after(rows, value):
-    return rows + (value[(0,) * value.ndim] * 0).astype(jnp.int32)
+def after(array, *values):
+    for value in values:
+        array = array + (value[(0,) * value.ndim] * 0).astype(array.dtype)
+    return array
 
 
 def constant(shape):
@@ -184,9 +187,17 @@
     column_shape = (n_x, 3, part, tokens, size)
     delta_shape = jax.ShapeDtypeStruct((3, part, tokens, size), BF16)
 
-    halves, sends = [], []
-    for c in range(chunks):
-        order = after(rows, sends[c - 2]) if c >= 2 else rows
+    turned = pl.pallas_call(
+        turn_kernel,
+        grid=(row_blocks,),
+        in_specs=[pl.BlockSpec((1, tokens, size), lambda r: (r // per, 0, r % per))] * n_dp,
+        out_specs=pl.BlockSpec((1, size, n_dp * tokens), lambda r: (r, 0, 0)),
+        out_shape=jax.ShapeDtypeStruct((row_blocks, size, n_dp * tokens), BF16),
+        cost_estimate=LITTLE,
+        name="turn",
+    )(*inputs)
+
+    def forward(c, order):
         mine, theirs = pl.pallas_call(
             functools.partial(forward_kernel, n_dp, keep, per, c * part),
             grid_spec=pltpu.PrefetchScalarGridSpec(
@@ -197,38 +208,74 @@
             ),
             out_shape=[jax.ShapeDtypeStruct(column_shape, F32), jax.ShapeDtypeStruct(column_shape, BF16)],
             compiler_params=params,
+            cost_estimate=LITTLE,
             name="forward",
         )(order, live, *inputs, *cotangents, gate_weight, up_weight, down_weight)
-        got = other_core(theirs)
-        send = (mine[1:] + got[1:].astype(F32)).astype(BF16)
-        sends.append(send)
-        halves.append((mine, got, [from_x(send[k - 1], n_x - k) for k in range(1, n_x)]))
-
-    turned = pl.pallas_call(
-        turn_kernel,
-        grid=(row_blocks,),
-        in_specs=[pl.BlockSpec((1, tokens, size), lambda r: (r // per, 0, r % per))] * n_dp,
-        out_specs=pl.BlockSpec((1, size, n_dp * tokens), lambda r: (r, 0, 0)),
-        out_shape=jax.ShapeDtypeStruct((row_blocks, size, n_dp * tokens), BF16),
-        name="turn",
-    )(*inputs)
-
-    deltas = []
-    for mine, got, arrived in halves:
-        delta = pl.pallas_call(
+        return mine, other_core(theirs)
+
+    def to_delta(mine, got, arrived):
+        return pl.pallas_call(
             delta_kernel,
             grid=(part,),
             in_specs=[pl.BlockSpec((1, 3, 1, tokens, size), lambda s: (0, 0, s, 0, 0))] * 2 + [per_slot] * (n_x - 1),
             out_specs=per_slot,
             out_shape=delta_shape,
+            cost_estimate=LITTLE,
             name="delta",
         )(mine, got, *arrived)
-        deltas.append(gather_dp(delta))
+
+    sends, own_deltas, columns = [], [], []
+    for c in range(chunks):
+        if c == 0:
+            order = after(rows, turned)
+        elif c == 1:
+            order = rows
+        elif c == 2:
+            order = after(rows, sends[0])
+        else:
+            order = after(rows, own_deltas[c - 3])
+        mine, got = forward(c, order)
+        send = mine[1:] + got[1:].astype(F32)
+        if c >= 2:
+            send = after(send, own_deltas[c - 2])
+        send = send.astype(BF16)
+        sends.append(send)
+        delta = to_delta(mine, got, [from_x(send[k - 1], n_x - k) for k in range(1, n_x)])
+        own_deltas.append(delta)
+        columns.append([from_x(delta, k) for k in range(1, n_x)])
+
+    grad_shape = jax.ShapeDtypeStruct(gate_weight.shape, BF16)
+
+    def weights(c, order, grads):
+        return pl.pallas_call(
+            functools.partial(weight_kernel, n_dp, keep, per, c * part),
+            grid_spec=pltpu.PrefetchScalarGridSpec(
+                num_scalar_prefetch=1,
+                grid=(part,),
+                in_specs=[constant(token_shape)] * n_dp
+                + [per_slot] * n_dp
+                + [constant((row_blocks, size, n_dp * tokens))]
+                + [pl.BlockSpec(memory_space=pl.ANY)] * len(grads),
+                out_specs=[weight_spec(c * part)] * 3,
+            ),
+            out_shape=[grad_shape] * 3,
+            input_output_aliases={2 * n_dp + 2 + i: i for i in range(len(grads))},
+            compiler_params=params,
+            cost_estimate=LITTLE,
+            name="weight",
+        )(order, *cotangents, *deltas[c], turned, *grads)
 
     total_shape = (n_x, n_blk, tokens, features)
-    totals = ()
+    totals, grads, deltas = (), (), []
     for c in range(chunks):
         first = c == 0
+        column = columns[c]
+        if not first:
+            ready = [totals[0]] + ([own_deltas[c + 1]] if c + 1 < chunks else [])
+            column = [after(v, *ready) for v in column]
+        column = [own_deltas[c]] + columns[c], [other_core(own_deltas[c])] + [other_core(v) for v in column]
+        deltas.append(column[0] + column[1])
+        order = after(rows, grads[0]) if c == 1 else rows
         held = [constant(total_shape)] * len(totals)
         totals = pl.pallas_call(
             functools.partial(input_kernel, n_dp, keep, per, c * part, first),
@@ -241,8 +288,11 @@
             out_shape=[jax.ShapeDtypeStruct(total_shape, F32)] * 2,
             input_output_aliases={} if first else {n_dp + 3 + i: i for i in range(2)},
             compiler_params=params,
+            cost_estimate=LITTLE,
             name="input",
-        )(rows, *deltas[c], gate_weight, up_weight, *totals)
+        )(order, *deltas[c], gate_weight, up_weight, *totals)
+        if first:
+            grads = weights(0, rows, grads)
 
     mine, theirs = totals[0], totals[1].astype(BF16)
     got = other_core(theirs)
@@ -250,7 +300,12 @@
     summed = mine[0] + got[0].astype(F32)
     for k in range(1, n_x):
         summed = summed + from_x(send[k - 1], n_x - k).astype(F32)
+    for c in range(1, chunks - 1):
+        grads = weights(c, after(rows, send), grads)
+    summed = after(summed, grads[0])
     rounded = summed.astype(BF16)
+    if chunks > 1:
+        grads = weights(chunks - 1, after(rows, rounded), grads)
 
     def for_blk(array, step):
         return lax.dynamic_index_in_dim(array, lax.rem(own + step, n_blk), 0, keepdims=False)
@@ -263,31 +318,6 @@
     for piece in pieces:
         input_grad = input_grad + piece.astype(F32)
 
-    grads = ()
-    grad_shape = jax.ShapeDtypeStruct(gate_weight.shape, BF16)
-    for c in range(chunks):
-        order = rows
-        if c == chunks - 1:
-            order = after(rows, rounded)
-        elif c > 0:
-            order = after(rows, send if c >= 2 else theirs)
-        held = [pl.BlockSpec(memory_space=pl.ANY)] * len(grads)
-        grads = pl.pallas_call(
-            functools.partial(weight_kernel, n_dp, keep, per, c * part),
-            grid_spec=pltpu.PrefetchScalarGridSpec(
-                num_scalar_prefetch=1,
-                grid=(part,),
-                in_specs=[constant(token_shape)] * n_dp
-                + [per_slot] * n_dp
-                + [constant((row_blocks, size, n_dp * tokens))]
-                + held,
-                out_specs=[weight_spec(c * part)] * 3,
-            ),
-            out_shape=[grad_shape] * 3,
-            input_output_aliases={2 * n_dp + 2 + i: i for i in range(len(grads))},
-            compiler_params=params,
-            name="weight",
-        )(order, *cotangents, *deltas[c], turned, *grads)
     return input_grad.astype(BF16), *grads
 
 

time: 490 us -> 464 us (0.947)
  waiting for transfers between devices: 210 us -> 160 us
  local copies, waits for them, and re-layouts: 10.4 us -> 23.6 us
  between operations: 17.6 us -> 22.8 us
    ppermute x11, waiting for transfers between devices: 145 us -> 86.1 us  [from_x(): lax.ppermute(value, 'dp', [((i + 2 * step) % n_dp, i) for i in range(n_dp)])]
    slice x5 -> x13, local copies, waits for them, and re-layouts: 4.69 us -> 13.7 us  [after(): array = array + (value[(0,) * value.ndim] * 0).astype(array.dtype)]
    ppermute x17, waiting for transfers between devices: 3.83 us -> 10.2 us  [other_core(): return lax.ppermute(value, 'dp', [(i, i ^ 1) for i in range(n_dp)])]
  transfers between devices with their start and end apart: 33 -> 33, of which waited for: 12 -> 12; matrix products, arithmetic and copies ran while one was open for 3% -> 6% of each run, Pallas kernels for 33% -> 37%
where the time goes in v3:
time: 464 us; the launch traced here: 455 us
  Pallas kernels  204 us (44%)
  waiting for transfers between devices  160 us (34%)
  other arithmetic  23.9 us (5%)
  local copies, waits for them, and re-layouts  23.6 us (5%)
  between operations  22.8 us (5%)
  starting transfers between devices  21.5 us (5%)
    ppermute x11, waiting for transfers between devices, from_x(): lax.ppermute(value, 'dp', [((i + 2 * step) % n_dp, i) for i in range(n_dp)])  86.1 us
    pallas_call x4, Pallas kernels, body(): pl.pallas_call(functools.partial(input_kernel, n_dp, keep, per, c * part,...  62.1 us
    pallas_call x4, Pallas kernels, forward(): pl.pallas_call(functools.partial(forward_kernel, n_dp, keep, per, c * par...  51 us
    pallas_call x4, Pallas kernels, weights(): pl.pallas_call(functools.partial(weight_kernel, n_dp, keep, per, c * part...  49.4 us
    all_gather x1, waiting for transfers between devices, body(): inputs = gather_dp(lax.all_gather(activations, 'blk', axis=0))  31.6 us
    all_gather x1, waiting for transfers between devices, body(): cotangents = gather_dp(lax.all_gather(output_grad, 'blk', axis=0))  27.6 us
    pallas_call x4, Pallas kernels, to_delta(): pl.pallas_call(delta_kernel, grid=(part,), in_specs=[pl.BlockSpec((1, 3,...  23.5 us
    pallas_call x1, Pallas kernels, body(): pl.pallas_call(turn_kernel, grid=(row_blocks,), in_specs=[pl.BlockSpec((1...  17.5 us
  transfers between devices with their start and end apart: 33, of which 12 were waited for; matrix products, arithmetic and copies ran while one was open for 6% of the time, Pallas kernels for 37%

profile of v3, /device:TPU:0, one launch (start us, length us, event | category | flops | bytes accessed | tf_op | source)
XLA Modules:
  0.0 455.4 jit_solution(8294401347967533669)
XLA Ops:
  8.6 31.6 %all-gather.5.cloned.1.call-done = bf16[512,1024]{1,0:T(8,128)(2,1)} async-done(((bf16[128,1024]{1,0:T(8,128)(2,1)}), bf16[512,1024]{1,0:T(8,128)(2,1)}) %all-gather.5.cloned.1.call-update) | async-done | bytes 1048592 | tf_op jit(solution)/shard_map/all_gather | solution.py:177
  40.2 1.5 collective-permute-start
  41.7 27.6 %all-gather.7.cloned.1.call-done = bf16[512,1024]{1,0:T(8,128)(2,1)} async-done(((bf16[128,1024]{1,0:T(8,128)(2,1)}), bf16[512,1024]{1,0:T(8,128)(2,1)}) %all-gather.7.cloned.1.call-update) | async-done | bytes 1048592 | tf_op jit(solution)/shard_map/all_gather | solution.py:178
  69.3 1.5 collective-permute-start.3
  71.2 23.0 %collective-permute-done.3.refs_5_.refs_1_ = bf16[4,128,1024]{2,1,0:T(8,128)(2,1)S(1)} collective-permute-done((bf16[4,128,1024]{2,1,0:T(8,128)(2,1)}, bf16[4,128,1024]{2,1,0:T(8,128)(2,1)S(1)}, u32[]{:S(2)}, u32[]{:S(2)}) %collective-permute-start.3) | collective-permute-done | bytes 1048608 | tf_op jit(solution)/shard_map/ppermute | solution.py:161
  97.7 17.5 %turn.1.refs_8_ = bf16[32,128,512]{2,1,0:T(8,128)(2,1)} custom-call(bf16[4,128,1024]{2,1,0:T(8,128)(2,1)} %bitcast.69, bf16[4,128,1024]{2,1,0:T(8,128)(2,1)} %collective-permute-done.refs_1_, bf16[4,128,1024]{2,1,0:T(8,128)(2,1)} %collective-permute-done.1.refs_2_, bf16[4,128,1024]{2,1,0:T(8,128)(2,1)} %collective-permute-done.2.refs_3_), custom_call_target="tpu_custom_call" | custom-call | flops 1 | bytes 1 | tf_op jit(solution)/shard_map/turn/pallas_call | solution.py:190
  119.0 12.8 %forward.4 = (f32[2,3,8,128,128]{4,3,2,1,0:T(8,128)}, bf16[2,3,8,128,128]{4,3,2,1,0:T(8,128)(2,1)}) custom-call(s32[3,32,4]{2,1,0:T(8,128)} %broadcast_add_fusion.5.rows_ref, s32[32]{0:T(128)} %get-tuple-element.68.live_ref, bf16[4,128,1024]{2,1,0:T(8,128)(2,1)} %bitcast.70, bf16[4,128,1024]{2,1,0:T(8,128)(2,1)} %collective-permute-done.refs_1_, ...), custom_call_target="tpu_custom_call" | custom-call | flops 1 | bytes 1 | tf_op jit(solution)/shard_map/forward/pallas_call | solution.py:201
  132.3 3.2 collective-permute-done.6.got_ref
  135.6 2.2 add_convert_fusion.4
  137.8 1.5 collective-permute-start.7
  139.3 18.4 %collective-permute-done.7.refs_0_ = bf16[3,8,128,128]{3,2,1,0:T(8,128)(2,1)S(1)} collective-permute-done((bf16[3,8,128,128]{3,2,1,0:T(8,128)(2,1)S(1)}, bf16[3,8,128,128]{3,2,1,0:T(8,128)(2,1)S(1)}, u32[]{:S(2)}, u32[]{:S(2)}) %collective-permute-start.7) | collective-permute-done | bytes 786464 | tf_op jit(solution)/shard_map/ppermute | solution.py:161
  158.6 5.9 %delta.4.refs_4_.refs_0_ = bf16[3,8,128,128]{3,2,1,0:T(8,128)(2,1)} custom-call(f32[2,3,8,128,128]{4,3,2,1,0:T(8,128)} %get-tuple-element.32.mine_ref, bf16[2,3,8,128,128]{4,3,2,1,0:T(8,128)(2,1)} %copy-done.12, bf16[3,8,128,128]{3,2,1,0:T(8,128)(2,1)} %copy-done.23), custom_call_target="tpu_custom_call" | custom-call | flops 1 | bytes 1 | tf_op jit(solution)/shard_map/delta/pallas_call | solution.py:217
  164.4 1.5 collective-permute-start.18
  165.9 17.8 %collective-permute-done.18.refs_5_.refs_1_ = bf16[3,8,128,128]{3,2,1,0:T(8,128)(2,1)S(1)} collective-permute-done((bf16[3,8,128,128]{3,2,1,0:T(8,128)(2,1)}, bf16[3,8,128,128]{3,2,1,0:T(8,128)(2,1)S(1)}, u32[]{:S(2)}, u32[]{:S(2)}) %collective-permute-start.18) | collective-permute-done | bytes 786464 | tf_op jit(solution)/shard_map/ppermute | solution.py:161
  183.6 12.8 %forward.6 = (f32[2,3,8,128,128]{4,3,2,1,0:T(8,128)}, bf16[2,3,8,128,128]{4,3,2,1,0:T(8,128)(2,1)}) custom-call(s32[3,32,4]{2,1,0:T(8,128)} %copy-done.9, s32[32]{0:T(128)} %get-tuple-element.68.live_ref, bf16[4,128,1024]{2,1,0:T(8,128)(2,1)} %bitcast.71, bf16[4,128,1024]{2,1,0:T(8,128)(2,1)} %collective-permute-done.refs_1_, ...), custom_call_target="tpu_custom_call" | custom-call | flops 1 | bytes 1 | tf_op jit(solution)/shard_map/forward/pallas_call | solution.py:201
  201.8 12.3 %weight.4 = (bf16[4,32,128,128]{3,2,1,0:T(8,128)(2,1)}, bf16[4,32,128,128]{3,2,1,0:T(8,128)(2,1)}, bf16[4,32,128,128]{3,2,1,0:T(8,128)(2,1)}) custom-call(s32[3,32,4]{2,1,0:T(8,128)} %copy-done.9, bf16[4,128,1024]{2,1,0:T(8,128)(2,1)} %bitcast.61, bf16[4,128,1024]{2,1,0:T(8,128)(2,1)} %copy-done.1, bf16[4,128,1024]{2,1,0:T(8,128)(2,1)} %copy-done.2, ...), custom_call_target="tpu_custom_call" | custom-call | flops 1 | bytes 1 | tf_op jit(solution)/shard_map/weight/pallas_call | solution.py:250
  216.7 12.8 %forward.7 = (f32[2,3,8,128,128]{4,3,2,1,0:T(8,128)}, bf16[2,3,8,128,128]{4,3,2,1,0:T(8,128)(2,1)}) custom-call(s32[3,32,4]{2,1,0:T(8,128)} %get-tuple-element.66.rows_ref, s32[32]{0:T(128)} %get-tuple-element.68.live_ref, bf16[4,128,1024]{2,1,0:T(8,128)(2,1)} %bitcast.72, bf16[4,128,1024]{2,1,0:T(8,128)(2,1)} %collective-permute-done.refs_1_, ...), custom_call_target="tpu_custom_call" | custom-call | flops 1 | bytes 1 | tf_op jit(solution)/shard_map/forward/pallas_call | solution.py:201
  229.6 12.5 %forward.5 = (f32[2,3,8,128,128]{4,3,2,1,0:T(8,128)}, bf16[2,3,8,128,128]{4,3,2,1,0:T(8,128)(2,1)}) custom-call(s32[3,32,4]{2,1,0:T(8,128)} %get-tuple-element.67.rows_ref, s32[32]{0:T(128)} %get-tuple-element.68.live_ref, bf16[4,128,1024]{2,1,0:T(8,128)(2,1)} %bitcast.73, bf16[4,128,1024]{2,1,0:T(8,128)(2,1)} %collective-permute-done.refs_1_, ...), custom_call_target="tpu_custom_call" | custom-call | flops 1 | bytes 1 | tf_op jit(solution)/shard_map/forward/pallas_call | solution.py:201
  242.6 2.3 fusion.1
  244.9 1.4 collective-permute-start.10
  246.3 1.9 fusion.3
  248.8 16.7 %collective-permute-done.10.refs_0_ = bf16[3,8,128,128]{3,2,1,0:T(8,128)(2,1)S(1)} collective-permute-done((bf16[3,8,128,128]{3,2,1,0:T(8,128)(2,1)}, bf16[3,8,128,128]{3,2,1,0:T(8,128)(2,1)S(1)}, u32[]{:S(2)}, u32[]{:S(2)}) %collective-permute-start.10) | collective-permute-done | bytes 786464 | tf_op jit(solution)/shard_map/ppermute | solution.py:161
  266.4 5.9 %delta.5.refs_0_.refs_4_ = bf16[3,8,128,128]{3,2,1,0:T(8,128)(2,1)} custom-call(f32[2,3,8,128,128]{4,3,2,1,0:T(8,128)} %get-tuple-element.36.mine_ref, bf16[2,3,8,128,128]{4,3,2,1,0:T(8,128)(2,1)} %collective-permute-done.9.got_ref, bf16[3,8,128,128]{3,2,1,0:T(8,128)(2,1)} %copy-done.22), custom_call_target="tpu_custom_call" | custom-call | flops 1 | bytes 1 | tf_op jit(solution)/shard_map/delta/pallas_call | solution.py:217
  272.3 1.4 collective-permute-start.21
  273.7 1.3 slice.107
  275.6 13.5 %input.4 = (f32[2,4,128,1024]{3,2,1,0:T(8,128)}, f32[2,4,128,1024]{3,2,1,0:T(8,128)}) custom-call(s32[3,32,4]{2,1,0:T(8,128)} %copy-done.9, bf16[3,8,128,128]{3,2,1,0:T(8,128)(2,1)} %delta.4.refs_4_.refs_0_, bf16[3,8,128,128]{3,2,1,0:T(8,128)(2,1)} %copy-done.17, bf16[3,8,128,128]{3,2,1,0:T(8,128)(2,1)} %copy-done.18, bf16[3,8,128,128]{3,2,1,0:T(8,128)(2,1)} %copy-done.19, ...), custom_call_target="tpu_custom_call" | custom-call | flops 1 | bytes 1 | tf_op jit(solution)/shard_map/input/pallas_call | solution.py:280
  289.1 1.2 slice.90
  291.0 2.8 fusion.2
  295.3 5.9 %delta.7.refs_0_.refs_4_ = bf16[3,8,128,128]{3,2,1,0:T(8,128)(2,1)} custom-call(f32[2,3,8,128,128]{4,3,2,1,0:T(8,128)} %get-tuple-element.38.mine_ref, bf16[2,3,8,128,128]{4,3,2,1,0:T(8,128)(2,1)} %collective-permute-done.14.got_ref, bf16[3,8,128,128]{3,2,1,0:T(8,128)(2,1)} %copy-done.21), custom_call_target="tpu_custom_call" | custom-call | flops 1 | bytes 1 | tf_op jit(solution)/shard_map/delta/pallas_call | solution.py:217
  301.1 1.3 slice.110
  304.4 1.4 collective-permute-start.16
  305.8 10.4 %collective-permute-done.11.refs_0_ = bf16[3,8,128,128]{3,2,1,0:T(8,128)(2,1)} collective-permute-done((bf16[3,8,128,128]{3,2,1,0:T(8,128)(2,1)}, bf16[3,8,128,128]{3,2,1,0:T(8,128)(2,1)}, u32[]{:S(2)}, u32[]{:S(2)}) %collective-permute-start.11) | collective-permute-done | bytes 786464 | tf_op jit(solution)/shard_map/ppermute | solution.py:161
  316.2 5.9 %delta.6.refs_0_.refs_4_ = bf16[3,8,128,128]{3,2,1,0:T(8,128)(2,1)} custom-call(f32[2,3,8,128,128]{4,3,2,1,0:T(8,128)} %get-tuple-element.34.mine_ref, bf16[2,3,8,128,128]{4,3,2,1,0:T(8,128)(2,1)} %collective-permute-done.8.got_ref, bf16[3,8,128,128]{3,2,1,0:T(8,128)(2,1)} %collective-permute-done.11.refs_0_), custom_call_target="tpu_custom_call" | custom-call | flops 1 | bytes 1 | tf_op jit(solution)/shard_map/delta/pallas_call | solution.py:217
  325.0 16.3 %input.5 = (f32[2,4,128,1024]{3,2,1,0:T(8,128)}, f32[2,4,128,1024]{3,2,1,0:T(8,128)}) custom-call(s32[3,32,4]{2,1,0:T(8,128)} %get-tuple-element.65.rows_ref, bf16[3,8,128,128]{3,2,1,0:T(8,128)(2,1)} %delta.5.refs_0_.refs_4_, bf16[3,8,128,128]{3,2,1,0:T(8,128)(2,1)} %copy-done.6, ...), custom_call_target="tpu_custom_call", output_to_operand_aliasing={{0}: (7, {}), {1}: (8, {})} | custom-call | flops 1 | bytes 1 | tf_op jit(solution)/shard_map/input/pallas_call | solution.py:280
  343.3 1.4 collective-permute-start.12
  345.7 16.2 %input.6 = (f32[2,4,128,1024]{3,2,1,0:T(8,128)}, f32[2,4,128,1024]{3,2,1,0:T(8,128)}) custom-call(s32[3,32,4]{2,1,0:T(8,128)} %copy-done.9, bf16[3,8,128,128]{3,2,1,0:T(8,128)(2,1)} %delta.7.refs_0_.refs_4_, bf16[3,8,128,128]{3,2,1,0:T(8,128)(2,1)} %copy-done.7, ...), custom_call_target="tpu_custom_call", output_to_operand_aliasing={{0}: (7, {}), {1}: (8, {})} | custom-call | flops 1 | bytes 1 | tf_op jit(solution)/shard_map/input/pallas_call | solution.py:280
  364.0 2.2 collective-permute-done.25.refs_3_.refs_7_
  367.0 16.2 %input.7 = (f32[2,4,128,1024]{3,2,1,0:T(8,128)}, f32[2,4,128,1024]{3,2,1,0:T(8,128)}) custom-call(s32[3,32,4]{2,1,0:T(8,128)} %copy-done.9, bf16[3,8,128,128]{3,2,1,0:T(8,128)(2,1)} %delta.6.refs_0_.refs_4_, bf16[3,8,128,128]{3,2,1,0:T(8,128)(2,1)} %copy-done.5, bf16[3,8,128,128]{3,2,1,0:T(8,128)(2,1)} %copy-done.14, ...), custom_call_target="tpu_custom_call", output_to_operand_aliasing={{0}: (7, {}), {1}: (8, {})} | custom-call | flops 1 | bytes 1 | tf_op jit(solution)/shard_map/input/pallas_call | solution.py:280
  383.2 2.7 convert_element_type.156
  386.1 4.0 collective-permute-done.26
  391.5 1.4 collective-permute-start.27
  394.7 12.3 %weight.5 = (bf16[4,32,128,128]{3,2,1,0:T(8,128)(2,1)}, bf16[4,32,128,128]{3,2,1,0:T(8,128)(2,1)}, bf16[4,32,128,128]{3,2,1,0:T(8,128)(2,1)}) custom-call(s32[3,32,4]{2,1,0:T(8,128)} %broadcast_add_fusion.6.rows_ref, bf16[4,128,1024]{2,1,0:T(8,128)(2,1)} %bitcast.64, ...), custom_call_target="tpu_custom_call", output_to_operand_aliasing={{0}: (10, {}), {1}: (11, {}), {2}: (12, {})} | custom-call | flops 1 | bytes 1 | tf_op jit(solution)/shard_map/weight/pallas_call | solution.py:250
  407.0 12.4 %weight.6 = (bf16[4,32,128,128]{3,2,1,0:T(8,128)(2,1)}, bf16[4,32,128,128]{3,2,1,0:T(8,128)(2,1)}, bf16[4,32,128,128]{3,2,1,0:T(8,128)(2,1)}) custom-call(s32[3,32,4]{2,1,0:T(8,128)} %broadcast_add_fusion.6.rows_ref, bf16[4,128,1024]{2,1,0:T(8,128)(2,1)} %bitcast.65, ...), custom_call_target="tpu_custom_call", output_to_operand_aliasing={{0}: (10, {}), {1}: (11, {}), {2}: (12, {})} | custom-call | flops 1 | bytes 1 | tf_op jit(solution)/shard_map/weight/pallas_call | solution.py:250
  421.3 2.9 fusion.11
  425.0 3.1 collective-permute-start.29
  431.1 12.3 %weight.7 = (bf16[4,32,128,128]{3,2,1,0:T(8,128)(2,1)}, bf16[4,32,128,128]{3,2,1,0:T(8,128)(2,1)}, bf16[4,32,128,128]{3,2,1,0:T(8,128)(2,1)}) custom-call(s32[3,32,4]{2,1,0:T(8,128)} %broadcast_add_fusion.1.rows_ref, bf16[4,128,1024]{2,1,0:T(8,128)(2,1)} %bitcast.66, ...), custom_call_target="tpu_custom_call", output_to_operand_aliasing={{0}: (10, {}), {1}: (11, {}), {2}: (12, {})} | custom-call | flops 1 | bytes 1 | tf_op jit(solution)/shard_map/weight/pallas_call | solution.py:250
  443.4 3.2 collective-permute-done.29
  446.6 2.0 fusion.6
  (123 shorter events, 34.8 us)
Async XLA Ops:
  7.2 33.1 %all-gather.5.cloned.1.call-start = ((), (), s32[]{:S(2)}) async-start(), calls=%async_computation | async-start | bytes 1310720 | tf_op jit(solution)/shard_map/all_gather | solution.py:177
  7.9 61.4 %all-gather.7.cloned.1.call-start = ((), (), s32[]{:S(2)}) async-start(), calls=%async_computation.1 | async-start | bytes 1310720 | tf_op jit(solution)/shard_map/all_gather | solution.py:178
  40.2 30.5 %collective-permute-start = (bf16[4,128,1024]{2,1,0:T(8,128)(2,1)}, bf16[4,128,1024]{2,1,0:T(8,128)(2,1)}, u32[]{:S(2)}, u32[]{:S(2)}) collective-permute-start(bf16[4,128,1024]{2,1,0:T(8,128)(2,1)} %bitcast.67), channel_id=1, source_target_pairs={{2,0},{3,1},{0,2},{1,3},{6,4},{7,5},{4,6},{5,7},{10,8},{11,9},{8,1... | collective-permute-start | bytes 3145736 | tf_op jit(solution)/shard_map/ppermute | solution.py:161
  69.3 25.0 %collective-permute-start.3 = (bf16[4,128,1024]{2,1,0:T(8,128)(2,1)}, bf16[4,128,1024]{2,1,0:T(8,128)(2,1)S(1)}, u32[]{:S(2)}, u32[]{:S(2)}) collective-permute-start(bf16[4,128,1024]{2,1,0:T(8,128)(2,1)} %bitcast.57), channel_id=1, source_target_pairs={{2,0},{3,1},{0,2},{1,3},{6,4},{7,5},{4,6},{5,7},{10,8},{11,9},{8,1... | collective-permute-start | bytes 3145736 | tf_op jit(solution)/shard_map/ppermute | solution.py:161
  70.7 27.0 %collective-permute-start.1 = (bf16[4,128,1024]{2,1,0:T(8,128)(2,1)}, bf16[4,128,1024]{2,1,0:T(8,128)(2,1)}, u32[]{:S(2)}, u32[]{:S(2)}) collective-permute-start(bf16[4,128,1024]{2,1,0:T(8,128)(2,1)} %bitcast.68), channel_id=1, source_target_pairs={{0,1},{1,0},{2,3},{3,2},{4,5},{5,4},{6,7},{7,6},{8,9},{9,8},{10,11... | collective-permute-start | bytes 3145736 | tf_op jit(solution)/shard_map/ppermute | solution.py:158
  70.7 27.0 %collective-permute-start.2 = (bf16[4,128,1024]{2,1,0:T(8,128)(2,1)}, bf16[4,128,1024]{2,1,0:T(8,128)(2,1)}, u32[]{:S(2)}, u32[]{:S(2)}) collective-permute-start(bf16[4,128,1024]{2,1,0:T(8,128)(2,1)} %collective-permute-done.refs_1_), channel_id=1, source_target_pairs={{0,1},{1,0},{2,3},{3,2},{4,5},{5,4},{6,7},{7,6},{8,9},{9,8},{10,11... | collective-permute-start | bytes 3145736 | tf_op jit(solution)/shard_map/ppermute | solution.py:158
  71.2 46.5 %collective-permute-start.4 = (bf16[4,128,1024]{2,1,0:T(8,128)(2,1)}, bf16[4,128,1024]{2,1,0:T(8,128)(2,1)S(1)}, u32[]{:S(2)}, u32[]{:S(2)}) collective-permute-start(bf16[4,128,1024]{2,1,0:T(8,128)(2,1)} %bitcast.58), channel_id=1, source_target_pairs={{0,1},{1,0},{2,3},{3,2},{4,5},{5,4},{6,7},{7,6},{8,9},{9,8},{10,11... | collective-permute-start | bytes 3145736 | tf_op jit(solution)/shard_map/ppermute | solution.py:158
  94.2 21.0 %copy-start.1 = (bf16[4,128,1024]{2,1,0:T(8,128)(2,1)}, bf16[4,128,1024]{2,1,0:T(8,128)(2,1)S(1)}, u32[]{:S(2)}) copy-start(bf16[4,128,1024]{2,1,0:T(8,128)(2,1)S(1)} %collective-permute-done.3.refs_5_.refs_1_) | copy-start | bytes 3145732
  94.2 23.5 %collective-permute-start.5 = (bf16[4,128,1024]{2,1,0:T(8,128)(2,1)S(1)}, bf16[4,128,1024]{2,1,0:T(8,128)(2,1)S(1)}, u32[]{:S(2)}, u32[]{:S(2)}) collective-permute-start(bf16[4,128,1024]{2,1,0:T(8,128)(2,1)S(1)} %collective-permute-done.3.refs_5_.refs_1_), channel_id=1, source_target_pairs={{0,1},{1,0},{2,3},{3,2},{4,5},{5,4},{6,7},{7,6},{8,9},{9,8},{10,11... | collective-permute-start | bytes 3145736 | tf_op jit(solution)/shard_map/ppermute | solution.py:158
  97.7 19.4 %copy-start.9 = (s32[3,32,4]{2,1,0:T(8,128)}, s32[3,32,4]{2,1,0:T(8,128)S(1)}, u32[]{:S(2)}) copy-start(s32[3,32,4]{2,1,0:T(8,128)S(1)} %copy.57.rows_ref) | copy-start | bytes 4612
  117.7 1.3 copy-start.3
  131.9 3.7 collective-permute-start.6
  135.6 22.1 %copy-start.12 = (bf16[2,3,8,128,128]{4,3,2,1,0:T(8,128)(2,1)}, bf16[2,3,8,128,128]{4,3,2,1,0:T(8,128)(2,1)S(1)}, u32[]{:S(2)}) copy-start(bf16[2,3,8,128,128]{4,3,2,1,0:T(8,128)(2,1)S(1)} %collective-permute-done.6.got_ref) | copy-start | bytes 4718596
  137.8 19.9 %collective-permute-start.7 = (bf16[3,8,128,128]{3,2,1,0:T(8,128)(2,1)S(1)}, bf16[3,8,128,128]{3,2,1,0:T(8,128)(2,1)S(1)}, u32[]{:S(2)}, u32[]{:S(2)}) collective-permute-start(bf16[3,8,128,128]{3,2,1,0:T(8,128)(2,1)S(1)} %bitcast.75), channel_id=1, source_target_pairs={{2,0},{3,1},{0,2},{1,3},{6,4},{7,5},{4,6},{5,7},{10,8},{11,9},{8,1... | collective-permute-start | bytes 2359304 | tf_op jit(solution)/shard_map/ppermute | solution.py:161
  164.4 19.2 %collective-permute-start.18 = (bf16[3,8,128,128]{3,2,1,0:T(8,128)(2,1)}, bf16[3,8,128,128]{3,2,1,0:T(8,128)(2,1)S(1)}, u32[]{:S(2)}, u32[]{:S(2)}) collective-permute-start(bf16[3,8,128,128]{3,2,1,0:T(8,128)(2,1)} %delta.4.refs_4_.refs_0_), channel_id=1, source_target_pairs={{2,0},{3,1},{0,2},{1,3},{6,4},{7,5},{4,6},{5,7},{10,8},{11,9},{8,1... | collective-permute-start | bytes 2359304 | tf_op jit(solution)/shard_map/ppermute | solution.py:161
  165.9 34.1 %collective-permute-start.19 = (bf16[3,8,128,128]{3,2,1,0:T(8,128)(2,1)}, bf16[3,8,128,128]{3,2,1,0:T(8,128)(2,1)S(1)}, u32[]{:S(2)}, u32[]{:S(2)}) collective-permute-start(bf16[3,8,128,128]{3,2,1,0:T(8,128)(2,1)} %delta.4.refs_4_.refs_0_), channel_id=1, source_target_pairs={{0,1},{1,0},{2,3},{3,2},{4,5},{5,4},{6,7},{7,6},{8,9},{9,8},{10,11... | collective-permute-start | bytes 2359304 | tf_op jit(solution)/shard_map/ppermute | solution.py:158
  183.6 12.8 %copy-start.17 = (bf16[3,8,128,128]{3,2,1,0:T(8,128)(2,1)}, bf16[3,8,128,128]{3,2,1,0:T(8,128)(2,1)S(1)}, u32[]{:S(2)}) copy-start(bf16[3,8,128,128]{3,2,1,0:T(8,128)(2,1)S(1)} %collective-permute-done.18.refs_5_.refs_1_) | copy-start | bytes 2359300
  183.6 16.4 %collective-permute-start.20 = (bf16[3,8,128,128]{3,2,1,0:T(8,128)(2,1)S(1)}, bf16[3,8,128,128]{3,2,1,0:T(8,128)(2,1)S(1)}, u32[]{:S(2)}, u32[]{:S(2)}) collective-permute-start(bf16[3,8,128,128]{3,2,1,0:T(8,128)(2,1)S(1)} %collective-permute-done.18.refs_5_.refs_1_), channel_id=1, source_target_pairs={{0,1},{1,0},{2,3},{3,2},{4,5},{5,4},{6,7},{7,6},{8,9},{9,8},{10,11... | collective-permute-start | bytes 2359304 | tf_op jit(solution)/shard_map/ppermute | solution.py:158
  196.4 46.2 %collective-permute-start.9 = (bf16[2,3,8,128,128]{4,3,2,1,0:T(8,128)(2,1)}, bf16[2,3,8,128,128]{4,3,2,1,0:T(8,128)(2,1)}, u32[]{:S(2)}, u32[]{:S(2)}) collective-permute-start(bf16[2,3,8,128,128]{4,3,2,1,0:T(8,128)(2,1)} %get-tuple-element.37), channel_id=1, source_target_pairs={{0,1},{1,0},{2,3},{3,2},{4,5},{5,4},{6,7},{7,6},{8,9},{9,8},{10,11... | collective-permute-start | bytes 4718600 | tf_op jit(solution)/shard_map/ppermute | solution.py:158
  200.0 16.0 %copy-start.10 = (s32[3,32,4]{2,1,0:T(8,128)S(1)}, s32[3,32,4]{2,1,0:T(8,128)}, u32[]{:S(2)}) copy-start(s32[3,32,4]{2,1,0:T(8,128)} %copy-done.9) | copy-start | bytes 4612
  229.6 16.7 %collective-permute-start.14 = (bf16[2,3,8,128,128]{4,3,2,1,0:T(8,128)(2,1)}, bf16[2,3,8,128,128]{4,3,2,1,0:T(8,128)(2,1)}, u32[]{:S(2)}, u32[]{:S(2)}) collective-permute-start(bf16[2,3,8,128,128]{4,3,2,1,0:T(8,128)(2,1)} %get-tuple-element.39), channel_id=1, source_target_pairs={{0,1},{1,0},{2,3},{3,2},{4,5},{5,4},{6,7},{7,6},{8,9},{9,8},{10,11... | collective-permute-start | bytes 4718600 | tf_op jit(solution)/shard_map/ppermute | solution.py:158
  229.6 13.0 %copy-start.8 = (f32[2,3,8,128,128]{4,3,2,1,0:T(8,128)S(1)}, f32[2,3,8,128,128]{4,3,2,1,0:T(8,128)}, u32[]{:S(2)}) copy-start(f32[2,3,8,128,128]{4,3,2,1,0:T(8,128)} %get-tuple-element.36.mine_ref) | copy-start | bytes 9437188
  242.1 48.9 %collective-permute-start.8 = (bf16[2,3,8,128,128]{4,3,2,1,0:T(8,128)(2,1)}, bf16[2,3,8,128,128]{4,3,2,1,0:T(8,128)(2,1)}, u32[]{:S(2)}, u32[]{:S(2)}) collective-permute-start(bf16[2,3,8,128,128]{4,3,2,1,0:T(8,128)(2,1)} %get-tuple-element.35), channel_id=1, source_target_pairs={{0,1},{1,0},{2,3},{3,2},{4,5},{5,4},{6,7},{7,6},{8,9},{9,8},{10,11... | collective-permute-start | bytes 4718600 | tf_op jit(solution)/shard_map/ppermute | solution.py:158
  244.9 20.6 %collective-permute-start.10 = (bf16[3,8,128,128]{3,2,1,0:T(8,128)(2,1)}, bf16[3,8,128,128]{3,2,1,0:T(8,128)(2,1)S(1)}, u32[]{:S(2)}, u32[]{:S(2)}) collective-permute-start(bf16[3,8,128,128]{3,2,1,0:T(8,128)(2,1)} %fusion.1), channel_id=1, source_target_pairs={{2,0},{3,1},{0,2},{1,3},{6,4},{7,5},{4,6},{5,7},{10,8},{11,9},{8,1... | collective-permute-start | bytes 2359304 | tf_op jit(solution)/shard_map/ppermute | solution.py:161
  248.1 46.2 %collective-permute-start.15 = (bf16[3,8,128,128]{3,2,1,0:T(8,128)(2,1)S(1)}, bf16[3,8,128,128]{3,2,1,0:T(8,128)(2,1)S(1)}, u32[]{:S(2)}, u32[]{:S(2)}) collective-permute-start(bf16[3,8,128,128]{3,2,1,0:T(8,128)(2,1)S(1)} %fusion.3), channel_id=1, source_target_pairs={{2,0},{3,1},{0,2},{1,3},{6,4},{7,5},{4,6},{5,7},{10,8},{11,9},{8,1... | collective-permute-start | bytes 2359304 | tf_op jit(solution)/shard_map/ppermute | solution.py:161
  272.3 30.8 %collective-permute-start.21 = (bf16[3,8,128,128]{3,2,1,0:T(8,128)(2,1)}, bf16[3,8,128,128]{3,2,1,0:T(8,128)(2,1)S(1)}, u32[]{:S(2)}, u32[]{:S(2)}) collective-permute-start(bf16[3,8,128,128]{3,2,1,0:T(8,128)(2,1)} %delta.5.refs_0_.refs_4_), channel_id=1, source_target_pairs={{2,0},{3,1},{0,2},{1,3},{6,4},{7,5},{4,6},{5,7},{10,8},{11,9},{8,1... | collective-permute-start | bytes 2359304 | tf_op jit(solution)/shard_map/ppermute | solution.py:161
  273.7 50.1 %collective-permute-start.22 = (bf16[3,8,128,128]{3,2,1,0:T(8,128)(2,1)}, bf16[3,8,128,128]{3,2,1,0:T(8,128)(2,1)S(1)}, u32[]{:S(2)}, u32[]{:S(2)}) collective-permute-start(bf16[3,8,128,128]{3,2,1,0:T(8,128)(2,1)} %delta.5.refs_0_.refs_4_), channel_id=1, source_target_pairs={{0,1},{1,0},{2,3},{3,2},{4,5},{5,4},{6,7},{7,6},{8,9},{9,8},{10,11... | collective-permute-start | bytes 2359304 | tf_op jit(solution)/shard_map/ppermute | solution.py:158
  293.7 22.4 %collective-permute-start.11 = (bf16[3,8,128,128]{3,2,1,0:T(8,128)(2,1)}, bf16[3,8,128,128]{3,2,1,0:T(8,128)(2,1)}, u32[]{:S(2)}, u32[]{:S(2)}) collective-permute-start(bf16[3,8,128,128]{3,2,1,0:T(8,128)(2,1)} %fusion.2), channel_id=1, source_target_pairs={{2,0},{3,1},{0,2},{1,3},{6,4},{7,5},{4,6},{5,7},{10,8},{11,9},{8,1... | collective-permute-start | bytes 2359304 | tf_op jit(solution)/shard_map/ppermute | solution.py:161
  303.1 18.9 %copy-start.6 = (bf16[3,8,128,128]{3,2,1,0:T(8,128)(2,1)}, bf16[3,8,128,128]{3,2,1,0:T(8,128)(2,1)S(1)}, u32[]{:S(2)}) copy-start(bf16[3,8,128,128]{3,2,1,0:T(8,128)(2,1)S(1)} %collective-permute-done.21.refs_1_.refs_5_) | copy-start | bytes 2359300
  304.2 19.6 %collective-permute-start.23 = (bf16[3,8,128,128]{3,2,1,0:T(8,128)(2,1)}, bf16[3,8,128,128]{3,2,1,0:T(8,128)(2,1)S(1)}, u32[]{:S(2)}, u32[]{:S(2)}) collective-permute-start(bf16[3,8,128,128]{3,2,1,0:T(8,128)(2,1)} %add_add_fusion.1), channel_id=1, source_target_pairs={{0,1},{1,0},{2,3},{3,2},{4,5},{5,4},{6,7},{7,6},{8,9},{9,8},{10,11... | collective-permute-start | bytes 2359304 | tf_op jit(solution)/shard_map/ppermute | solution.py:158
  304.4 38.7 %collective-permute-start.16 = (bf16[3,8,128,128]{3,2,1,0:T(8,128)(2,1)}, bf16[3,8,128,128]{3,2,1,0:T(8,128)(2,1)S(1)}, u32[]{:S(2)}, u32[]{:S(2)}) collective-permute-start(bf16[3,8,128,128]{3,2,1,0:T(8,128)(2,1)} %delta.7.refs_0_.refs_4_), channel_id=1, source_target_pairs={{2,0},{3,1},{0,2},{1,3},{6,4},{7,5},{4,6},{5,7},{10,8},{11,9},{8,1... | collective-permute-start | bytes 2359304 | tf_op jit(solution)/shard_map/ppermute | solution.py:161
  305.8 39.1 %collective-permute-start.17 = (bf16[3,8,128,128]{3,2,1,0:T(8,128)(2,1)}, bf16[3,8,128,128]{3,2,1,0:T(8,128)(2,1)}, u32[]{:S(2)}, u32[]{:S(2)}) collective-permute-start(bf16[3,8,128,128]{3,2,1,0:T(8,128)(2,1)} %delta.7.refs_0_.refs_4_), channel_id=1, source_target_pairs={{0,1},{1,0},{2,3},{3,2},{4,5},{5,4},{6,7},{7,6},{8,9},{9,8},{10,11... | collective-permute-start | bytes 2359304 | tf_op jit(solution)/shard_map/ppermute | solution.py:158
  325.0 18.3 %copy-start.4 = (bf16[3,8,128,128]{3,2,1,0:T(8,128)(2,1)S(1)}, bf16[3,8,128,128]{3,2,1,0:T(8,128)(2,1)}, u32[]{:S(2)}) copy-start(bf16[3,8,128,128]{3,2,1,0:T(8,128)(2,1)} %delta.6.refs_0_.refs_4_) | copy-start | bytes 2359300
  343.1 2.6 copy-start.7
  343.2 2.5 collective-permute-start.24
  343.3 20.4 %collective-permute-start.12 = (bf16[3,8,128,128]{3,2,1,0:T(8,128)(2,1)S(1)}, bf16[3,8,128,128]{3,2,1,0:T(8,128)(2,1)S(1)}, u32[]{:S(2)}, u32[]{:S(2)}) collective-permute-start(bf16[3,8,128,128]{3,2,1,0:T(8,128)(2,1)S(1)} %copy-done.4), channel_id=1, source_target_pairs={{2,0},{3,1},{0,2},{1,3},{6,4},{7,5},{4,6},{5,7},{10,8},{11,9},{8,1... | collective-permute-start | bytes 2359304 | tf_op jit(solution)/shard_map/ppermute | solution.py:161
  344.7 19.2 %collective-permute-start.13 = (bf16[3,8,128,128]{3,2,1,0:T(8,128)(2,1)S(1)}, bf16[3,8,128,128]{3,2,1,0:T(8,128)(2,1)S(1)}, u32[]{:S(2)}, u32[]{:S(2)}) collective-permute-start(bf16[3,8,128,128]{3,2,1,0:T(8,128)(2,1)S(1)} %copy-done.4), channel_id=1, source_target_pairs={{0,1},{1,0},{2,3},{3,2},{4,5},{5,4},{6,7},{7,6},{8,9},{9,8},{10,11... | collective-permute-start | bytes 2359304 | tf_op jit(solution)/shard_map/ppermute | solution.py:158
  363.7 2.4 copy-start.5
  363.8 2.4 collective-permute-start.25
  364.0 2.2 copy-start.14
  383.2 6.9 %copy-start = (f32[2,4,128,1024]{3,2,1,0:T(8,128)S(1)}, f32[2,4,128,1024]{3,2,1,0:T(8,128)}, u32[]{:S(2)}) copy-start(f32[2,4,128,1024]{3,2,1,0:T(8,128)} %get-tuple-element.47) | copy-start | bytes 12582916
  385.9 4.2 collective-permute-start.26
  390.1 1.3 copy-start.20
  390.1 3.9 copy-start.11
  391.5 29.8 %collective-permute-start.27 = (bf16[4,128,1024]{2,1,0:T(8,128)(2,1)S(1)}, bf16[4,128,1024]{2,1,0:T(8,128)(2,1)}, u32[]{:S(2)}, u32[]{:S(2)}) collective-permute-start(bf16[4,128,1024]{2,1,0:T(8,128)(2,1)S(1)} %bitcast.74), channel_id=1, source_target_pairs={{2,0},{3,1},{0,2},{1,3},{6,4},{7,5},{4,6},{5,7},{10,8},{11,9},{8,1... | collective-permute-start | bytes 3145736 | tf_op jit(solution)/shard_map/ppermute | solution.py:161
  425.0 18.4 %collective-permute-start.28 = (bf16[128,1024]{1,0:T(8,128)(2,1)}, bf16[128,1024]{1,0:T(8,128)(2,1)}, u32[]{:S(2)}, u32[]{:S(2)}) collective-permute-start(bf16[128,1024]{1,0:T(8,128)(2,1)} %get-tuple-element.62), channel_id=1, source_target_pairs={{0,4},{4,8},{8,12},{12,0},{1,5},{5,9},{9,13},{13,1},{2,6},{6,10},{... | collective-permute-start | bytes 786440 | tf_op jit(solution)/shard_map/ppermute | solution.py:314
  425.0 21.6 %collective-permute-start.29 = (bf16[128,1024]{1,0:T(8,128)(2,1)}, bf16[128,1024]{1,0:T(8,128)(2,1)}, u32[]{:S(2)}, u32[]{:S(2)}) collective-permute-start(bf16[128,1024]{1,0:T(8,128)(2,1)} %get-tuple-element.64), channel_id=1, source_target_pairs={{0,8},{4,12},{8,0},{12,4},{1,9},{5,13},{9,1},{13,5},{2,10},{6,14},... | collective-permute-start | bytes 786440 | tf_op jit(solution)/shard_map/ppermute | solution.py:314
  428.2 18.5 %collective-permute-start.30 = (bf16[128,1024]{1,0:T(8,128)(2,1)S(1)}, bf16[128,1024]{1,0:T(8,128)(2,1)}, u32[]{:S(2)}, u32[]{:S(2)}) collective-permute-start(bf16[128,1024]{1,0:T(8,128)(2,1)S(1)} %get-tuple-element.63), channel_id=1, source_target_pairs={{0,12},{4,0},{8,4},{12,8},{1,13},{5,1},{9,5},{13,9},{2,14},{6,2},{... | collective-permute-start | bytes 786440 | tf_op jit(solution)/shard_map/ppermute | solution.py:314
  (9 other events, 8.5 us)
Sparse Core Ops, SparseCore 0:
  9.6 30.6 all-gather.4
  41.8 27.4 all-gather.6

commit v4 on v3

--- a/solution.py
+++ b/solution.py
@@ -175,7 +175,8 @@
     rows = jnp.sum(chosen[None, :, :, None] * listing[:, None, :, :], axis=2)
 
     inputs = gather_dp(lax.all_gather(activations, "blk", axis=0))
-    cotangents = gather_dp(lax.all_gather(output_grad, "blk", axis=0))
+    cotangents = lax.all_gather(output_grad, "blk", axis=0)
+    cotangents = [cotangents] + [from_x(cotangents, k) for k in range(1, n_x)]
     token_shape = (n_blk, tokens, features)
     params = pltpu.CompilerParams(vmem_limit_bytes=VMEM_LIMIT)
 
@@ -196,6 +197,7 @@
         cost_estimate=LITTLE,
         name="turn",
     )(*inputs)
+    cotangents = cotangents + [other_core(cotangents[0])] + [other_core(after(v, turned)) for v in cotangents[1:]]
 
     def forward(c, order):
         mine, theirs = pl.pallas_call(
@@ -224,25 +226,34 @@
             name="delta",
         )(mine, got, *arrived)
 
-    sends, own_deltas, columns = [], [], []
+    sends, own_deltas, columns, halves = [], [], [], []
+
+    def finish(c, *values):
+        mine, got, arrived = halves[c]
+        delta = to_delta(mine, got, [after(v, *values) for v in arrived])
+        own_deltas.append(delta)
+        columns.append([from_x(delta, k) for k in range(1, n_x)])
+
     for c in range(chunks):
         if c == 0:
             order = after(rows, turned)
-        elif c == 1:
-            order = rows
         elif c == 2:
-            order = after(rows, sends[0])
+            order = after(rows, own_deltas[0])
         else:
-            order = after(rows, own_deltas[c - 3])
+            order = after(rows, sends[c - 1])
         mine, got = forward(c, order)
+        if c == 1:
+            finish(0, mine)
+        elif c == 2:
+            finish(1, mine)
         send = mine[1:] + got[1:].astype(F32)
         if c >= 2:
             send = after(send, own_deltas[c - 2])
         send = send.astype(BF16)
         sends.append(send)
-        delta = to_delta(mine, got, [from_x(send[k - 1], n_x - k) for k in range(1, n_x)])
-        own_deltas.append(delta)
-        columns.append([from_x(delta, k) for k in range(1, n_x)])
+        halves.append((mine, got, [from_x(send[k - 1], n_x - k) for k in range(1, n_x)]))
+    for c in range(len(own_deltas), chunks):
+        finish(c)
 
     grad_shape = jax.ShapeDtypeStruct(gate_weight.shape, BF16)
 

time: 464 us -> 417 us (0.90)
  waiting for transfers between devices: 160 us -> 108 us
    ppermute x11, waiting for transfers between devices: 86.1 us -> 56.1 us  [from_x(): lax.ppermute(value, 'dp', [((i + 2 * step) % n_dp, i) for i in range(n_dp)])]
    all_gather x1, waiting for transfers between devices: 27.6 us -> 4.05 us  [body(): cotangents = lax.all_gather(output_grad, 'blk', axis=0)]
    slice x13 -> x16, local copies, waits for them, and re-layouts: 13.7 us -> 17.4 us  [after(): array = array + (value[(0,) * value.ndim] * 0).astype(array.dtype)]
  transfers between devices with their start and end apart: 33 -> 33, of which waited for: 12 -> 15; matrix products, arithmetic and copies ran while one was open for 6% -> 8% of each run, Pallas kernels for 37% -> 41%
where the time goes in v4:
time: 417 us; the launch traced here: 408 us
  Pallas kernels  204 us (49%)
  waiting for transfers between devices  108 us (26%)
  other arithmetic  26.2 us (6%)
  between operations  24.8 us (6%)
  local copies, waits for them, and re-layouts  24.3 us (6%)
  starting transfers between devices  20.6 us (5%)
    pallas_call x4, Pallas kernels, body(): pl.pallas_call(functools.partial(input_kernel, n_dp, keep, per, c * part,...  62.1 us
    ppermute x11, waiting for transfers between devices, from_x(): lax.ppermute(value, 'dp', [((i + 2 * step) % n_dp, i) for i in range(n_dp)])  56.1 us
    pallas_call x4, Pallas kernels, forward(): pl.pallas_call(functools.partial(forward_kernel, n_dp, keep, per, c * par...  51.5 us
    pallas_call x4, Pallas kernels, weights(): pl.pallas_call(functools.partial(weight_kernel, n_dp, keep, per, c * part...  49.5 us
    all_gather x1, waiting for transfers between devices, body(): inputs = gather_dp(lax.all_gather(activations, 'blk', axis=0))  31.6 us
    pallas_call x4, Pallas kernels, to_delta(): pl.pallas_call(delta_kernel, grid=(part,), in_specs=[pl.BlockSpec((1, 3,...  23.6 us
    pallas_call x1, Pallas kernels, body(): pl.pallas_call(turn_kernel, grid=(row_blocks,), in_specs=[pl.BlockSpec((1...  17.5 us
    slice x16, local copies, waits for them, and re-layouts, after(): array = array + (value[(0,) * value.ndim] * 0).astype(array.dtype)  17.4 us
  transfers between devices with their start and end apart: 33, of which 15 were waited for; matrix products, arithmetic and copies ran while one was open for 8% of the time, Pallas kernels for 41%

profile of v4, /device:TPU:0, one launch (start us, length us, event | category | flops | bytes accessed | tf_op | source)
XLA Modules:
  0.0 408.4 jit_solution(10989833056846768972)
XLA Ops:
  8.6 31.6 %all-gather.5.cloned.1.call-done = bf16[512,1024]{1,0:T(8,128)(2,1)} async-done(((bf16[128,1024]{1,0:T(8,128)(2,1)}), bf16[512,1024]{1,0:T(8,128)(2,1)}) %all-gather.5.cloned.1.call-update) | async-done | bytes 1048592 | tf_op jit(solution)/shard_map/all_gather | solution.py:177
  40.2 1.5 collective-permute-start
  41.7 23.5 %collective-permute-done.refs_1_ = bf16[4,128,1024]{2,1,0:T(8,128)(2,1)S(1)} collective-permute-done((bf16[4,128,1024]{2,1,0:T(8,128)(2,1)}, bf16[4,128,1024]{2,1,0:T(8,128)(2,1)S(1)}, u32[]{:S(2)}, u32[]{:S(2)}) %collective-permute-start) | collective-permute-done | bytes 1048608 | tf_op jit(solution)/shard_map/ppermute | solution.py:161
  65.2 4.0 all-gather.7.cloned.1.call-done
  69.3 1.5 collective-permute-start.3
  70.7 17.5 %turn.1.refs_8_ = bf16[32,128,512]{2,1,0:T(8,128)(2,1)} custom-call(bf16[4,128,1024]{2,1,0:T(8,128)(2,1)} %bitcast.71, bf16[4,128,1024]{2,1,0:T(8,128)(2,1)} %copy-done.4, bf16[4,128,1024]{2,1,0:T(8,128)(2,1)} %collective-permute-done.1.refs_2_, bf16[4,128,1024]{2,1,0:T(8,128)(2,1)} %collective-permute-done.2.refs_3_), custom_call_target="tpu_custom_call" | custom-call | flops 1 | bytes 1 | tf_op jit(solution)/shard_map/turn/pallas_call | solution.py:191
  90.2 4.0 collective-permute-done.3.refs_5_.refs_1_
  99.3 12.8 %forward.4 = (f32[2,3,8,128,128]{4,3,2,1,0:T(8,128)}, bf16[2,3,8,128,128]{4,3,2,1,0:T(8,128)(2,1)}) custom-call(s32[3,32,4]{2,1,0:T(8,128)} %broadcast_add_fusion.9.rows_ref, s32[32]{0:T(128)} %get-tuple-element.67.live_ref, bf16[4,128,1024]{2,1,0:T(8,128)(2,1)} %bitcast.72, bf16[4,128,1024]{2,1,0:T(8,128)(2,1)} %copy-done.4, ...), custom_call_target="tpu_custom_call" | custom-call | flops 1 | bytes 1 | tf_op jit(solution)/shard_map/forward/pallas_call | solution.py:203
  112.3 3.5 collective-permute-done.6.got_ref
  115.7 2.2 add_convert_fusion.4
  117.9 1.6 collective-permute-start.7
  121.3 12.8 %forward.5 = (f32[2,3,8,128,128]{4,3,2,1,0:T(8,128)}, bf16[2,3,8,128,128]{4,3,2,1,0:T(8,128)(2,1)}) custom-call(s32[3,32,4]{2,1,0:T(8,128)} %broadcast_add_fusion.8.rows_ref, s32[32]{0:T(128)} %get-tuple-element.67.live_ref, bf16[4,128,1024]{2,1,0:T(8,128)(2,1)} %bitcast.73, bf16[4,128,1024]{2,1,0:T(8,128)(2,1)} %copy-done.4, ...), custom_call_target="tpu_custom_call" | custom-call | flops 1 | bytes 1 | tf_op jit(solution)/shard_map/forward/pallas_call | solution.py:203
  136.0 1.6 collective-permute-done.7
  138.5 5.9 %delta.4.refs_4_.refs_0_ = bf16[3,8,128,128]{3,2,1,0:T(8,128)(2,1)} custom-call(f32[2,3,8,128,128]{4,3,2,1,0:T(8,128)} %get-tuple-element.32.mine_ref, bf16[2,3,8,128,128]{4,3,2,1,0:T(8,128)(2,1)} %copy-done.14, bf16[3,8,128,128]{3,2,1,0:T(8,128)(2,1)} %broadcast_add_fusion.3.refs_0_), custom_call_target="tpu_custom_call" | custom-call | flops 1 | bytes 1 | tf_op jit(solution)/shard_map/delta/pallas_call | solution.py:219
  144.5 1.5 collective-permute-start.18
  146.0 17.5 %collective-permute-done.18.refs_5_.refs_1_ = bf16[3,8,128,128]{3,2,1,0:T(8,128)(2,1)S(1)} collective-permute-done((bf16[3,8,128,128]{3,2,1,0:T(8,128)(2,1)}, bf16[3,8,128,128]{3,2,1,0:T(8,128)(2,1)S(1)}, u32[]{:S(2)}, u32[]{:S(2)}) %collective-permute-start.18) | collective-permute-done | bytes 786464 | tf_op jit(solution)/shard_map/ppermute | solution.py:161
  167.7 12.4 %weight.4 = (bf16[4,32,128,128]{3,2,1,0:T(8,128)(2,1)}, bf16[4,32,128,128]{3,2,1,0:T(8,128)(2,1)}, bf16[4,32,128,128]{3,2,1,0:T(8,128)(2,1)}) custom-call(s32[3,32,4]{2,1,0:T(8,128)} %copy-done.11, bf16[4,128,1024]{2,1,0:T(8,128)(2,1)} %bitcast.63, bf16[4,128,1024]{2,1,0:T(8,128)(2,1)} %copy-done, bf16[4,128,1024]{2,1,0:T(8,128)(2,1)} %copy-done.2, ...), custom_call_target="tpu_custom_call" | custom-call | flops 1 | bytes 1 | tf_op jit(solution)/shard_map/weight/pallas_call | solution.py:261
  182.6 13.0 %forward.6 = (f32[2,3,8,128,128]{4,3,2,1,0:T(8,128)}, bf16[2,3,8,128,128]{4,3,2,1,0:T(8,128)(2,1)}) custom-call(s32[3,32,4]{2,1,0:T(8,128)} %get-tuple-element.66.rows_ref, s32[32]{0:T(128)} %get-tuple-element.67.live_ref, bf16[4,128,1024]{2,1,0:T(8,128)(2,1)} %bitcast.74, bf16[4,128,1024]{2,1,0:T(8,128)(2,1)} %copy-done.4, ...), custom_call_target="tpu_custom_call" | custom-call | flops 1 | bytes 1 | tf_op jit(solution)/shard_map/forward/pallas_call | solution.py:203
  195.8 2.4 fusion.1
  198.2 1.5 collective-permute-start.11
  199.7 2.3 add_convert_fusion.3
  204.5 12.9 %forward.7 = (f32[2,3,8,128,128]{4,3,2,1,0:T(8,128)}, bf16[2,3,8,128,128]{4,3,2,1,0:T(8,128)(2,1)}) custom-call(s32[3,32,4]{2,1,0:T(8,128)} %broadcast_add_fusion.6.rows_ref, s32[32]{0:T(128)} %get-tuple-element.67.live_ref, bf16[4,128,1024]{2,1,0:T(8,128)(2,1)} %bitcast.75, bf16[4,128,1024]{2,1,0:T(8,128)(2,1)} %copy-done.4, ...), custom_call_target="tpu_custom_call" | custom-call | flops 1 | bytes 1 | tf_op jit(solution)/shard_map/forward/pallas_call | solution.py:203
  219.2 1.3 collective-permute-start.15
  221.5 5.9 %delta.5.refs_0_.refs_4_ = bf16[3,8,128,128]{3,2,1,0:T(8,128)(2,1)} custom-call(f32[2,3,8,128,128]{4,3,2,1,0:T(8,128)} %get-tuple-element.34.mine_ref, bf16[2,3,8,128,128]{4,3,2,1,0:T(8,128)(2,1)} %collective-permute-done.10.got_ref, bf16[3,8,128,128]{3,2,1,0:T(8,128)(2,1)} %broadcast_add_fusion.2.refs_0_), custom_call_target="tpu_custom_call" | custom-call | flops 1 | bytes 1 | tf_op jit(solution)/shard_map/delta/pallas_call | solution.py:219
  228.2 13.4 %input.4 = (f32[2,4,128,1024]{3,2,1,0:T(8,128)}, f32[2,4,128,1024]{3,2,1,0:T(8,128)}) custom-call(s32[3,32,4]{2,1,0:T(8,128)} %copy-done.11, bf16[3,8,128,128]{3,2,1,0:T(8,128)(2,1)} %delta.4.refs_4_.refs_0_, bf16[3,8,128,128]{3,2,1,0:T(8,128)(2,1)} %copy-done.19, bf16[3,8,128,128]{3,2,1,0:T(8,128)(2,1)} %copy-done.20, bf16[3,8,128,128]{3,2,1,0:T(8,128)(2,1)} %copy-done.21, ...), custom_call_target="tpu_custom_call" | custom-call | flops 1 | bytes 1 | tf_op jit(solution)/shard_map/input/pallas_call | solution.py:291
  241.6 1.3 slice.123
  246.4 5.9 %delta.7.refs_0_.refs_4_ = bf16[3,8,128,128]{3,2,1,0:T(8,128)(2,1)} custom-call(f32[2,3,8,128,128]{4,3,2,1,0:T(8,128)} %get-tuple-element.35.mine_ref, bf16[2,3,8,128,128]{4,3,2,1,0:T(8,128)(2,1)} %collective-permute-done.8.got_ref, bf16[3,8,128,128]{3,2,1,0:T(8,128)(2,1)} %copy-done.23), custom_call_target="tpu_custom_call" | custom-call | flops 1 | bytes 1 | tf_op jit(solution)/shard_map/delta/pallas_call | solution.py:219
  254.1 2.1 collective-permute-done.21.refs_1_.refs_5_
  256.4 3.1 fusion.2
  262.7 16.2 %input.5 = (f32[2,4,128,1024]{3,2,1,0:T(8,128)}, f32[2,4,128,1024]{3,2,1,0:T(8,128)}) custom-call(s32[3,32,4]{2,1,0:T(8,128)} %get-tuple-element.65.rows_ref, bf16[3,8,128,128]{3,2,1,0:T(8,128)(2,1)} %delta.5.refs_0_.refs_4_, bf16[3,8,128,128]{3,2,1,0:T(8,128)(2,1)} %copy-done.7, ...), custom_call_target="tpu_custom_call", output_to_operand_aliasing={{0}: (7, {}), {1}: (8, {})} | custom-call | flops 1 | bytes 1 | tf_op jit(solution)/shard_map/input/pallas_call | solution.py:291
  278.8 1.3 slice.105
  280.8 5.9 %delta.6.refs_0_.refs_4_ = bf16[3,8,128,128]{3,2,1,0:T(8,128)(2,1)} custom-call(f32[2,3,8,128,128]{4,3,2,1,0:T(8,128)} %get-tuple-element.37.mine_ref, bf16[2,3,8,128,128]{4,3,2,1,0:T(8,128)(2,1)} %collective-permute-done.9.got_ref, bf16[3,8,128,128]{3,2,1,0:T(8,128)(2,1)} %collective-permute-done.12.refs_0_), custom_call_target="tpu_custom_call" | custom-call | flops 1 | bytes 1 | tf_op jit(solution)/shard_map/delta/pallas_call | solution.py:219
  286.7 1.3 slice.125
  288.7 7.5 %collective-permute-done.16.refs_1_.refs_5_ = bf16[3,8,128,128]{3,2,1,0:T(8,128)(2,1)S(1)} collective-permute-done((bf16[3,8,128,128]{3,2,1,0:T(8,128)(2,1)S(1)}, bf16[3,8,128,128]{3,2,1,0:T(8,128)(2,1)S(1)}, u32[]{:S(2)}, u32[]{:S(2)}) %collective-permute-start.16) | collective-permute-done | bytes 786464 | tf_op jit(solution)/shard_map/ppermute | solution.py:161
  298.7 16.2 %input.6 = (f32[2,4,128,1024]{3,2,1,0:T(8,128)}, f32[2,4,128,1024]{3,2,1,0:T(8,128)}) custom-call(s32[3,32,4]{2,1,0:T(8,128)} %copy-done.11, bf16[3,8,128,128]{3,2,1,0:T(8,128)(2,1)} %delta.7.refs_0_.refs_4_, bf16[3,8,128,128]{3,2,1,0:T(8,128)(2,1)} %copy-done.8, ...), custom_call_target="tpu_custom_call", output_to_operand_aliasing={{0}: (7, {}), {1}: (8, {})} | custom-call | flops 1 | bytes 1 | tf_op jit(solution)/shard_map/input/pallas_call | solution.py:291
  314.9 1.3 slice.107
  317.1 2.1 collective-permute-done.25.refs_3_.refs_7_
  320.1 16.3 %input.7 = (f32[2,4,128,1024]{3,2,1,0:T(8,128)}, f32[2,4,128,1024]{3,2,1,0:T(8,128)}) custom-call(s32[3,32,4]{2,1,0:T(8,128)} %copy-done.11, bf16[3,8,128,128]{3,2,1,0:T(8,128)(2,1)} %delta.6.refs_0_.refs_4_, bf16[3,8,128,128]{3,2,1,0:T(8,128)(2,1)} %copy-done.6, bf16[3,8,128,128]{3,2,1,0:T(8,128)(2,1)} %copy-done.16, ...), custom_call_target="tpu_custom_call", output_to_operand_aliasing={{0}: (7, {}), {1}: (8, {})} | custom-call | flops 1 | bytes 1 | tf_op jit(solution)/shard_map/input/pallas_call | solution.py:291
  336.5 2.7 convert_element_type.176
  339.3 4.0 collective-permute-done.26
  347.6 12.4 %weight.5 = (bf16[4,32,128,128]{3,2,1,0:T(8,128)(2,1)}, bf16[4,32,128,128]{3,2,1,0:T(8,128)(2,1)}, bf16[4,32,128,128]{3,2,1,0:T(8,128)(2,1)}) custom-call(s32[3,32,4]{2,1,0:T(8,128)} %broadcast_add_fusion.10.rows_ref, bf16[4,128,1024]{2,1,0:T(8,128)(2,1)} %bitcast.66, ...), custom_call_target="tpu_custom_call", output_to_operand_aliasing={{0}: (10, {}), {1}: (11, {}), {2}: (12, {})} | custom-call | flops 1 | bytes 1 | tf_op jit(solution)/shard_map/weight/pallas_call | solution.py:261
  360.0 12.3 %weight.6 = (bf16[4,32,128,128]{3,2,1,0:T(8,128)(2,1)}, bf16[4,32,128,128]{3,2,1,0:T(8,128)(2,1)}, bf16[4,32,128,128]{3,2,1,0:T(8,128)(2,1)}) custom-call(s32[3,32,4]{2,1,0:T(8,128)} %broadcast_add_fusion.10.rows_ref, bf16[4,128,1024]{2,1,0:T(8,128)(2,1)} %bitcast.67, ...), custom_call_target="tpu_custom_call", output_to_operand_aliasing={{0}: (10, {}), {1}: (11, {}), {2}: (12, {})} | custom-call | flops 1 | bytes 1 | tf_op jit(solution)/shard_map/weight/pallas_call | solution.py:261
  374.2 2.9 fusion.10
  378.0 2.0 collective-permute-start.29
  379.9 2.9 collective-permute-start.30
  384.5 12.4 %weight.7 = (bf16[4,32,128,128]{3,2,1,0:T(8,128)(2,1)}, bf16[4,32,128,128]{3,2,1,0:T(8,128)(2,1)}, bf16[4,32,128,128]{3,2,1,0:T(8,128)(2,1)}) custom-call(s32[3,32,4]{2,1,0:T(8,128)} %broadcast_add_fusion.4.rows_ref, bf16[4,128,1024]{2,1,0:T(8,128)(2,1)} %bitcast.68, ...), custom_call_target="tpu_custom_call", output_to_operand_aliasing={{0}: (10, {}), {1}: (11, {}), {2}: (12, {})} | custom-call | flops 1 | bytes 1 | tf_op jit(solution)/shard_map/weight/pallas_call | solution.py:261
  396.9 2.6 collective-permute-done.29
  399.6 2.0 fusion.5
  (139 shorter events, 38.9 us)
Async XLA Ops:
  7.2 33.1 %all-gather.5.cloned.1.call-start = ((), (), s32[]{:S(2)}) async-start(), calls=%async_computation | async-start | bytes 1310720 | tf_op jit(solution)/shard_map/all_gather | solution.py:177
  7.9 61.4 %all-gather.7.cloned.1.call-start = ((), (), s32[]{:S(2)}) async-start(), calls=%async_computation.1 | async-start | bytes 1310720 | tf_op jit(solution)/shard_map/all_gather | solution.py:178
  40.2 25.0 %collective-permute-start = (bf16[4,128,1024]{2,1,0:T(8,128)(2,1)}, bf16[4,128,1024]{2,1,0:T(8,128)(2,1)S(1)}, u32[]{:S(2)}, u32[]{:S(2)}) collective-permute-start(bf16[4,128,1024]{2,1,0:T(8,128)(2,1)} %bitcast.69), channel_id=1, source_target_pairs={{2,0},{3,1},{0,2},{1,3},{6,4},{7,5},{4,6},{5,7},{10,8},{11,9},{8,1... | collective-permute-start | bytes 3145736 | tf_op jit(solution)/shard_map/ppermute | solution.py:161
  41.7 29.0 %collective-permute-start.1 = (bf16[4,128,1024]{2,1,0:T(8,128)(2,1)}, bf16[4,128,1024]{2,1,0:T(8,128)(2,1)}, u32[]{:S(2)}, u32[]{:S(2)}) collective-permute-start(bf16[4,128,1024]{2,1,0:T(8,128)(2,1)} %bitcast.70), channel_id=1, source_target_pairs={{0,1},{1,0},{2,3},{3,2},{4,5},{5,4},{6,7},{7,6},{8,9},{9,8},{10,11... | collective-permute-start | bytes 3145736 | tf_op jit(solution)/shard_map/ppermute | solution.py:158
  65.2 5.5 %copy-start.4 = (bf16[4,128,1024]{2,1,0:T(8,128)(2,1)}, bf16[4,128,1024]{2,1,0:T(8,128)(2,1)S(1)}, u32[]{:S(2)}) copy-start(bf16[4,128,1024]{2,1,0:T(8,128)(2,1)S(1)} %collective-permute-done.refs_1_) | copy-start | bytes 3145732
  65.2 5.5 %collective-permute-start.2 = (bf16[4,128,1024]{2,1,0:T(8,128)(2,1)S(1)}, bf16[4,128,1024]{2,1,0:T(8,128)(2,1)}, u32[]{:S(2)}, u32[]{:S(2)}) collective-permute-start(bf16[4,128,1024]{2,1,0:T(8,128)(2,1)S(1)} %collective-permute-done.refs_1_), channel_id=1, source_target_pairs={{0,1},{1,0},{2,3},{3,2},{4,5},{5,4},{6,7},{7,6},{8,9},{9,8},{10,11... | collective-permute-start | bytes 3145736 | tf_op jit(solution)/shard_map/ppermute | solution.py:158
  69.3 25.0 %collective-permute-start.3 = (bf16[4,128,1024]{2,1,0:T(8,128)(2,1)}, bf16[4,128,1024]{2,1,0:T(8,128)(2,1)S(1)}, u32[]{:S(2)}, u32[]{:S(2)}) collective-permute-start(bf16[4,128,1024]{2,1,0:T(8,128)(2,1)} %bitcast.59), channel_id=1, source_target_pairs={{2,0},{3,1},{0,2},{1,3},{6,4},{7,5},{4,6},{5,7},{10,8},{11,9},{8,1... | collective-permute-start | bytes 3145736 | tf_op jit(solution)/shard_map/ppermute | solution.py:161
  70.7 26.8 %collective-permute-start.4 = (bf16[4,128,1024]{2,1,0:T(8,128)(2,1)}, bf16[4,128,1024]{2,1,0:T(8,128)(2,1)S(1)}, u32[]{:S(2)}, u32[]{:S(2)}) collective-permute-start(bf16[4,128,1024]{2,1,0:T(8,128)(2,1)} %bitcast.60), channel_id=1, source_target_pairs={{0,1},{1,0},{2,3},{3,2},{4,5},{5,4},{6,7},{7,6},{8,9},{9,8},{10,11... | collective-permute-start | bytes 3145736 | tf_op jit(solution)/shard_map/ppermute | solution.py:158
  88.3 7.1 %copy-start.27 = (s32[112]{0:T(128)S(1)}, s32[112]{0:T(128)}, u32[]{:S(2)}) copy-start(s32[112]{0:T(128)} %param.17) | copy-start | bytes 1348
  88.3 7.4 %copy-start.24 = (s32[112,16]{0,1:T(8,128)S(1)}, s32[112,16]{0,1:T(8,128)}, u32[]{:S(2)}) copy-start(s32[112,16]{0,1:T(8,128)} %param.14) | copy-start | bytes 21508
  88.3 7.4 %copy-start.25 = (s32[112,16]{0,1:T(8,128)S(1)}, s32[112,16]{0,1:T(8,128)}, u32[]{:S(2)}) copy-start(s32[112,16]{0,1:T(8,128)} %param.15) | copy-start | bytes 21508
  88.3 7.4 %copy-start.26 = (s32[112,16]{0,1:T(8,128)S(1)}, s32[112,16]{0,1:T(8,128)}, u32[]{:S(2)}) copy-start(s32[112,16]{0,1:T(8,128)} %param.16) | copy-start | bytes 21508
  94.2 4.0 copy-start
  95.4 2.9 collective-permute-start.5
  96.9 23.8 %copy-start.11 = (s32[3,32,4]{2,1,0:T(8,128)}, s32[3,32,4]{2,1,0:T(8,128)S(1)}, u32[]{:S(2)}) copy-start(s32[3,32,4]{2,1,0:T(8,128)S(1)} %copy.58.rows_ref) | copy-start | bytes 4612
  112.1 3.6 collective-permute-start.6
  115.7 18.5 %copy-start.14 = (bf16[2,3,8,128,128]{4,3,2,1,0:T(8,128)(2,1)}, bf16[2,3,8,128,128]{4,3,2,1,0:T(8,128)(2,1)S(1)}, u32[]{:S(2)}) copy-start(bf16[2,3,8,128,128]{4,3,2,1,0:T(8,128)(2,1)S(1)} %collective-permute-done.6.got_ref) | copy-start | bytes 4718596
  117.9 19.7 %collective-permute-start.7 = (bf16[3,8,128,128]{3,2,1,0:T(8,128)(2,1)S(1)}, bf16[3,8,128,128]{3,2,1,0:T(8,128)(2,1)S(1)}, u32[]{:S(2)}, u32[]{:S(2)}) collective-permute-start(bf16[3,8,128,128]{3,2,1,0:T(8,128)(2,1)S(1)} %bitcast.77), channel_id=1, source_target_pairs={{2,0},{3,1},{0,2},{1,3},{6,4},{7,5},{4,6},{5,7},{10,8},{11,9},{8,1... | collective-permute-start | bytes 2359304 | tf_op jit(solution)/shard_map/ppermute | solution.py:161
  144.5 19.0 %collective-permute-start.18 = (bf16[3,8,128,128]{3,2,1,0:T(8,128)(2,1)}, bf16[3,8,128,128]{3,2,1,0:T(8,128)(2,1)S(1)}, u32[]{:S(2)}, u32[]{:S(2)}) collective-permute-start(bf16[3,8,128,128]{3,2,1,0:T(8,128)(2,1)} %delta.4.refs_4_.refs_0_), channel_id=1, source_target_pairs={{2,0},{3,1},{0,2},{1,3},{6,4},{7,5},{4,6},{5,7},{10,8},{11,9},{8,1... | collective-permute-start | bytes 2359304 | tf_op jit(solution)/shard_map/ppermute | solution.py:161
  146.0 19.9 %collective-permute-start.19 = (bf16[3,8,128,128]{3,2,1,0:T(8,128)(2,1)}, bf16[3,8,128,128]{3,2,1,0:T(8,128)(2,1)S(1)}, u32[]{:S(2)}, u32[]{:S(2)}) collective-permute-start(bf16[3,8,128,128]{3,2,1,0:T(8,128)(2,1)} %delta.4.refs_4_.refs_0_), channel_id=1, source_target_pairs={{0,1},{1,0},{2,3},{3,2},{4,5},{5,4},{6,7},{7,6},{8,9},{9,8},{10,11... | collective-permute-start | bytes 2359304 | tf_op jit(solution)/shard_map/ppermute | solution.py:158
  163.4 3.4 copy-start.19
  163.4 3.4 collective-permute-start.20
  163.4 32.3 %collective-permute-start.10 = (bf16[2,3,8,128,128]{4,3,2,1,0:T(8,128)(2,1)}, bf16[2,3,8,128,128]{4,3,2,1,0:T(8,128)(2,1)}, u32[]{:S(2)}, u32[]{:S(2)}) collective-permute-start(bf16[2,3,8,128,128]{4,3,2,1,0:T(8,128)(2,1)} %get-tuple-element.39), channel_id=1, source_target_pairs={{0,1},{1,0},{2,3},{3,2},{4,5},{5,4},{6,7},{7,6},{8,9},{9,8},{10,11... | collective-permute-start | bytes 4718600 | tf_op jit(solution)/shard_map/ppermute | solution.py:158
  165.8 16.1 %copy-start.12 = (s32[3,32,4]{2,1,0:T(8,128)S(1)}, s32[3,32,4]{2,1,0:T(8,128)}, u32[]{:S(2)}) copy-start(s32[3,32,4]{2,1,0:T(8,128)} %copy-done.11) | copy-start | bytes 4612
  182.6 13.1 %copy-start.9 = (f32[2,3,8,128,128]{4,3,2,1,0:T(8,128)S(1)}, f32[2,3,8,128,128]{4,3,2,1,0:T(8,128)}, u32[]{:S(2)}) copy-start(f32[2,3,8,128,128]{4,3,2,1,0:T(8,128)} %get-tuple-element.34.mine_ref) | copy-start | bytes 9437188
  195.6 4.1 collective-permute-start.8
  195.8 3.9 copy-start.10
  198.2 22.4 %collective-permute-start.11 = (bf16[3,8,128,128]{3,2,1,0:T(8,128)(2,1)}, bf16[3,8,128,128]{3,2,1,0:T(8,128)(2,1)S(1)}, u32[]{:S(2)}, u32[]{:S(2)}) collective-permute-start(bf16[3,8,128,128]{3,2,1,0:T(8,128)(2,1)} %fusion.1), channel_id=1, source_target_pairs={{2,0},{3,1},{0,2},{1,3},{6,4},{7,5},{4,6},{5,7},{10,8},{11,9},{8,1... | collective-permute-start | bytes 2359304 | tf_op jit(solution)/shard_map/ppermute | solution.py:161
  217.4 39.0 %collective-permute-start.9 = (bf16[2,3,8,128,128]{4,3,2,1,0:T(8,128)(2,1)}, bf16[2,3,8,128,128]{4,3,2,1,0:T(8,128)(2,1)}, u32[]{:S(2)}, u32[]{:S(2)}) collective-permute-start(bf16[2,3,8,128,128]{4,3,2,1,0:T(8,128)(2,1)} %get-tuple-element.38), channel_id=1, source_target_pairs={{0,1},{1,0},{2,3},{3,2},{4,5},{5,4},{6,7},{7,6},{8,9},{9,8},{10,11... | collective-permute-start | bytes 4718600 | tf_op jit(solution)/shard_map/ppermute | solution.py:158
  219.2 26.2 %collective-permute-start.15 = (bf16[3,8,128,128]{3,2,1,0:T(8,128)(2,1)}, bf16[3,8,128,128]{3,2,1,0:T(8,128)(2,1)S(1)}, u32[]{:S(2)}, u32[]{:S(2)}) collective-permute-start(bf16[3,8,128,128]{3,2,1,0:T(8,128)(2,1)} %bitcast.17), channel_id=1, source_target_pairs={{2,0},{3,1},{0,2},{1,3},{6,4},{7,5},{4,6},{5,7},{10,8},{11,9},{8,1... | collective-permute-start | bytes 2359304 | tf_op jit(solution)/shard_map/ppermute | solution.py:161
  227.4 28.8 %collective-permute-start.21 = (bf16[3,8,128,128]{3,2,1,0:T(8,128)(2,1)}, bf16[3,8,128,128]{3,2,1,0:T(8,128)(2,1)S(1)}, u32[]{:S(2)}, u32[]{:S(2)}) collective-permute-start(bf16[3,8,128,128]{3,2,1,0:T(8,128)(2,1)} %delta.5.refs_0_.refs_4_), channel_id=1, source_target_pairs={{2,0},{3,1},{0,2},{1,3},{6,4},{7,5},{4,6},{5,7},{10,8},{11,9},{8,1... | collective-permute-start | bytes 2359304 | tf_op jit(solution)/shard_map/ppermute | solution.py:161
  228.2 33.4 %collective-permute-start.22 = (bf16[3,8,128,128]{3,2,1,0:T(8,128)(2,1)}, bf16[3,8,128,128]{3,2,1,0:T(8,128)(2,1)S(1)}, u32[]{:S(2)}, u32[]{:S(2)}) collective-permute-start(bf16[3,8,128,128]{3,2,1,0:T(8,128)(2,1)} %delta.5.refs_0_.refs_4_), channel_id=1, source_target_pairs={{0,1},{1,0},{2,3},{3,2},{4,5},{5,4},{6,7},{7,6},{8,9},{9,8},{10,11... | collective-permute-start | bytes 2359304 | tf_op jit(solution)/shard_map/ppermute | solution.py:158
  256.2 4.5 %copy-start.5 = (bf16[3,8,128,128]{3,2,1,0:T(8,128)(2,1)S(1)}, bf16[3,8,128,128]{3,2,1,0:T(8,128)(2,1)}, u32[]{:S(2)}) copy-start(bf16[3,8,128,128]{3,2,1,0:T(8,128)(2,1)} %delta.7.refs_0_.refs_4_) | copy-start | bytes 2359300
  256.3 5.3 %collective-permute-start.23 = (bf16[3,8,128,128]{3,2,1,0:T(8,128)(2,1)S(1)}, bf16[3,8,128,128]{3,2,1,0:T(8,128)(2,1)S(1)}, u32[]{:S(2)}, u32[]{:S(2)}) collective-permute-start(bf16[3,8,128,128]{3,2,1,0:T(8,128)(2,1)S(1)} %add_add_fusion.1), channel_id=1, source_target_pairs={{0,1},{1,0},{2,3},{3,2},{4,5},{5,4},{6,7},{7,6},{8,9},{9,8},{10,11... | collective-permute-start | bytes 2359304 | tf_op jit(solution)/shard_map/ppermute | solution.py:158
  259.5 21.3 %collective-permute-start.12 = (bf16[3,8,128,128]{3,2,1,0:T(8,128)(2,1)}, bf16[3,8,128,128]{3,2,1,0:T(8,128)(2,1)}, u32[]{:S(2)}, u32[]{:S(2)}) collective-permute-start(bf16[3,8,128,128]{3,2,1,0:T(8,128)(2,1)} %fusion.2), channel_id=1, source_target_pairs={{2,0},{3,1},{0,2},{1,3},{6,4},{7,5},{4,6},{5,7},{10,8},{11,9},{8,1... | collective-permute-start | bytes 2359304 | tf_op jit(solution)/shard_map/ppermute | solution.py:161
  260.7 35.5 %collective-permute-start.16 = (bf16[3,8,128,128]{3,2,1,0:T(8,128)(2,1)S(1)}, bf16[3,8,128,128]{3,2,1,0:T(8,128)(2,1)S(1)}, u32[]{:S(2)}, u32[]{:S(2)}) collective-permute-start(bf16[3,8,128,128]{3,2,1,0:T(8,128)(2,1)S(1)} %copy-done.5), channel_id=1, source_target_pairs={{2,0},{3,1},{0,2},{1,3},{6,4},{7,5},{4,6},{5,7},{10,8},{11,9},{8,1... | collective-permute-start | bytes 2359304 | tf_op jit(solution)/shard_map/ppermute | solution.py:161
  261.5 36.2 %collective-permute-start.17 = (bf16[3,8,128,128]{3,2,1,0:T(8,128)(2,1)S(1)}, bf16[3,8,128,128]{3,2,1,0:T(8,128)(2,1)}, u32[]{:S(2)}, u32[]{:S(2)}) collective-permute-start(bf16[3,8,128,128]{3,2,1,0:T(8,128)(2,1)S(1)} %copy-done.5), channel_id=1, source_target_pairs={{0,1},{1,0},{2,3},{3,2},{4,5},{5,4},{6,7},{7,6},{8,9},{9,8},{10,11... | collective-permute-start | bytes 2359304 | tf_op jit(solution)/shard_map/ppermute | solution.py:158
  296.2 2.5 collective-permute-start.24
  296.3 20.5 %collective-permute-start.13 = (bf16[3,8,128,128]{3,2,1,0:T(8,128)(2,1)}, bf16[3,8,128,128]{3,2,1,0:T(8,128)(2,1)S(1)}, u32[]{:S(2)}, u32[]{:S(2)}) collective-permute-start(bf16[3,8,128,128]{3,2,1,0:T(8,128)(2,1)} %delta.6.refs_0_.refs_4_), channel_id=1, source_target_pairs={{2,0},{3,1},{0,2},{1,3},{6,4},{7,5},{4,6},{5,7},{10,8},{11,9},{8,1... | collective-permute-start | bytes 2359304 | tf_op jit(solution)/shard_map/ppermute | solution.py:161
  297.5 19.6 %collective-permute-start.14 = (bf16[3,8,128,128]{3,2,1,0:T(8,128)(2,1)}, bf16[3,8,128,128]{3,2,1,0:T(8,128)(2,1)S(1)}, u32[]{:S(2)}, u32[]{:S(2)}) collective-permute-start(bf16[3,8,128,128]{3,2,1,0:T(8,128)(2,1)} %delta.6.refs_0_.refs_4_), channel_id=1, source_target_pairs={{0,1},{1,0},{2,3},{3,2},{4,5},{5,4},{6,7},{7,6},{8,9},{9,8},{10,11... | collective-permute-start | bytes 2359304 | tf_op jit(solution)/shard_map/ppermute | solution.py:158
  316.9 2.4 collective-permute-start.25
  336.5 6.9 %copy-start.1 = (f32[2,4,128,1024]{3,2,1,0:T(8,128)S(1)}, f32[2,4,128,1024]{3,2,1,0:T(8,128)}, u32[]{:S(2)}) copy-start(f32[2,4,128,1024]{3,2,1,0:T(8,128)} %get-tuple-element.47) | copy-start | bytes 12582916
  339.2 4.2 %collective-permute-start.26 = (bf16[2,4,128,1024]{3,2,1,0:T(8,128)(2,1)S(1)}, bf16[2,4,128,1024]{3,2,1,0:T(8,128)(2,1)S(1)}, u32[]{:S(2)}, u32[]{:S(2)}) collective-permute-start(bf16[2,4,128,1024]{3,2,1,0:T(8,128)(2,1)S(1)} %convert_element_type.176), channel_id=1, source_target_pairs={{0,1},{1,0},{2,3},{3,2},{4,5},{5,4},{6,7},{7,6},{8,9},{9,8},{10,11... | collective-permute-start | bytes 6291464 | tf_op jit(solution)/shard_map/ppermute | solution.py:158
  343.4 3.6 copy-start.13
  344.7 29.5 %collective-permute-start.27 = (bf16[4,128,1024]{2,1,0:T(8,128)(2,1)S(1)}, bf16[4,128,1024]{2,1,0:T(8,128)(2,1)}, u32[]{:S(2)}, u32[]{:S(2)}) collective-permute-start(bf16[4,128,1024]{2,1,0:T(8,128)(2,1)S(1)} %bitcast.76), channel_id=1, source_target_pairs={{2,0},{3,1},{0,2},{1,3},{6,4},{7,5},{4,6},{5,7},{10,8},{11,9},{8,1... | collective-permute-start | bytes 3145736 | tf_op jit(solution)/shard_map/ppermute | solution.py:161
  377.9 19.0 %collective-permute-start.28 = (bf16[128,1024]{1,0:T(8,128)(2,1)}, bf16[128,1024]{1,0:T(8,128)(2,1)}, u32[]{:S(2)}, u32[]{:S(2)}) collective-permute-start(bf16[128,1024]{1,0:T(8,128)(2,1)} %get-tuple-element.62), channel_id=1, source_target_pairs={{0,4},{4,8},{8,12},{12,0},{1,5},{5,9},{9,13},{13,1},{2,6},{6,10},{... | collective-permute-start | bytes 786440 | tf_op jit(solution)/shard_map/ppermute | solution.py:325
  378.0 21.6 %collective-permute-start.29 = (bf16[128,1024]{1,0:T(8,128)(2,1)}, bf16[128,1024]{1,0:T(8,128)(2,1)}, u32[]{:S(2)}, u32[]{:S(2)}) collective-permute-start(bf16[128,1024]{1,0:T(8,128)(2,1)} %get-tuple-element.64), channel_id=1, source_target_pairs={{0,8},{4,12},{8,0},{12,4},{1,9},{5,13},{9,1},{13,5},{2,10},{6,14},... | collective-permute-start | bytes 786440 | tf_op jit(solution)/shard_map/ppermute | solution.py:325
  379.9 19.6 %collective-permute-start.30 = (bf16[128,1024]{1,0:T(8,128)(2,1)S(1)}, bf16[128,1024]{1,0:T(8,128)(2,1)}, u32[]{:S(2)}, u32[]{:S(2)}) collective-permute-start(bf16[128,1024]{1,0:T(8,128)(2,1)S(1)} %get-tuple-element.63), channel_id=1, source_target_pairs={{0,12},{4,0},{8,4},{12,8},{1,13},{5,1},{9,5},{13,9},{2,14},{6,2},{... | collective-permute-start | bytes 786440 | tf_op jit(solution)/shard_map/ppermute | solution.py:325
  (13 other events, 19.5 us)
Sparse Core Ops, SparseCore 0:
  9.6 30.6 all-gather.4
  41.8 27.4 all-gather.6
